TPU v7x, 32 devices: a whole 2x2x4 slice. The times are simulated.
32 devices in a mesh: dp: 8 (over y, x, core), tensor: 4 (over z).
Axes of the slice: x: 2, y: 2, z: 4, core: 2. Of those that a mesh axis runs over, the one named last changes fastest.
Arguments:
- inputs: bfloat16 [2, 8, 1024, 1024], P(None, 'dp', 'tensor'), may hold values from -6 to 6
- cotangent: bfloat16 [2, 8, 1024, 1024], P(None, 'dp', 'tensor'), may hold values from -6 to 6
- attention_in: float32 [1024, 3, 1024], P('dp', None, 'tensor'), may hold values from -0.1875 to 0.1875
- attention_out: float32 [1024, 1024], P('dp', 'tensor'), may hold values from -3 to 3
- expand_weight: float32 [1024, 2, 2624], P('dp', None, 'tensor'), may hold values from -0.1875 to 0.1875
- contract_weight: float32 [1024, 2624], P('dp', 'tensor'), may hold values from -0.125 to 0.125
- norm_gains: float32 [2, 1024], P(None, 'dp'), may hold values from 0.5 to 1.5
- attention_in_first: float32 [1024, 3, 1024], P('dp', None, 'tensor'), may hold values from -64 to 64
- attention_in_second: float32 [1024, 3, 1024], P('dp', None, 'tensor'), may hold values from 163.84 to 655.36
- attention_out_first: float32 [1024, 1024], P('dp', 'tensor'), may hold values from -6 to 6
- attention_out_second: float32 [1024, 1024], P('dp', 'tensor'), may hold values from 1.6 to 6.4
- expand_first: float32 [1024, 2, 2624], P('dp', None, 'tensor'), may hold values from -32 to 32
- expand_second: float32 [1024, 2, 2624], P('dp', None, 'tensor'), may hold values from 40.96 to 163.84
- contract_first: float32 [1024, 2624], P('dp', 'tensor'), may hold values from -40 to 40
- contract_second: float32 [1024, 2624], P('dp', 'tensor'), may hold values from 65.536 to 262.144
- gains_first: float32 [2, 1024], P(None, 'dp'), may hold values from -80 to 80
- gains_second: float32 [2, 1024], P(None, 'dp'), may hold values from 327.68 to 1310.72
Outputs:
- layer_output: bfloat16 [2, 8, 1024, 1024], P(None, 'dp', 'tensor')
- input_gradient: bfloat16 [2, 8, 1024, 1024], P(None, 'dp', 'tensor')
- attention_in_new: float32 [1024, 3, 1024], P('dp', None, 'tensor')
- attention_in_first_new: float32 [1024, 3, 1024], P('dp', None, 'tensor')
- attention_in_second_new: float32 [1024, 3, 1024], P('dp', None, 'tensor')
- attention_out_new: float32 [1024, 1024], P('dp', 'tensor')
- attention_out_first_new: float32 [1024, 1024], P('dp', 'tensor')
- attention_out_second_new: float32 [1024, 1024], P('dp', 'tensor')
- expand_new: float32 [1024, 2, 2624], P('dp', None, 'tensor')
- expand_first_new: float32 [1024, 2, 2624], P('dp', None, 'tensor')
- expand_second_new: float32 [1024, 2, 2624], P('dp', None, 'tensor')
- contract_new: float32 [1024, 2624], P('dp', 'tensor')
- contract_first_new: float32 [1024, 2624], P('dp', 'tensor')
- contract_second_new: float32 [1024, 2624], P('dp', 'tensor')
- gains_new: float32 [2, 1024], P(None, 'dp')
- gains_first_new: float32 [2, 1024], P(None, 'dp')
- gains_second_new: float32 [2, 1024], P(None, 'dp')
All inputs are finite; a program needn't handle non-finite values.
Results may differ from a plain program's by a relative error of at most 0.02.
Values may be sent and summed in bfloat16 or wider, within the bound.
No kernel may reach another device: no remote copies, remote signals or barrier semaphores. Data moves between devices by JAX's collectives and lax.ppermute only.
A program may use at most 192 MiB of HBM per device.

v0:
```python
import jax
import jax.numpy as jnp
from jax import lax
from jax.sharding import PartitionSpec as P

D = 1024
H = 16
DH = 64
FF = 2624
SEQ = 1024
STEP = 10


epsilon_norm = 1e-05
rope_theta = 160000.0
beta_first = 0.9
beta_second = 0.98
epsilon_adam = 1e-06
weight_decay = 1e-05


def layer_norm(values):
    centered = values - jnp.mean(values, axis=-1, keepdims=True)
    variance = jnp.mean(centered * centered, axis=-1, keepdims=True)
    return centered * lax.rsqrt(variance + epsilon_norm)


def norm_scaled(values, gain_row):
    return layer_norm(values) * gain_row


def rotary_tables(seq_length, head_size):
    positions = jnp.arange(seq_length).astype(jnp.float32)
    exponents = jnp.arange(0, head_size, 2).astype(jnp.float32) / head_size
    angles = positions[:, None] * jnp.power(rope_theta, -exponents)[None, :]
    angles = jnp.concatenate([angles, angles], axis=-1)
    return (jnp.cos(angles), jnp.sin(angles))


def rotate(values, cosine, sine):
    half_size = values.shape[-1] // 2
    turned = jnp.concatenate([-values[..., half_size:], values[..., :half_size]], axis=-1)
    return values * cosine[:, None, :] + turned * sine[:, None, :]


def contract_rows(left, right):
    return lax.dot_general(
        left, right, (((0,), (0,)), ((), ())), preferred_element_type=jnp.float32
    )


def contract_cols(left, right):
    return lax.dot_general(
        left, right, (((1,), (1,)), ((), ())), preferred_element_type=jnp.float32
    )


def attend_forward(queries, key_rows, value_rows, score_scale):
    seq_length, heads_local, head_size = queries.shape
    block_rows = min(512, seq_length)
    query_blocks = queries.reshape(seq_length // block_rows, block_rows, heads_local, head_size)

    def one_block(query_block):
        scores = (
            jnp.einsum("qhd,khd->hqk", query_block, key_rows, preferred_element_type=jnp.float32)
            * score_scale
        )
        row_peak = jnp.max(scores, axis=-1, keepdims=True)
        exponent = jnp.exp(scores - row_peak)
        row_total = jnp.sum(exponent, axis=-1, keepdims=True)
        soft_weights = (exponent / row_total).astype(jnp.bfloat16)
        block_out = jnp.einsum(
            "hqk,khd->qhd", soft_weights, value_rows, preferred_element_type=jnp.float32
        )
        return (block_out, (row_peak + jnp.log(row_total))[..., 0])

    blocks_out, log_totals = lax.map(one_block, query_blocks)
    return (blocks_out.reshape(seq_length, heads_local * head_size), log_totals)


def attend_backward(queries, key_rows, value_rows, grad_attended, log_totals, score_scale):
    seq_length, heads_local, head_size = queries.shape
    block_rows = min(512, seq_length)
    block_count = seq_length // block_rows
    query_blocks = queries.reshape(block_count, block_rows, heads_local, head_size)
    grad_blocks = grad_attended.reshape(block_count, block_rows, heads_local, head_size)

    def one_block(running, pieces):
        grad_keys, grad_values = running
        query_block, grad_block, total_block = pieces
        scores = (
            jnp.einsum("qhd,khd->hqk", query_block, key_rows, preferred_element_type=jnp.float32)
            * score_scale
        )
        soft_weights = jnp.exp(scores - total_block[..., None])
        grad_soft = jnp.einsum(
            "qhd,khd->hqk", grad_block, value_rows, preferred_element_type=jnp.float32
        )
        row_delta = jnp.sum(soft_weights * grad_soft, axis=-1, keepdims=True)
        grad_scores = (soft_weights * (grad_soft - row_delta)).astype(jnp.bfloat16)
        grad_query = (
            jnp.einsum("hqk,khd->qhd", grad_scores, key_rows, preferred_element_type=jnp.float32)
            * score_scale
        )
        grad_keys = (
            grad_keys
            + jnp.einsum(
                "hqk,qhd->khd", grad_scores, query_block, preferred_element_type=jnp.float32
            )
            * score_scale
        )
        grad_values = grad_values + jnp.einsum(
            "hqk,qhd->khd",
            soft_weights.astype(jnp.bfloat16),
            grad_block,
            preferred_element_type=jnp.float32,
        )
        return ((grad_keys, grad_values), grad_query)

    zeros_start = jnp.zeros((seq_length, heads_local, head_size), jnp.float32)
    (grad_keys, grad_values), grad_queries = lax.scan(
        one_block, (zeros_start, zeros_start), (query_blocks, grad_blocks, log_totals)
    )
    return (grad_queries.reshape(seq_length, heads_local, head_size), grad_keys, grad_values)


def fetch(masters):
    return (
        lax.all_gather(masters[0].astype(jnp.bfloat16), "dp", axis=0, tiled=True),
        lax.all_gather(masters[1].astype(jnp.bfloat16), "dp", axis=0, tiled=True),
        lax.all_gather(masters[2].astype(jnp.bfloat16), "dp", axis=0, tiled=True),
        lax.all_gather(masters[3].astype(jnp.bfloat16), "dp", axis=0, tiled=True),
        lax.all_gather(masters[4].astype(jnp.bfloat16), "dp", axis=1, tiled=True),
    )


def reduce_grads(grad_list):
    return (
        lax.psum_scatter(grad_list[0], "dp", scatter_dimension=0, tiled=True),
        lax.psum_scatter(grad_list[1], "dp", scatter_dimension=0, tiled=True),
        lax.psum_scatter(grad_list[2], "dp", scatter_dimension=0, tiled=True),
        lax.psum_scatter(grad_list[3], "dp", scatter_dimension=0, tiled=True),
        lax.psum_scatter(grad_list[4], "dp", scatter_dimension=1, tiled=True),
    )


def adamw_update(weight, first_moment, second_moment, gradient, step_rate):
    first_new = beta_first * first_moment + (1.0 - beta_first) * gradient
    second_new = beta_second * second_moment + (1.0 - beta_second) * gradient * gradient
    first_hat = first_new / (1.0 - beta_first**STEP)
    second_hat = second_new / (1.0 - beta_second**STEP)
    weight_new = weight - step_rate * (
        first_hat / (jnp.sqrt(second_hat) + epsilon_adam) + weight_decay * weight
    )
    return (weight_new, first_new, second_new)


def per_device(
    inputs,
    cotangent,
    attention_in,
    attention_out,
    expand_weight,
    contract_weight,
    norm_gains,
    attention_in_first,
    attention_in_second,
    attention_out_first,
    attention_out_second,
    expand_first,
    expand_second,
    contract_first,
    contract_second,
    gains_first,
    gains_second,
):
    masters = (attention_in, attention_out, expand_weight, contract_weight, norm_gains)
    micro_count = inputs.shape[0]
    local_rows = inputs.shape[2]
    model_width = inputs.shape[3]
    head_size = DH
    heads_local = attention_in.shape[2] // head_size
    hidden_local = expand_weight.shape[2]
    score_scale = head_size ** (-0.5)
    seq_length = local_rows * lax.axis_size("tensor")
    cosine, sine = rotary_tables(seq_length, head_size)

    def turn_both(query_part, key_part):
        return (rotate(query_part, cosine, sine), rotate(key_part, cosine, sine))

    def geglu(lifted):
        return jax.nn.gelu(lifted[:, :hidden_local], approximate=False) * lifted[:, hidden_local:]

    running = None
    outputs = []
    input_grads = []
    for micro_index in range(micro_count):
        gathered = fetch(masters)
        qkv_flat = gathered[0].reshape(model_width, -1)
        attn_full = gathered[1]
        expand_flat = gathered[2].reshape(model_width, -1)
        contract_full = gathered[3]
        gain_values = gathered[4].astype(jnp.float32)
        sequence = inputs[micro_index, 0].astype(jnp.float32)
        normed, norm_back = jax.vjp(norm_scaled, sequence, gain_values[0])
        normed_rows = lax.all_gather(normed.astype(jnp.bfloat16), "tensor", axis=0, tiled=True)
        mixed_rows = jnp.dot(normed_rows, qkv_flat, preferred_element_type=jnp.float32)
        mixed_rows = mixed_rows.reshape(seq_length, 3, heads_local, head_size)
        (query_turned, key_turned), rope_back = jax.vjp(
            turn_both, mixed_rows[:, 0], mixed_rows[:, 1]
        )
        queries = query_turned.astype(jnp.bfloat16)
        key_rows = key_turned.astype(jnp.bfloat16)
        value_rows = mixed_rows[:, 2].astype(jnp.bfloat16)
        attended, log_totals = attend_forward(queries, key_rows, value_rows, score_scale)
        attended = attended.astype(jnp.bfloat16)
        branch = lax.psum_scatter(
            contract_cols(attended, attn_full).astype(jnp.bfloat16),
            "tensor",
            scatter_dimension=0,
            tiled=True,
        ).astype(jnp.float32)
        middle = sequence + branch
        normed_two, norm_two_back = jax.vjp(norm_scaled, middle, gain_values[1])
        rows_two = lax.all_gather(normed_two.astype(jnp.bfloat16), "tensor", axis=0, tiled=True)
        lifted = jnp.dot(rows_two, expand_flat, preferred_element_type=jnp.float32)
        hidden, geglu_back = jax.vjp(geglu, lifted)
        hidden = hidden.astype(jnp.bfloat16)
        branch_two = lax.psum_scatter(
            contract_cols(hidden, contract_full).astype(jnp.bfloat16),
            "tensor",
            scatter_dimension=0,
            tiled=True,
        ).astype(jnp.float32)
        outputs.append((middle + branch_two).astype(jnp.bfloat16))
        grad_output = cotangent[micro_index, 0]
        grad_rows = lax.all_gather(grad_output, "tensor", axis=0, tiled=True)
        grad_contract = contract_rows(grad_rows, hidden)
        grad_hidden = jnp.dot(grad_rows, contract_full, preferred_element_type=jnp.float32)
        (grad_lifted,) = geglu_back(grad_hidden)
        grad_lifted = grad_lifted.astype(jnp.bfloat16)
        grad_expand = contract_rows(rows_two, grad_lifted).reshape(model_width, 2, hidden_local)
        grad_normed_two = lax.psum_scatter(
            contract_cols(grad_lifted, expand_flat).astype(jnp.bfloat16),
            "tensor",
            scatter_dimension=0,
            tiled=True,
        ).astype(jnp.float32)
        grad_middle_norm, grad_gain_two = norm_two_back(grad_normed_two)
        grad_middle = grad_output.astype(jnp.float32) + grad_middle_norm
        middle_rows = lax.all_gather(grad_middle.astype(jnp.bfloat16), "tensor", axis=0, tiled=True)
        grad_attn_out = contract_rows(middle_rows, attended)
        grad_attended = jnp.dot(middle_rows, attn_full, preferred_element_type=jnp.float32).astype(
            jnp.bfloat16
        )
        grad_queries, grad_keys, grad_values = attend_backward(
            queries, key_rows, value_rows, grad_attended, log_totals, score_scale
        )
        grad_query_pre, grad_key_pre = rope_back((grad_queries, grad_keys))
        grad_mixed = jnp.stack([grad_query_pre, grad_key_pre, grad_values], axis=1)
        grad_mixed = grad_mixed.reshape(seq_length, -1).astype(jnp.bfloat16)
        grad_attn_in = contract_rows(normed_rows, grad_mixed).reshape(
            model_width, 3, heads_local * head_size
        )
        grad_normed = lax.psum_scatter(
            contract_cols(grad_mixed, qkv_flat).astype(jnp.bfloat16),
            "tensor",
            scatter_dimension=0,
            tiled=True,
        ).astype(jnp.float32)
        grad_input_norm, grad_gain_one = norm_back(grad_normed)
        input_grads.append((grad_middle + grad_input_norm).astype(jnp.bfloat16))
        local_grads = (
            grad_attn_in,
            grad_attn_out,
            grad_expand,
            grad_contract,
            jnp.stack([grad_gain_one, grad_gain_two]),
        )
        local_grads = reduce_grads(local_grads)
        if running is None:
            running = local_grads
        else:
            running = tuple(
                (summed + fresh_grad for summed, fresh_grad in zip(running, local_grads))
            )
    gain_total = lax.psum(running[4], "tensor")
    step_rates = (
        2.5 * D ** (-0.5),
        2.5 * max(1, 4 * H * DH // SEQ) ** (-0.5),
        2.5 * D ** (-0.5),
        2.5 * FF ** (-0.5),
        0.25,
    )
    qkv_new = adamw_update(
        attention_in, attention_in_first, attention_in_second, running[0], step_rates[0]
    )
    out_new = adamw_update(
        attention_out, attention_out_first, attention_out_second, running[1], step_rates[1]
    )
    expand_new = adamw_update(expand_weight, expand_first, expand_second, running[2], step_rates[2])
    contract_new = adamw_update(
        contract_weight, contract_first, contract_second, running[3], step_rates[3]
    )
    gains_new = adamw_update(norm_gains, gains_first, gains_second, gain_total, step_rates[4])
    layer_output = jnp.stack(outputs)[:, None]
    input_gradient = jnp.stack(input_grads)[:, None]
    return (
        layer_output,
        input_gradient,
        qkv_new[0],
        qkv_new[1],
        qkv_new[2],
        out_new[0],
        out_new[1],
        out_new[2],
        expand_new[0],
        expand_new[1],
        expand_new[2],
        contract_new[0],
        contract_new[1],
        contract_new[2],
        gains_new[0],
        gains_new[1],
        gains_new[2],
    )


def solution(mesh):
    return jax.shard_map(
        per_device,
        mesh=mesh,
        in_specs=(
            P(None, "dp", "tensor", None),
            P(None, "dp", "tensor", None),
            P("dp", None, "tensor"),
            P("dp", "tensor"),
            P("dp", None, "tensor"),
            P("dp", "tensor"),
            P(None, "dp"),
            P("dp", None, "tensor"),
            P("dp", None, "tensor"),
            P("dp", "tensor"),
            P("dp", "tensor"),
            P("dp", None, "tensor"),
            P("dp", None, "tensor"),
            P("dp", "tensor"),
            P("dp", "tensor"),
            P(None, "dp"),
            P(None, "dp"),
        ),
        out_specs=(
            P(None, "dp", "tensor", None),
            P(None, "dp", "tensor", None),
            P("dp", None, "tensor"),
            P("dp", None, "tensor"),
            P("dp", None, "tensor"),
            P("dp", "tensor"),
            P("dp", "tensor"),
            P("dp", "tensor"),
            P("dp", None, "tensor"),
            P("dp", None, "tensor"),
            P("dp", None, "tensor"),
            P("dp", "tensor"),
            P("dp", "tensor"),
            P("dp", "tensor"),
            P(None, "dp"),
            P(None, "dp"),
            P(None, "dp"),
        ),
        check_vma=False,
    )
```

profile of v0, /device:TPU:0, one launch (start us, length us, event | category | flops | bytes accessed | tf_op | source)
XLA Modules:
  0.0 1242.7 jit_solution(804871529718517015)
XLA Ops:
  39.8 48.1 %all-gather.14.cloned.1.call-done = bf16[1024,1024]{1,0:T(8,128)(2,1)} async-done(((bf16[256,1024]{1,0:T(8,128)(2,1)}), bf16[1024,1024]{1,0:T(8,128)(2,1)}) %all-gather.14.cloned.1.call-update) | async-done | bytes 2097168 | tf_op jit(solution)/shard_map/all_gather | solution.py:206
  105.0 16.2 %while.54 = (s32[]{:T(128)}, bf16[2,512,4,64]{1,3,2,0:T(8,128)(2,1)}, f32[2,4,512]{2,1,0:T(4,128)S(1)}, bf16[2,512,4,64]{1,3,2,0:T(8,128)(2,1)}, bf16[1024,4,64]...) while((s32[]{:T(128)}, bf16[2,512,4,64]{1,3,2,0:T(8,128)(2,1)}, ...), condition=%wide.region_5.6_spmd, body=%wide.region_2.5_spmd.sunk | while | flops 555743232 | bytes 31260824 | solution.py:77
  126.6 42.2 %reduce-scatter.16.cloned.1.call-done = bf16[256,1024]{1,0:T(8,128)(2,1)} async-done(((bf16[1024,1024]{1,0:T(8,128)(2,1)}), bf16[256,1024]{1,0:T(8,128)(2,1)}) %reduce-scatter.16.cloned.1.call-update) | async-done | bytes 524304 | tf_op jit(solution)/shard_map/reduce_scatter | solution.py:217
  171.4 45.4 %all-gather.24.cloned.1.call-done = bf16[1024,1024]{1,0:T(8,128)(2,1)} async-done(((bf16[256,1024]{1,0:T(8,128)(2,1)}), bf16[1024,1024]{1,0:T(8,128)(2,1)}) %all-gather.24.cloned.1.call-update) | async-done | bytes 2097168 | tf_op jit(solution)/shard_map/all_gather | solution.py:206
  251.2 40.7 %reduce-scatter.20.cloned.1.call-done = bf16[256,1024]{1,0:T(8,128)(2,1)} async-done(((bf16[1024,1024]{1,0:T(8,128)(2,1)}), bf16[256,1024]{1,0:T(8,128)(2,1)}) %reduce-scatter.20.cloned.1.call-update) | async-done | bytes 524304 | tf_op jit(solution)/shard_map/reduce_scatter | solution.py:217
  301.1 23.3 %all-gather.20.cloned.1.call-done = bf16[1024,2,656]{0,2,1:T(8,128)(2,1)} async-done(((bf16[128,2,656]{0,2,1:T(8,128)(2,1)}), bf16[1024,2,656]{0,2,1:T(8,128)(2,1)}) %all-gather.20.cloned.1.call-update) | async-done | bytes 2686992 | tf_op jit(solution)/shard_map/all_gather | solution.py:131
  324.4 48.1 %all-gather.18.cloned.1.call-done = bf16[1024,1024]{1,0:T(8,128)(2,1)} async-done(((bf16[256,1024]{1,0:T(8,128)(2,1)}), bf16[1024,1024]{1,0:T(8,128)(2,1)}) %all-gather.18.cloned.1.call-update) | async-done | bytes 2097168 | tf_op jit(solution)/shard_map/all_gather | solution.py:225
  380.3 18.3 %all-gather.22.cloned.1.call-done = bf16[1024,656]{0,1:T(8,128)(2,1)} async-done(((bf16[128,656]{0,1:T(8,128)(2,1)}), bf16[1024,656]{0,1:T(8,128)(2,1)}) %all-gather.22.cloned.1.call-update) | async-done | bytes 1343504 | tf_op jit(solution)/shard_map/all_gather | solution.py:132
  398.6 48.1 %all-gather.32.cloned.1.call-done = bf16[1,1,1024,1024]{3,2,1,0:T(8,128)(2,1)} async-done(((bf16[1,1,256,1024]{3,2,1,0:T(8,128)(2,1)}), bf16[1,1,1024,1024]{3,2,1,0:T(8,128)(2,1)}) %all-gather.32.cloned.1.call-update) | async-done | bytes 2097168 | tf_op jit(solution)/shard_map/all_gather | solution.py:237
  465.9 27.5 %all-gather.26.cloned.1.call-done = bf16[1024,1024]{1,0:T(8,128)(2,1)} async-done(((bf16[256,1024]{1,0:T(8,128)(2,1)}), bf16[1024,1024]{1,0:T(8,128)(2,1)}) %all-gather.26.cloned.1.call-update) | async-done | bytes 2097168 | tf_op jit(solution)/shard_map/all_gather | solution.py:225
  501.1 38.5 %all-gather.34.cloned.1.call-done = bf16[1,1,1024,1024]{3,2,1,0:T(8,128)(2,1)} async-done(((bf16[1,1,256,1024]{3,2,1,0:T(8,128)(2,1)}), bf16[1,1,1024,1024]{3,2,1,0:T(8,128)(2,1)}) %all-gather.34.cloned.1.call-update) | async-done | bytes 2097168 | tf_op jit(solution)/shard_map/all_gather | solution.py:237
  568.3 16.1 %reduce-scatter.24.cloned.1.call-done = bf16[256,1024]{1,0:T(8,128)(2,1)} async-done(((bf16[1024,1024]{1,0:T(8,128)(2,1)}), bf16[256,1024]{1,0:T(8,128)(2,1)}) %reduce-scatter.24.cloned.1.call-update) | async-done | bytes 524304 | tf_op jit(solution)/shard_map/reduce_scatter | solution.py:243
  584.4 45.6 %reduce-scatter.28.cloned.1.call-done = bf16[256,1024]{1,0:T(8,128)(2,1)} async-done(((bf16[1024,1024]{1,0:T(8,128)(2,1)}), bf16[256,1024]{1,0:T(8,128)(2,1)}) %reduce-scatter.28.cloned.1.call-update) | async-done | bytes 524304 | tf_op jit(solution)/shard_map/reduce_scatter | solution.py:243
  632.9 42.6 %reduce-scatter.18.cloned.1.call-done = bf16[256,1024]{1,0:T(8,128)(2,1)} async-done(((bf16[1024,1024]{1,0:T(8,128)(2,1)}), bf16[256,1024]{1,0:T(8,128)(2,1)}) %reduce-scatter.18.cloned.1.call-update) | async-done | bytes 524304 | tf_op jit(solution)/shard_map/reduce_scatter | solution.py:229
  675.4 45.4 %reduce-scatter.22.cloned.1.call-done = bf16[256,1024]{1,0:T(8,128)(2,1)} async-done(((bf16[1024,1024]{1,0:T(8,128)(2,1)}), bf16[256,1024]{1,0:T(8,128)(2,1)}) %reduce-scatter.22.cloned.1.call-update) | async-done | bytes 524304 | tf_op jit(solution)/shard_map/reduce_scatter | solution.py:229
  726.8 44.8 %all-gather.30.cloned.1.call-done = bf16[1024,1024]{1,0:T(8,128)(2,1)} async-done(((bf16[256,1024]{1,0:T(8,128)(2,1)}), bf16[1024,1024]{1,0:T(8,128)(2,1)}) %all-gather.30.cloned.1.call-update) | async-done | bytes 2097168 | tf_op jit(solution)/shard_map/all_gather | solution.py:251
  781.2 51.8 %while.57 = (s32[]{:T(128)}, f32[1024,4,64]{0,2,1:T(8,128)S(1)}, f32[1024,4,64]{0,2,1:T(8,128)}, f32[2,512,4,64]{1,0,3,2:T(2,128)}, bf16[2,512,4,64]{1,3,2,0:T(8...) while((s32[]{:T(128)}, f32[1024,4,64]{0,2,1:T(8,128)S(1)}, ...), condition=%wide.region_34.35_spmd.clone, body=%wide.region_32.34_spmd.clone.sunk | while | flops 1368782848 | bytes 72409232 | solution.py:121
  843.6 52.3 %while.56 = (s32[]{:T(128)}, f32[1024,4,64]{0,2,1:T(8,128)S(1)}, f32[1024,4,64]{0,2,1:T(8,128)}, f32[2,512,4,64]{1,0,3,2:T(2,128)}, bf16[2,512,4,64]{1,3,2,0:T(8...) while((s32[]{:T(128)}, f32[1024,4,64]{0,2,1:T(8,128)S(1)}, ...), condition=%wide.region_25.26_spmd.clone, body=%wide.region_23.25_spmd.clone.sunk | while | flops 1368782848 | bytes 72409232 | solution.py:121
  952.8 45.6 %reduce-scatter.26.cloned.1.call-done = bf16[256,1024]{1,0:T(8,128)(2,1)} async-done(((bf16[1024,1024]{1,0:T(8,128)(2,1)}), bf16[256,1024]{1,0:T(8,128)(2,1)}) %reduce-scatter.26.cloned.1.call-update) | async-done | bytes 524304 | tf_op jit(solution)/shard_map/reduce_scatter | solution.py:265
  1010.7 35.0 %reduce-scatter.38.cloned.1.call-done = f32[128,656]{0,1:T(8,128)} async-done(((f32[1024,656]{0,1:T(8,128)}), f32[128,656]{0,1:T(8,128)}) %reduce-scatter.38.cloned.1.call-update) | async-done | bytes 335888 | tf_op jit(solution)/shard_map/reduce_scatter | solution.py:142
  1048.9 57.5 %reduce-scatter.36.cloned.1.call-done = f32[128,2,656]{0,2,1:T(8,128)} async-done(((f32[1024,2,656]{0,2,1:T(8,128)}), f32[128,2,656]{0,2,1:T(8,128)}) %reduce-scatter.36.cloned.1.call-update) | async-done | bytes 671760 | tf_op jit(solution)/shard_map/reduce_scatter | solution.py:141
  1109.7 36.5 %reduce-scatter.34.cloned.1.call-done = f32[128,256]{1,0:T(8,128)} async-done(((f32[1024,256]{1,0:T(8,128)}), f32[128,256]{1,0:T(8,128)}) %reduce-scatter.34.cloned.1.call-update) | async-done | bytes 131088 | tf_op jit(solution)/shard_map/reduce_scatter | solution.py:140
  1152.8 30.6 %reduce-scatter.40.cloned.1.call-done = f32[128,2]{1,0:T(8,128)} async-done(((f32[1024,2]{1,0:T(8,128)}), f32[128,2]{1,0:T(8,128)}) %reduce-scatter.40.cloned.1.call-update) | async-done | bytes 1040
  1197.3 36.0 %reduce-scatter.32.cloned.1.call-done = f32[128,3,256]{2,0,1:T(8,128)} async-done(((f32[1024,3,256]{2,0,1:T(8,128)}), f32[128,3,256]{2,0,1:T(8,128)}) %reduce-scatter.32.cloned.1.call-update) | async-done | bytes 393232 | tf_op jit(solution)/shard_map/reduce_scatter | solution.py:139
  (406 shorter events, 425.0 us)
Async XLA Ops:
  7.2 32.6 %all-gather.16.cloned.1.call-start = ((), (), s32[]{:S(2)}) async-start(), calls=%async_computation.14 | async-start | bytes 1769472 | tf_op jit(solution)/shard_map/all_gather | solution.py:129
  9.2 78.7 %all-gather.14.cloned.1.call-start = ((), (), s32[]{:S(2)}) async-start(), calls=%async_computation.13 | async-start | bytes 2621440 | tf_op jit(solution)/shard_map/all_gather | solution.py:206
  24.6 144.2 %reduce-scatter.16.cloned.1.call-start = ((), (), s32[]{:S(2)}) async-start(), calls=%async_computation.15 | async-start | bytes 2621440 | tf_op jit(solution)/shard_map/reduce_scatter | solution.py:217
  126.1 90.7 %all-gather.24.cloned.1.call-start = ((), (), s32[]{:S(2)}) async-start(), calls=%async_computation.20 | async-start | bytes 2621440 | tf_op jit(solution)/shard_map/all_gather | solution.py:206
  171.4 120.6 %reduce-scatter.20.cloned.1.call-start = ((), (), s32[]{:S(2)}) async-start(), calls=%async_computation.21 | async-start | bytes 2621440 | tf_op jit(solution)/shard_map/reduce_scatter | solution.py:217
  249.2 75.2 %all-gather.20.cloned.1.call-start = ((), (), s32[]{:S(2)}) async-start(), calls=%async_computation.17 | async-start | bytes 3022848 | tf_op jit(solution)/shard_map/all_gather | solution.py:131
  251.2 121.3 %all-gather.18.cloned.1.call-start = ((), (), s32[]{:S(2)}) async-start(), calls=%async_computation.16 | async-start | bytes 2621440 | tf_op jit(solution)/shard_map/all_gather | solution.py:225
  296.4 102.2 %all-gather.22.cloned.1.call-start = ((), (), s32[]{:S(2)}) async-start(), calls=%async_computation.18 | async-start | bytes 1511424 | tf_op jit(solution)/shard_map/all_gather | solution.py:132
  297.2 149.5 %all-gather.32.cloned.1.call-start = ((), (), s32[]{:S(2)}) async-start(), calls=%async_computation.30 | async-start | bytes 2621440 | tf_op jit(solution)/shard_map/all_gather | solution.py:237
  299.5 193.9 %all-gather.26.cloned.1.call-start = ((), (), s32[]{:S(2)}) async-start(), calls=%async_computation.22 | async-start | bytes 2621440 | tf_op jit(solution)/shard_map/all_gather | solution.py:225
  300.1 239.5 %all-gather.34.cloned.1.call-start = ((), (), s32[]{:S(2)}) async-start(), calls=%async_computation.31 | async-start | bytes 2621440 | tf_op jit(solution)/shard_map/all_gather | solution.py:237
  300.8 283.5 %reduce-scatter.24.cloned.1.call-start = ((), (), s32[]{:S(2)}) async-start(), calls=%async_computation.24 | async-start | bytes 2621440 | tf_op jit(solution)/shard_map/reduce_scatter | solution.py:243
  465.4 164.6 %reduce-scatter.28.cloned.1.call-start = ((), (), s32[]{:S(2)}) async-start(), calls=%async_computation.27 | async-start | bytes 2621440 | tf_op jit(solution)/shard_map/reduce_scatter | solution.py:243
  558.3 117.2 %reduce-scatter.18.cloned.1.call-start = ((), (), s32[]{:S(2)}) async-start(), calls=%async_computation.19 | async-start | bytes 2621440 | tf_op jit(solution)/shard_map/reduce_scatter | solution.py:229
  563.2 157.6 %reduce-scatter.22.cloned.1.call-start = ((), (), s32[]{:S(2)}) async-start(), calls=%async_computation.23 | async-start | bytes 2621440 | tf_op jit(solution)/shard_map/reduce_scatter | solution.py:229
  568.2 203.4 %all-gather.30.cloned.1.call-start = ((), (), s32[]{:S(2)}) async-start(), calls=%async_computation.28 | async-start | bytes 2621440 | tf_op jit(solution)/shard_map/all_gather | solution.py:251
  726.2 109.9 %all-gather.28.cloned.1.call-start = ((), (), s32[]{:S(2)}) async-start(), calls=%async_computation.25 | async-start | bytes 2621440 | tf_op jit(solution)/shard_map/all_gather | solution.py:251
  726.8 226.0 %reduce-scatter.30.cloned.1.call-start = ((), (), s32[]{:S(2)}) async-start(), calls=%async_computation.29 | async-start | bytes 2621440 | tf_op jit(solution)/shard_map/reduce_scatter | solution.py:265
  910.1 88.3 %reduce-scatter.26.cloned.1.call-start = ((), (), s32[]{:S(2)}) async-start(), calls=%async_computation.26 | async-start | bytes 2621440 | tf_op jit(solution)/shard_map/reduce_scatter | solution.py:265
  917.4 128.3 %reduce-scatter.38.cloned.1.call-start = ((), (), s32[]{:S(2)}) async-start(), calls=%async_computation.35 | async-start | bytes 3022848 | tf_op jit(solution)/shard_map/reduce_scatter | solution.py:142
  924.3 182.1 %reduce-scatter.36.cloned.1.call-start = ((), (), s32[]{:S(2)}) async-start(), calls=%async_computation.34 | async-start | bytes 6045696 | tf_op jit(solution)/shard_map/reduce_scatter | solution.py:141
  936.8 209.4 %reduce-scatter.34.cloned.1.call-start = ((), (), s32[]{:S(2)}) async-start(), calls=%async_computation.33 | async-start | bytes 1179648 | tf_op jit(solution)/shard_map/reduce_scatter | solution.py:140
  942.1 241.2 %reduce-scatter.40.cloned.1.call-start = ((), (), s32[]{:S(2)}) async-start(), calls=%async_computation.36 | async-start | bytes 589824
  1004.3 229.0 %reduce-scatter.32.cloned.1.call-start = ((), (), s32[]{:S(2)}) async-start(), calls=%async_computation.32 | async-start | bytes 3538944 | tf_op jit(solution)/shard_map/reduce_scatter | solution.py:139
  (87 other events, 3270.1 us)
Sparse Core Ops, SparseCore 0:
  10.5 29.2 all-gather.15
  42.0 45.9 all-gather.13
  126.2 42.5 reduce-scatter.15
  171.5 45.2 all-gather.23
  249.3 42.5 reduce-scatter.19
  294.3 30.0 all-gather.19
  326.5 45.9 all-gather.17
  375.0 23.5 all-gather.21
  400.7 45.9 all-gather.31
  448.7 44.6 all-gather.25
  495.0 44.6 all-gather.33
  541.8 42.5 reduce-scatter.23
  586.8 43.1 reduce-scatter.27
  632.2 43.1 reduce-scatter.17
  677.7 43.1 reduce-scatter.21
  726.3 45.2 all-gather.29
  773.0 44.6 all-gather.27
  910.2 42.5 reduce-scatter.29
  955.2 43.1 reduce-scatter.25
  1001.7 43.9 reduce-scatter.37
  1049.1 57.1 reduce-scatter.35
  1110.1 36.0 reduce-scatter.33
  1149.3 34.0 reduce-scatter.39
  1187.0 46.2 reduce-scatter.31
where the time goes:
time: 1260 us; the launch traced here: 1240 us
  waiting for transfers between devices  825 us (65%)
  matrix products  186 us (15%)
  local copies, waits for them, and re-layouts  97 us (8%)
  other arithmetic  83.5 us (7%)
  blocking collectives  33.1 us (3%)
  between operations  15.7 us (1%)
    all_gather x2, waiting for transfers between devices, per_device(): lax.all_gather(normed.astype(jnp.bfloat16), 'tensor', axis=0, tiled=True)  93.5 us
    reduce_scatter x2, waiting for transfers between devices, per_device(): lax.psum_scatter(contract_cols(hidden, contract_full).astype(jnp.bfloat16...  88 us
    all_gather x2, waiting for transfers between devices, per_device(): grad_rows = lax.all_gather(grad_output, 'tensor', axis=0, tiled=True)  86.7 us
    reduce_scatter x2, waiting for transfers between devices, per_device(): lax.psum_scatter(contract_cols(attended, attn_full).astype(jnp.bfloat16),...  82.9 us
    all_gather x2, waiting for transfers between devices, per_device(): lax.all_gather(normed_two.astype(jnp.bfloat16), 'tensor', axis=0, tiled=T...  75.6 us
    reduce_scatter x2, waiting for transfers between devices, per_device(): lax.psum_scatter(contract_cols(grad_lifted, expand_flat).astype(jnp.bfloa...  61.8 us
    reduce_scatter x1, waiting for transfers between devices, reduce_grads(): lax.psum_scatter(grad_list[2], 'dp', scatter_dimension=0, tiled=True)  57.5 us
    reduce_scatter x2, waiting for transfers between devices, per_device(): lax.psum_scatter(contract_cols(grad_mixed, qkv_flat).astype(jnp.bfloat16)...  50.9 us
  transfers between devices with their start and end apart: 24, of which 23 were waited for; matrix products, arithmetic and copies ran while one was open for 16% of the time, Pallas kernels for 0%

commit v1 on v0

v1 whole, which is shorter than its diff:
```python
import jax
import jax.numpy as jnp
from jax import lax
from jax.experimental import pallas as pl
from jax.experimental.pallas import tpu as pltpu
from jax.sharding import PartitionSpec as P

D = 1024
H = 16
DH = 64
FF = 2624
SEQ = 1024
STEP = 10

epsilon_norm = 1e-05
rope_theta = 160000.0
beta_first = 0.9
beta_second = 0.98
epsilon_adam = 1e-06
weight_decay = 1e-05

AXES = ("dp", "tensor")
bf16 = jnp.bfloat16
f32 = jnp.float32


def dot_nt(left, right):
    return lax.dot_general(left, right, (((1,), (1,)), ((), ())), preferred_element_type=f32)


def dot_tn(left, right):
    return lax.dot_general(left, right, (((0,), (0,)), ((), ())), preferred_element_type=f32)


def dot_nn(left, right):
    return jnp.dot(left, right, preferred_element_type=f32)


def adamw_update(weight, first_moment, second_moment, gradient, step_rate):
    first_new = beta_first * first_moment + (1.0 - beta_first) * gradient
    second_new = beta_second * second_moment + (1.0 - beta_second) * gradient * gradient
    first_hat = first_new / (1.0 - beta_first**STEP)
    second_hat = second_new / (1.0 - beta_second**STEP)
    weight_new = weight - step_rate * (
        first_hat / (jnp.sqrt(second_hat) + epsilon_adam) + weight_decay * weight
    )
    return (weight_new, first_new, second_new)


def swap_halves(values):
    lane = lax.broadcasted_iota(jnp.int32, values.shape, 1)
    return jnp.where(
        lane % DH < DH // 2,
        pltpu.roll(values, values.shape[1] - DH // 2, 1),
        pltpu.roll(values, DH // 2, 1),
    )


def qkv_kernel(own_ref, oth_ref, w_own_ref, w_oth_ref, cos_ref, sin_ref, q_ref, kv_ref):
    mixed = dot_nt(own_ref[...], w_own_ref[0]) + dot_nt(oth_ref[...], w_oth_ref[0])
    cosine, sine = cos_ref[...], sin_ref[...]
    query, key = mixed[:, :128], mixed[:, 128:256]
    query = query * cosine + swap_halves(query) * sine
    key = key * cosine + swap_halves(key) * sine
    q_ref[...] = query.astype(bf16) * bf16(DH**-0.5)
    kv_ref[:, :128] = key.astype(bf16)
    kv_ref[:, 128:] = mixed[:, 256:].astype(bf16)


def qkv_call(own, oth, w_own, w_oth, cosine, sine):
    rows = own.shape[0]
    blocks = w_own.shape[0]
    whole = lambda a: pl.BlockSpec(a.shape, lambda z: (0, 0))
    weight = pl.BlockSpec((1,) + w_own.shape[1:], lambda z: (z, 0, 0))
    return pl.pallas_call(
        qkv_kernel,
        grid=(blocks,),
        in_specs=[whole(own), whole(oth), weight, weight, whole(cosine), whole(sine)],
        out_specs=[
            pl.BlockSpec((rows, 128), lambda z: (0, z)),
            pl.BlockSpec((rows, 256), lambda z: (0, z)),
        ],
        out_shape=[
            jax.ShapeDtypeStruct((rows, blocks * 128), bf16),
            jax.ShapeDtypeStruct((rows, blocks * 256), bf16),
        ],
        compiler_params=pltpu.CompilerParams(vmem_limit_bytes=40 << 20),
        cost_estimate=pl.CostEstimate(
            flops=2 * rows * w_own.shape[1] * blocks * 2 * own.shape[1],
            bytes_accessed=4 * w_own.size + 8 * own.size,
            transcendentals=0,
        ),
        name="qkv_projection",
    )(own, oth, w_own, w_oth, cosine, sine)


def attend_kernel(q_ref, kv_own_ref, kv_oth_ref, out_ref, lse_ref):
    query = q_ref[...]
    key = jnp.concatenate([kv_own_ref[:, :128], kv_oth_ref[:, :128]], axis=0)
    value = jnp.concatenate([kv_own_ref[:, 128:], kv_oth_ref[:, 128:]], axis=0)
    value_t = value.astype(f32).T.astype(bf16)
    lane = lax.broadcasted_iota(jnp.int32, query.shape, 1)
    outs = []
    for head in range(2):
        query_head = jnp.where(lane // DH == head, query, jnp.zeros_like(query))
        scores = dot_nt(key, query_head)
        peak = jnp.max(scores, axis=0, keepdims=True)
        weights = jnp.exp(scores - peak)
        total = jnp.sum(weights, axis=0, keepdims=True)
        out = dot_nn(value_t[head * DH : (head + 1) * DH], weights.astype(bf16))
        outs.append(out / total)
        lse_ref[0, head : head + 1, :] = peak + jnp.log(total)
    out_ref[...] = jnp.concatenate(outs, axis=0).T.astype(bf16)


def attend_call(query, kv_own, kv_oth):
    rows = query.shape[0]
    blocks = query.shape[1] // 128
    kv_spec = pl.BlockSpec((rows, 256), lambda z: (0, z))
    q_spec = pl.BlockSpec((rows, 128), lambda z: (0, z))
    return pl.pallas_call(
        attend_kernel,
        grid=(blocks,),
        in_specs=[q_spec, kv_spec, kv_spec],
        out_specs=[q_spec, pl.BlockSpec((1, 2, rows), lambda z: (z, 0, 0))],
        out_shape=[
            jax.ShapeDtypeStruct(query.shape, bf16),
            jax.ShapeDtypeStruct((blocks, 2, rows), f32),
        ],
        compiler_params=pltpu.CompilerParams(vmem_limit_bytes=48 << 20),
        cost_estimate=pl.CostEstimate(
            flops=16 * rows * 2 * rows * 128 * blocks,
            bytes_accessed=12 * rows * 128 * blocks,
            transcendentals=4 * rows * rows * blocks,
        ),
        name="attention_forward",
    )(query, kv_own, kv_oth)


def attend_back_kernel(
    q_ref, kv_own_ref, kv_oth_ref, grad_ref, out_ref, lse_ref, cos_ref, sin_ref,
    dq_ref, dkv_own_ref, dkv_oth_ref,
):
    query, grad = q_ref[...], grad_ref[...]
    rows = query.shape[0]
    key = jnp.concatenate([kv_own_ref[:, :128], kv_oth_ref[:, :128]], axis=0)
    value = jnp.concatenate([kv_own_ref[:, 128:], kv_oth_ref[:, 128:]], axis=0)
    key_t = key.astype(f32).T.astype(bf16)
    product_t = (grad.astype(f32) * out_ref[...].astype(f32)).T
    lane = lax.broadcasted_iota(jnp.int32, query.shape, 1)
    grad_key = jnp.zeros((2 * rows, 128), f32)
    grad_value = jnp.zeros((2 * rows, 128), f32)
    grad_queries = []
    for head in range(2):
        mine = lane // DH == head
        query_head = jnp.where(mine, query, jnp.zeros_like(query))
        grad_head = jnp.where(mine, grad, jnp.zeros_like(grad))
        delta = jnp.sum(product_t[head * DH : (head + 1) * DH], axis=0, keepdims=True)
        weights = jnp.exp(dot_nt(key, query_head) - lse_ref[0, head : head + 1, :])
        grad_soft = dot_nt(value, grad_head)
        grad_scores = (weights * (grad_soft - delta)).astype(bf16)
        grad_value += dot_nn(weights.astype(bf16), grad_head)
        grad_key += dot_nn(grad_scores, query_head)
        grad_queries.append(dot_nn(key_t[head * DH : (head + 1) * DH], grad_scores))
    grad_query = jnp.concatenate(grad_queries, axis=0).T * (DH**-0.5)
    cosine, sine = cos_ref[...], sin_ref[...]
    dq_ref[...] = (grad_query * cosine - swap_halves(grad_query) * sine).astype(bf16)
    dkv_own_ref[:, :128] = grad_key[:rows]
    dkv_own_ref[:, 128:] = grad_value[:rows]
    dkv_oth_ref[:, :128] = grad_key[rows:].astype(bf16)
    dkv_oth_ref[:, 128:] = grad_value[rows:].astype(bf16)


def attend_back_call(query, kv_own, kv_oth, grad, out, lse, cosine, sine):
    rows = query.shape[0]
    blocks = query.shape[1] // 128
    kv_spec = pl.BlockSpec((rows, 256), lambda z: (0, z))
    q_spec = pl.BlockSpec((rows, 128), lambda z: (0, z))
    whole = lambda a: pl.BlockSpec(a.shape, lambda z: (0, 0))
    return pl.pallas_call(
        attend_back_kernel,
        grid=(blocks,),
        in_specs=[
            q_spec, kv_spec, kv_spec, q_spec, q_spec,
            pl.BlockSpec((1, 2, rows), lambda z: (z, 0, 0)), whole(cosine), whole(sine),
        ],
        out_specs=[q_spec, kv_spec, kv_spec],
        out_shape=[
            jax.ShapeDtypeStruct(query.shape, bf16),
            jax.ShapeDtypeStruct(kv_own.shape, f32),
            jax.ShapeDtypeStruct(kv_own.shape, bf16),
        ],
        compiler_params=pltpu.CompilerParams(vmem_limit_bytes=56 << 20),
        cost_estimate=pl.CostEstimate(
            flops=40 * rows * 2 * rows * 128 * blocks,
            bytes_accessed=30 * rows * 128 * blocks,
            transcendentals=4 * rows * rows * blocks,
        ),
        name="attention_backward",
    )(query, kv_own, kv_oth, grad, out, lse, cosine, sine)


def join_kernel(dq_ref, own_ref, got_ref, cos_ref, sin_ref, mixed_ref):
    total = own_ref[...] + got_ref[...].astype(f32)
    key = total[:, :128]
    mixed_ref[:, :128] = dq_ref[...]
    mixed_ref[:, 128:256] = (key * cos_ref[...] - swap_halves(key) * sin_ref[...]).astype(bf16)
    mixed_ref[:, 256:] = total[:, 128:].astype(bf16)


def join_call(dq, dkv_own, dkv_got, cosine, sine):
    rows = dq.shape[0]
    blocks = dq.shape[1] // 128
    spec = lambda width: pl.BlockSpec((rows, width), lambda z: (0, z))
    whole = lambda a: pl.BlockSpec(a.shape, lambda z: (0, 0))
    return pl.pallas_call(
        join_kernel,
        grid=(blocks,),
        in_specs=[spec(128), spec(256), spec(256), whole(cosine), whole(sine)],
        out_specs=spec(384),
        out_shape=jax.ShapeDtypeStruct((rows, 384 * blocks), bf16),
        cost_estimate=pl.CostEstimate(
            flops=rows * 384 * blocks, bytes_accessed=10 * rows * 256 * blocks, transcendentals=0
        ),
        name="grad_mixed",
    )(dq, dkv_own, dkv_got, cosine, sine)


def norm_stats(halves):
    width = sum(h.shape[1] for h in halves)
    mean = sum(jnp.sum(h, axis=1, keepdims=True) for h in halves) / width
    centered = [h - mean for h in halves]
    variance = sum(jnp.sum(c * c, axis=1, keepdims=True) for c in centered) / width
    return mean, lax.rsqrt(variance + epsilon_norm)


def norm_back(grads, halves, mean, scale, gains):
    width = sum(h.shape[1] for h in halves)
    hats = [(h - mean) * scale for h in halves]
    gain_grads = [jnp.sum(g * n, axis=0) for g, n in zip(grads, hats)]
    errors = [g * gain[None, :] for g, gain in zip(grads, gains)]
    average = sum(jnp.sum(e, axis=1, keepdims=True) for e in errors) / width
    along = sum(jnp.sum(e * n, axis=1, keepdims=True) for e, n in zip(errors, hats)) / width
    return [scale * (e - average - n * along) for e, n in zip(errors, hats)], gain_grads


def make_per_device(dp, tensor):
    count = dp * tensor
    chips = dp // 2
    chip_bits = chips.bit_length() - 1

    def permute(value, pairs):
        return lax.ppermute(value, AXES, pairs)

    def exchange(value, mask):
        return permute(value, [(i, i ^ mask) for i in range(count)])

    def over_chip(value, bit):
        return exchange(value, (2 * tensor) << bit)

    def over_core(value):
        return exchange(value, tensor)

    def spread_pairs(r, k):
        pairs = []
        for i in range(count):
            z = i % tensor
            core = (i // tensor) % 2
            chip = i // (2 * tensor)
            a, b = z // 2, z % 2
            pairs.append((i, (chip * 2 + (k ^ b)) * tensor + (r ^ a) * 2 + core))
        return pairs

    combos = [(r, k) for r in range(2) for k in range(2)]

    def gather_chunks(chunks):
        if chip_bits != 2:
            results = []
            for chunk in chunks:
                current = jnp.stack([chunk] + [exchange(chunk, k) for k in range(1, tensor)])[None]
                for bit in range(chip_bits):
                    current = jnp.concatenate([current, over_chip(current, bit)], axis=0)
                current = current.transpose(1, 2, 0, 3)
                current = current.reshape(current.shape[:2] + (-1,))
                results.append((current, over_core(current)))
            return results
        total = len(chunks)
        column, near, far, owned, results = ({} for _ in range(5))
        before = None
        for slot in range(total + 3):
            inputs = {}
            if slot < total:
                inputs["a"] = chunks[slot]
            if 0 <= slot - 1 < total:
                inputs["b"] = column[slot - 1]
            if 0 <= slot - 2 < total:
                x_got, y_got = near[slot - 2]
                inputs["c"] = (x_got[: tensor // 2], y_got[tensor // 2 :])
            if 0 <= slot - 3 < total:
                inputs["d"] = owned[slot - 3]
            if before is not None:
                inputs, before = lax.optimization_barrier((inputs, before))
            outputs = {}
            if "c" in inputs:
                outputs["c"] = (over_chip(inputs["c"][0], 1), over_chip(inputs["c"][1], 0))
            if "b" in inputs:
                outputs["b"] = (over_chip(inputs["b"], 0), over_chip(inputs["b"], 1))
            if "a" in inputs:
                outputs["a"] = [exchange(inputs["a"], k) for k in range(1, tensor)]
            if "d" in inputs:
                outputs["d"] = over_core(inputs["d"])
            if "a" in inputs:
                column[slot] = jnp.stack([inputs["a"]] + outputs["a"])
            if "b" in inputs:
                near[slot - 1] = outputs["b"]
            if "c" in inputs:
                k = slot - 2
                diagonal = jnp.concatenate(outputs["c"], axis=0)
                owned[k] = jnp.concatenate([column[k], near[k][0], near[k][1], diagonal], axis=-1)
            if "d" in inputs:
                results[slot - 3] = (inputs["d"], outputs["d"])
            before = outputs
        return [results[k] for k in range(total)]

    def low_sum(left, right):
        return (left.astype(f32) + right.astype(f32)).astype(bf16)

    def reduce_chunk(own, other):
        block = own.shape[-1] // chips
        total = low_sum(own, over_core(other))
        parts = [total[..., j * block : (j + 1) * block] for j in range(chips)]
        if chip_bits != 2:
            current = jnp.stack(parts)
            for bit in reversed(range(chip_bits)):
                half = current.shape[0] // 2
                current = low_sum(current[:half], over_chip(current[half:], bit))
            mine = current[0]
        else:
            mine, x_part, y_part, diagonal = parts
            half = tensor // 2
            to_y = over_chip(diagonal[:half], 0)
            to_x = over_chip(diagonal[half:], 1)
            y_part = jnp.concatenate([low_sum(y_part[:half], to_y), y_part[half:]], axis=0)
            x_part = jnp.concatenate([x_part[:half], low_sum(x_part[half:], to_x)], axis=0)
            x_got, y_got = over_chip(x_part, 0), over_chip(y_part, 1)
            mine = (mine.astype(f32) + x_got.astype(f32) + y_got.astype(f32)).astype(bf16)
        result = mine[0].astype(f32)
        for k in range(1, tensor):
            result = result + exchange(mine[k], k).astype(f32)
        return result

    def per_device(
        inputs,
        cotangent,
        attention_in,
        attention_out,
        expand_weight,
        contract_weight,
        norm_gains,
        attention_in_first,
        attention_in_second,
        attention_out_first,
        attention_out_second,
        expand_first,
        expand_second,
        contract_first,
        contract_second,
        gains_first,
        gains_second,
    ):
        block = attention_in.shape[0]
        head_columns = attention_in.shape[2]
        hidden_local = expand_weight.shape[2]
        local_rows = inputs.shape[2]
        piece = local_rows // 2
        width = inputs.shape[3]
        me_dp = lax.axis_index("dp")
        me_z = lax.axis_index("tensor")
        core = me_dp % 2
        z_high, z_low = me_z // 2, me_z % 2

        order = [(j % chips) * 2 + j // chips for j in range(dp)]

        def to_relative(values):
            pieces = [
                lax.dynamic_slice_in_dim(values, (me_dp ^ o) * block, block, values.ndim - 1)
                for o in order
            ]
            return (
                jnp.concatenate(pieces[:chips], axis=-1),
                jnp.concatenate(pieces[chips:], axis=-1),
            )

        def from_relative(own, other):
            both = jnp.concatenate([own, other], axis=-1)
            pieces = []
            for i in range(dp):
                relative = me_dp ^ i
                j = (relative % 2) * chips + relative // 2
                pieces.append(lax.dynamic_slice_in_dim(both, j * block, block, both.ndim - 1))
            return jnp.concatenate(pieces, axis=-1)

        def spread(values):
            got = []
            for r, k in combos:
                part = lax.dynamic_index_in_dim(values[:, 0], r ^ z_high, 0, keepdims=False)
                part = lax.dynamic_slice_in_dim(part, (k ^ z_low) * piece, piece, 0)
                got.append(permute(part, spread_pairs(r, k)))
            return jnp.concatenate(got, axis=0)

        def collect(values):
            back = []
            for index, (r, k) in enumerate(combos):
                part = values[index * piece : (index + 1) * piece]
                back.append(permute(part, [(b, a) for a, b in spread_pairs(r, k)]))
            back = jnp.stack(back)
            rows = []
            for m in range(2):
                halves = [
                    lax.dynamic_index_in_dim(
                        back, (m ^ z_high) * 2 + (h ^ z_low), 0, keepdims=False
                    )
                    for h in range(2)
                ]
                rows.append(jnp.concatenate(halves, axis=0))
            return jnp.stack(rows)[:, None]

        low_in = attention_in.astype(bf16).reshape(block, 3, 2, head_columns // 2)
        low_in = low_in.transpose(2, 1, 3, 0).reshape(2, -1, block)
        low_out = attention_out.astype(bf16).T
        low_expand = expand_weight.astype(bf16).transpose(1, 2, 0)
        low_contract = contract_weight.astype(bf16).T
        gathered = gather_chunks(
            [low_in[0], low_in[1], low_out, low_expand[0], low_expand[1], low_contract]
        )
        w_in = gathered[:2]
        flat = lambda a: a.reshape(-1, a.shape[-1])
        w_out, w_up, w_gate, w_down = [tuple(flat(h) for h in pair) for pair in gathered[2:]]
        gains = lax.all_gather(norm_gains.astype(bf16), "dp", axis=1, tiled=True).astype(f32)
        gain_own, gain_oth = to_relative(gains)
        gain_one = (gain_own[0], gain_oth[0])
        gain_two = (gain_own[1], gain_oth[1])

        starts = [((r ^ z_high) * 2 + (k ^ core)) * local_rows + core * piece for r, k in combos]
        positions = jnp.concatenate([s + jnp.arange(piece) for s in starts]).astype(f32)
        exponents = jnp.arange(0, DH, 2).astype(f32) / DH
        angles = positions[:, None] * jnp.power(rope_theta, -exponents)[None, :]
        cosine, sine = jnp.cos(angles), jnp.sin(angles)
        cosine = jnp.concatenate([cosine] * 4, axis=-1)
        sine = jnp.concatenate([-sine, sine] * 2, axis=-1)

        sequence = to_relative(spread(inputs))
        sequence = [h.astype(f32) for h in sequence]
        mean_one, scale_one = norm_stats(sequence)
        normed = [
            ((h - mean_one) * scale_one * g[None, :]).astype(bf16)
            for h, g in zip(sequence, gain_one)
        ]
        queries, kv_own, kv_oth, attended, lse = [], [], [], [], []
        for p in range(2):
            q, kv = qkv_call(*normed, *w_in[p], cosine, sine)
            got = over_core(kv)
            out, totals = attend_call(q, kv, got)
            queries.append(q)
            kv_own.append(kv)
            kv_oth.append(got)
            attended.append(out)
            lse.append(totals)
        rows = attended[0].shape[0]
        attended_all = jnp.stack([a.reshape(rows, tensor, -1) for a in attended], axis=2)
        attended_all = attended_all.reshape(rows, -1)
        middle = [s + dot_nn(attended_all, w) for s, w in zip(sequence, w_out)]
        mean_two, scale_two = norm_stats(middle)
        normed_two = [
            ((h - mean_two) * scale_two * g[None, :]).astype(bf16)
            for h, g in zip(middle, gain_two)
        ]
        lifted_in = dot_nt(normed_two[0], w_up[0]) + dot_nt(normed_two[1], w_up[1])
        lifted_gate = dot_nt(normed_two[0], w_gate[0]) + dot_nt(normed_two[1], w_gate[1])
        phi = 0.5 * (1.0 + lax.erf(lifted_in * (0.5**0.5)))
        gelu = lifted_in * phi
        hidden = (gelu * lifted_gate).astype(bf16)
        slope = phi + lifted_in * jnp.exp(-0.5 * lifted_in * lifted_in) * 0.3989422804014327
        to_gate = gelu.astype(bf16)
        to_in = (lifted_gate * slope).astype(bf16)
        outputs = [
            (m + dot_nn(hidden, w)).astype(bf16) for m, w in zip(middle, w_down)
        ]
        layer_output = collect(from_relative(*outputs))

        grad_rows = to_relative(spread(cotangent))

        def shards(left, right):
            grads = dot_tn(left, right).astype(bf16)
            return grads.reshape(tensor, -1, grads.shape[-1])

        grad_down = reduce_chunk(*[shards(hidden, g) for g in grad_rows])
        grad_hidden = dot_nt(grad_rows[0], w_down[0]) + dot_nt(grad_rows[1], w_down[1])
        grad_in = (grad_hidden * to_in.astype(f32)).astype(bf16)
        grad_gate = (grad_hidden * to_gate.astype(f32)).astype(bf16)
        grad_up = reduce_chunk(*[shards(grad_in, n) for n in normed_two])
        grad_gates = reduce_chunk(*[shards(grad_gate, n) for n in normed_two])
        grad_two = [dot_nn(grad_in, u) + dot_nn(grad_gate, g) for u, g in zip(w_up, w_gate)]
        back_two, gain_two_grad = norm_back(grad_two, middle, mean_two, scale_two, gain_two)
        grad_middle = [g.astype(f32) + b for g, b in zip(grad_rows, back_two)]
        middle_low = [g.astype(bf16) for g in grad_middle]
        grad_out = reduce_chunk(*[shards(attended_all, m) for m in middle_low])
        grad_attended = dot_nt(middle_low[0], w_out[0]) + dot_nt(middle_low[1], w_out[1])
        grad_attended = grad_attended.astype(bf16).reshape(rows, tensor, 2, -1)
        grad_in_parts, grad_one = [], [0.0, 0.0]
        for p in range(2):
            dq, dkv, dkv_far = attend_back_call(
                queries[p],
                kv_own[p],
                kv_oth[p],
                grad_attended[:, :, p].reshape(rows, -1),
                attended[p],
                lse[p],
                cosine,
                sine,
            )
            grad_mixed = join_call(dq, dkv, over_core(dkv_far), cosine, sine)
            grad_in_parts.append(reduce_chunk(*[shards(grad_mixed, n) for n in normed]))
            grad_one = [g + dot_nn(grad_mixed, flat(w)) for g, w in zip(grad_one, w_in[p])]
        back_one, gain_one_grad = norm_back(grad_one, sequence, mean_one, scale_one, gain_one)
        input_grads = [(g + b).astype(bf16) for g, b in zip(grad_middle, back_one)]
        input_gradient = collect(from_relative(*input_grads))

        gain_grads = jnp.stack(
            [from_relative(*gain_one_grad), from_relative(*gain_two_grad)]
        )
        gain_total = lax.psum(gain_grads, AXES)
        gain_total = lax.dynamic_slice_in_dim(gain_total, me_dp * block, block, 1)
        grad_qkv = jnp.stack([g.reshape(3, -1, block) for g in grad_in_parts], axis=1)
        grad_qkv = grad_qkv.reshape(3, head_columns, block).transpose(2, 0, 1)
        grad_expand = jnp.stack([grad_up, grad_gates]).transpose(2, 0, 1)
        step_rates = (
            2.5 * D ** (-0.5),
            2.5 * max(1, 4 * H * DH // SEQ) ** (-0.5),
            2.5 * D ** (-0.5),
            2.5 * FF ** (-0.5),
            0.25,
        )
        qkv_new = adamw_update(
            attention_in, attention_in_first, attention_in_second, grad_qkv, step_rates[0]
        )
        out_new = adamw_update(
            attention_out, attention_out_first, attention_out_second, grad_out.T, step_rates[1]
        )
        expand_new = adamw_update(
            expand_weight, expand_first, expand_second, grad_expand, step_rates[2]
        )
        contract_new = adamw_update(
            contract_weight, contract_first, contract_second, grad_down.T, step_rates[3]
        )
        gains_new = adamw_update(norm_gains, gains_first, gains_second, gain_total, step_rates[4])
        return (
            layer_output,
            input_gradient,
            *qkv_new,
            *out_new,
            *expand_new,
            *contract_new,
            *gains_new,
        )

    return per_device


def solution(mesh):
    activation = P(None, "dp", "tensor", None)
    cube = P("dp", None, "tensor")
    flat = P("dp", "tensor")
    gain = P(None, "dp")
    return jax.shard_map(
        make_per_device(mesh.shape["dp"], mesh.shape["tensor"]),
        mesh=mesh,
        in_specs=(
            activation, activation, cube, flat, cube, flat, gain,
            cube, cube, flat, flat, cube, cube, flat, flat, gain, gain,
        ),
        out_specs=(
            activation, activation, cube, cube, cube, flat, flat, flat,
            cube, cube, cube, flat, flat, flat, gain, gain, gain,
        ),
        check_vma=False,
    )
```

time: 1260 us -> 660 us (0.52)
  waiting for transfers between devices: 825 us -> 174 us
  starting transfers between devices: 2.04 us -> 134 us
  matrix products: 186 us -> 97.5 us
  Pallas kernels: 0 us -> 67.1 us
  local copies, waits for them, and re-layouts: 97 us -> 55.6 us
  blocking collectives: 33.1 us -> 57.1 us
  other arithmetic: 83.5 us -> 60.7 us
    reduce_scatter x12 -> x0, waiting for transfers between devices: 449 us -> none  [the longest x2 88 us: per_device(): lax.psum_scatter(contract_cols(hidden, contract_full).astype(jnp.bfloat16...]
    all_gather x11 -> x0, waiting for transfers between devices: 344 us -> none  [the longest x2 93.5 us: per_device(): lax.all_gather(normed.astype(jnp.bfloat16), 'tensor', axis=0, tiled=True)]
    ppermute x0 -> x116, waiting for transfers between devices: none -> 174 us  [permute(): return lax.ppermute(value, AXES, pairs)]
    ppermute x0 -> x116, starting transfers between devices: none -> 134 us  [permute(): return lax.ppermute(value, AXES, pairs)]
    dot_general x52 -> x32, matrix products: 186 us -> 97.5 us  [the longest x12 34.7 us: dot_nn(): return jnp.dot(left, right, preferred_element_type=f32)]
    pallas_call x0 -> x8, Pallas kernels: none -> 67.1 us  [the longest x2 29 us: attend_back_call(): pl.pallas_call(attend_back_kernel, grid=(blocks,), in_specs=[q_spec, kv_s...]
    dynamic_update_slice x8 -> x0, local copies, waits for them, and re-layouts: 43.7 us -> none  [attend_forward(): blocks_out, log_totals = lax.map(one_block, query_blocks)]
    unnamed x25 -> x0, waiting for transfers between devices: 32.7 us -> none
  transfers between devices with their start and end apart: 24 -> 116, of which waited for: 23 -> 51; matrix products, arithmetic and copies ran while one was open for 16% -> 22% of each run, Pallas kernels for 0% -> 8%
where the time goes in v1:
time: 660 us; the launch traced here: 649 us
  waiting for transfers between devices  174 us (26%)
  starting transfers between devices  134 us (20%)
  matrix products  97.5 us (15%)
  Pallas kernels  67.1 us (10%)
  other arithmetic  60.7 us (9%)
  blocking collectives  57.1 us (9%)
  local copies, waits for them, and re-layouts  55.6 us (8%)
    ppermute x116, waiting for transfers between devices, permute(): return lax.ppermute(value, AXES, pairs)  174 us
    ppermute x116, starting transfers between devices, permute(): return lax.ppermute(value, AXES, pairs)  134 us
    psum x1, blocking collectives, per_device(): gain_total = lax.psum(gain_grads, AXES)  37.4 us
    dot_general x12, matrix products, dot_nn(): return jnp.dot(left, right, preferred_element_type=f32)  34.7 us
    dot_general x12, matrix products, dot_tn(): lax.dot_general(left, right, (((0,), (0,)), ((), ())), preferred_element_...  34.1 us
    pallas_call x2, Pallas kernels, attend_back_call(): pl.pallas_call(attend_back_kernel, grid=(blocks,), in_specs=[q_spec, kv_s...  29 us
    dot_general x8, matrix products, dot_nt(): lax.dot_general(left, right, (((1,), (1,)), ((), ())), preferred_element_...  28.8 us
    all_gather x1, blocking collectives, per_device(): lax.all_gather(norm_gains.astype(bf16), 'dp', axis=1, tiled=True)  19.6 us
  transfers between devices with their start and end apart: 116, of which 51 were waited for; matrix products, arithmetic and copies ran while one was open for 22% of the time, Pallas kernels for 8%

profile of v1, /device:TPU:0, one launch (start us, length us, event | category | flops | bytes accessed | tf_op | source)
XLA Modules:
  0.0 649.1 jit_solution(6340382016102880623)
XLA Ops:
  2.0 5.1 collective-permute-start.6
  41.8 5.2 collective-permute-done.15
  57.9 6.7 %collective-permute-done.22 = bf16[656,128]{1,0:T(8,128)(2,1)S(1)} collective-permute-done((bf16[656,128]{1,0:T(8,128)(2,1)S(1)}, bf16[656,128]{1,0:T(8,128)(2,1)S(1)}, u32[]{:S(2)}, u32[]{:S(2)}) %collective-permute-start.22) | collective-permute-done | bytes 167968 | tf_op jit(solution)/shard_map/ppermute | solution.py:253
  80.0 19.6 %all_gather.3 = bf16[2,1024]{1,0:T(2,128)(2,1)S(1)} all-gather(bf16[2,128]{1,0:T(2,128)(2,1)S(1)} %convert_element_type.478), channel_id=1, replica_groups=mesh['dp'=8,'tensor'=4] {'dp'}, dimensions={1}, use_global_device_ids=true | all-gather | bytes 4608 | tf_op jit(solution)/shard_map/all_gather | solution.py:439
  102.4 5.1 collective-permute-done.35
  108.1 6.1 collective-permute-start.30
  132.9 5.3 collective-permute-done.39
  165.1 8.6 %collective-permute-done.2 = bf16[128,1024]{1,0:T(8,128)(2,1)} collective-permute-done((bf16[128,1024]{1,0:T(8,128)(2,1)}, bf16[128,1024]{1,0:T(8,128)(2,1)}, u32[]{:S(2)}, u32[]{:S(2)}) %collective-permute-start.2) | collective-permute-done | bytes 262176 | tf_op jit(solution)/shard_map/ppermute | solution.py:253
  185.6 13.1 %collective-permute-done.49 = bf16[2,656,128]{2,1,0:T(8,128)(2,1)S(1)} collective-permute-done((bf16[2,656,128]{2,1,0:T(8,128)(2,1)S(1)}, bf16[2,656,128]{2,1,0:T(8,128)(2,1)S(1)}, u32[]{:S(2)}, u32[]{:S(2)}) %collective-permute-start.49) | collective-permute-done | bytes 335904 | tf_op jit(solution)/shard_map/ppermute | solution.py:253
  202.1 6.0 qkv_projection.3
  217.0 13.4 %collective-permute-done.60 = bf16[128,1024]{1,0:T(8,128)(2,1)S(1)} collective-permute-done((bf16[128,1024]{1,0:T(8,128)(2,1)S(1)}, bf16[128,1024]{1,0:T(8,128)(2,1)S(1)}, u32[]{:S(2)}, u32[]{:S(2)}) %collective-permute-start.60) | collective-permute-done | bytes 262176 | tf_op jit(solution)/shard_map/ppermute | solution.py:253
  231.6 8.9 %attention_forward.2 = (bf16[512,512]{1,0:T(8,128)(2,1)S(1)}, f32[4,2,512]{2,1,0:T(2,128)S(1)}) custom-call(bf16[512,512]{1,0:T(8,128)(2,1)S(1)} %get-tuple-element.67.q_ref, bf16[512,1024]{1,0:T(8,128)(2,1)S(1)} %get-tuple-element.68.kv_own_ref, bf16[512,1024]{1,0:T(8,128)(2,1)S(1)} %collective-permute-done.20.kv_oth_ref), custom_call_target="tpu_custom_call" | custom-call | flops 4294967296 | bytes 3145728 | tf_op jit(solution)/shard_map/attention_forward/pallas_call | solution.py:121
  242.5 9.9 %attention_forward.3 = (bf16[512,512]{1,0:T(8,128)(2,1)S(1)}, f32[4,2,512]{2,1,0:T(2,128)S(1)}) custom-call(bf16[512,512]{1,0:T(8,128)(2,1)S(1)} %copy-done.13, bf16[512,1024]{1,0:T(8,128)(2,1)} %get-tuple-element.76.kv_own_ref, bf16[512,1024]{1,0:T(8,128)(2,1)} %collective-permute-done.29.kv_oth_ref), custom_call_target="tpu_custom_call" | custom-call | flops 4294967296 | bytes 3145728 | tf_op jit(solution)/shard_map/attention_forward/pallas_call | solution.py:121
  287.4 8.4 %multiply_convert_fusion.1 = (bf16[512,2624]{0,1:T(8,128)(2,1)}, bf16[512,2624]{0,1:T(8,128)(2,1)}, bf16[512,2624]{0,1:T(8,128)(2,1)}) fusion(f32[512,2624]{0,1:T(8,128)S(1)} %convolution_add_fusion.1, f32[512,2624]{0,1:T(8,128)S(1)} %convolution_add_fusion.2, f32[512,2624]{0,1:T(8,128)S(1)} %fusion.101, bf16[2624,512]{1,0:T(8,128)(2,1)} %bitcast.325, ...), kind=kOutput, calls=%fused_computation.14 | convolution fusion | flops 1406042112 | bytes 27394048 | tf_op jit(solution)/shard_map/dot_general | solution.py:28
  337.4 7.7 %slice_reduce_fusion.1 = (bf16[512,4,128]{2,1,0:T(4,128)(2,1)S(1)}, bf16[512,4,128]{2,1,0:T(4,128)(2,1)S(1)}) fusion(bf16[512,4,2,128]{3,2,1,0:T(2,128)(2,1)} %reshape.266), kind=kLoop, calls=%fused_computation.121 | loop fusion | bytes 2097152 | tf_op jit(solution)/shard_map/slice | solution.py:516
  346.0 14.5 %attention_backward.3 = (bf16[512,512]{1,0:T(8,128)(2,1)}, f32[512,1024]{1,0:T(8,128)}, bf16[512,1024]{1,0:T(8,128)(2,1)}) custom-call(bf16[512,512]{1,0:T(8,128)(2,1)} %copy-done.12, bf16[512,1024]{1,0:T(8,128)(2,1)} %get-tuple-element.76.kv_own_ref, bf16[512,1024]{1,0:T(8,128)(2,1)} %collective-permute-done.29.kv_oth_ref, bf16[512,512]{1,0:T(8,128)(2,1)} %bitcast.374, ...), custom_call_target="tpu_custom_call" | custom-call | flops 10737418240 | bytes 7864320 | tf_op jit(solution)/shard_map/attention_backward/pallas_call | solution.py:180
  368.9 14.5 %attention_backward.2 = (bf16[512,512]{1,0:T(8,128)(2,1)}, f32[512,1024]{1,0:T(8,128)}, bf16[512,1024]{1,0:T(8,128)(2,1)}) custom-call(bf16[512,512]{1,0:T(8,128)(2,1)} %copy-done.11, bf16[512,1024]{1,0:T(8,128)(2,1)} %copy-done.9, bf16[512,1024]{1,0:T(8,128)(2,1)} %copy-done.10, bf16[512,512]{1,0:T(8,128)(2,1)} %bitcast.373, bf16[512,512]{1,0:T(8,128)(2,1)} %copy-done.2, ...), custom_call_target="tpu_custom_call" | custom-call | flops 10737418240 | bytes 7864320 | tf_op jit(solution)/shard_map/attention_backward/pallas_call | solution.py:180
  394.6 5.1 convolution_convert_fusion.4
  420.8 4.7 grad_mixed.2
  448.9 37.4 %psum.7 = f32[2,1024]{1,0:T(2,128)S(1)} all-reduce(f32[2,1024]{1,0:T(2,128)S(1)} %pad_maximum_fusion.28), channel_id=1, replica_groups=mesh['dp'=8,'tensor'=4] {'dp','tensor'}, use_global_device_ids=true, to_apply=%region_20.21 | all-reduce | flops 2048 | bytes 16384 | tf_op jit(solution)/shard_map/psum | solution.py:532
  506.4 5.9 collective-permute-done.91
  512.4 5.2 collective-permute-done.90
  612.3 6.5 collective-permute-done.112
  632.5 9.3 %collective-permute-done.98 = bf16[656,128]{1,0:T(8,128)(2,1)S(1)} collective-permute-done((bf16[656,128]{1,0:T(8,128)(2,1)S(1)}, bf16[656,128]{1,0:T(8,128)(2,1)S(1)}, u32[]{:S(2)}, u32[]{:S(2)}) %collective-permute-start.98) | collective-permute-done | bytes 167968 | tf_op jit(solution)/shard_map/ppermute | solution.py:253
  (743 shorter events, 413.2 us)
Async XLA Ops:
  75.5 47.5 %collective-permute-start.28 = (bf16[4,384,512]{2,1,0:T(8,128)(2,1)}, bf16[4,384,512]{2,1,0:T(8,128)(2,1)}, u32[]{:S(2)}, u32[]{:S(2)}) collective-permute-start(bf16[4,384,512]{2,1,0:T(8,128)(2,1)} %maximum_maximum_fusion.4.w_own_ref), channel_id=1, source_target_pairs={{0,4},{1,5},{2,6},{3,7},{4,0},{5,1},{6,2},{7,3},{8,12},{9,13},{10,... | collective-permute-start | bytes 4718600 | tf_op jit(solution)/shard_map/ppermute | solution.py:253
  75.6 44.0 %collective-permute-start.33 = (bf16[4,656,128]{2,1,0:T(8,128)(2,1)}, bf16[4,656,128]{2,1,0:T(8,128)(2,1)}, u32[]{:S(2)}, u32[]{:S(2)}) collective-permute-start(bf16[4,656,128]{2,1,0:T(8,128)(2,1)} %pad_maximum_fusion.3), channel_id=1, source_target_pairs={{0,8},{1,9},{2,10},{3,11},{4,12},{5,13},{6,14},{7,15},{8,0},{9,1},... | collective-permute-start | bytes 2015240 | tf_op jit(solution)/shard_map/ppermute | solution.py:253
  76.7 44.7 %collective-permute-start.34 = (bf16[4,656,128]{2,1,0:T(8,128)(2,1)}, bf16[4,656,128]{2,1,0:T(8,128)(2,1)}, u32[]{:S(2)}, u32[]{:S(2)}) collective-permute-start(bf16[4,656,128]{2,1,0:T(8,128)(2,1)} %pad_maximum_fusion.3), channel_id=1, source_target_pairs={{0,16},{1,17},{2,18},{3,19},{4,20},{5,21},{6,22},{7,23},{8,24},{9,... | collective-permute-start | bytes 2015240 | tf_op jit(solution)/shard_map/ppermute | solution.py:253
  125.2 31.6 %collective-permute-start.37 = (bf16[4,256,512]{2,1,0:T(8,128)(2,1)S(1)}, bf16[4,256,512]{2,1,0:T(8,128)(2,1)}, u32[]{:S(2)}, u32[]{:S(2)}) collective-permute-start(bf16[4,256,512]{2,1,0:T(8,128)(2,1)S(1)} %maximum_maximum_fusion.5), channel_id=1, source_target_pairs={{0,4},{1,5},{2,6},{3,7},{4,0},{5,1},{6,2},{7,3},{8,12},{9,13},{10,... | collective-permute-start | bytes 3145736 | tf_op jit(solution)/shard_map/ppermute | solution.py:253
  156.8 55.5 %collective-permute-start.45 = (bf16[4,656,512]{2,1,0:T(8,128)(2,1)}, bf16[4,656,512]{2,1,0:T(8,128)(2,1)}, u32[]{:S(2)}, u32[]{:S(2)}) collective-permute-start(bf16[4,656,512]{2,1,0:T(8,128)(2,1)} %maximum_maximum_fusion), channel_id=1, source_target_pairs={{0,4},{1,5},{2,6},{3,7},{4,0},{5,1},{6,2},{7,3},{8,12},{9,13},{10,... | collective-permute-start | bytes 8060936 | tf_op jit(solution)/shard_map/ppermute | solution.py:253
  176.9 31.4 %collective-permute-start.46 = (bf16[4,656,128]{2,1,0:T(8,128)(2,1)S(1)}, bf16[4,656,128]{2,1,0:T(8,128)(2,1)S(1)}, u32[]{:S(2)}, u32[]{:S(2)}) collective-permute-start(bf16[4,656,128]{2,1,0:T(8,128)(2,1)S(1)} %copy-done.89), channel_id=1, source_target_pairs={{0,8},{1,9},{2,10},{3,11},{4,12},{5,13},{6,14},{7,15},{8,0},{9,1},... | collective-permute-start | bytes 2015240 | tf_op jit(solution)/shard_map/ppermute | solution.py:253
  177.6 34.4 %collective-permute-start.47 = (bf16[4,656,128]{2,1,0:T(8,128)(2,1)S(1)}, bf16[4,656,128]{2,1,0:T(8,128)(2,1)S(1)}, u32[]{:S(2)}, u32[]{:S(2)}) collective-permute-start(bf16[4,656,128]{2,1,0:T(8,128)(2,1)S(1)} %copy-done.89), channel_id=1, source_target_pairs={{0,16},{1,17},{2,18},{3,19},{4,20},{5,21},{6,22},{7,23},{8,24},{9,... | collective-permute-start | bytes 2015240 | tf_op jit(solution)/shard_map/ppermute | solution.py:253
  179.9 28.1 %collective-permute-start.48 = (bf16[2,656,128]{2,1,0:T(8,128)(2,1)S(1)}, bf16[2,656,128]{2,1,0:T(8,128)(2,1)S(1)}, u32[]{:S(2)}, u32[]{:S(2)}) collective-permute-start(bf16[2,656,128]{2,1,0:T(8,128)(2,1)S(1)} %copy-done.122), channel_id=1, source_target_pairs={{0,16},{1,17},{2,18},{3,19},{4,20},{5,21},{6,22},{7,23},{8,24},{9,... | collective-permute-start | bytes 1007624 | tf_op jit(solution)/shard_map/ppermute | solution.py:253
  198.7 32.8 %collective-permute-start.20 = (bf16[512,1024]{1,0:T(8,128)(2,1)S(1)}, bf16[512,1024]{1,0:T(8,128)(2,1)S(1)}, u32[]{:S(2)}, u32[]{:S(2)}) collective-permute-start(bf16[512,1024]{1,0:T(8,128)(2,1)S(1)} %get-tuple-element.68.kv_own_ref), channel_id=1, source_target_pairs={{0,4},{1,5},{2,6},{3,7},{4,0},{5,1},{6,2},{7,3},{8,12},{9,13},{10,... | collective-permute-start | bytes 3145736 | tf_op jit(solution)/shard_map/ppermute | solution.py:253
  212.3 29.2 %collective-permute-start.29 = (bf16[512,1024]{1,0:T(8,128)(2,1)}, bf16[512,1024]{1,0:T(8,128)(2,1)}, u32[]{:S(2)}, u32[]{:S(2)}) collective-permute-start(bf16[512,1024]{1,0:T(8,128)(2,1)} %get-tuple-element.76.kv_own_ref), channel_id=1, source_target_pairs={{0,4},{1,5},{2,6},{3,7},{4,0},{5,1},{6,2},{7,3},{8,12},{9,13},{10,... | collective-permute-start | bytes 3145736 | tf_op jit(solution)/shard_map/ppermute | solution.py:253
  216.9 50.1 %collective-permute-start.50 = (bf16[4,656,512]{2,1,0:T(8,128)(2,1)}, bf16[4,656,512]{2,1,0:T(8,128)(2,1)}, u32[]{:S(2)}, u32[]{:S(2)}) collective-permute-start(bf16[4,656,512]{2,1,0:T(8,128)(2,1)} %maximum_maximum_fusion.1), channel_id=1, source_target_pairs={{0,4},{1,5},{2,6},{3,7},{4,0},{5,1},{6,2},{7,3},{8,12},{9,13},{10,... | collective-permute-start | bytes 8060936 | tf_op jit(solution)/shard_map/ppermute | solution.py:253
  360.6 45.1 %collective-permute-start.63 = (bf16[512,1024]{1,0:T(8,128)(2,1)}, bf16[512,1024]{1,0:T(8,128)(2,1)}, u32[]{:S(2)}, u32[]{:S(2)}) collective-permute-start(bf16[512,1024]{1,0:T(8,128)(2,1)} %get-tuple-element.102), channel_id=1, source_target_pairs={{0,4},{1,5},{2,6},{3,7},{4,0},{5,1},{6,2},{7,3},{8,12},{9,13},{10,... | collective-permute-start | bytes 3145736 | tf_op jit(solution)/shard_map/ppermute | solution.py:253
  363.4 39.4 %collective-permute-start.57 = (bf16[128,1024]{1,0:T(8,128)(2,1)}, bf16[128,1024]{1,0:T(8,128)(2,1)}, u32[]{:S(2)}, u32[]{:S(2)}) collective-permute-start(bf16[128,1024]{1,0:T(8,128)(2,1)} %get-tuple-element.203), channel_id=1, source_target_pairs={{6,0},{2,1},{4,2},{0,3},{7,4},{3,5},{5,6},{1,7},{14,8},{10,9},{12,... | collective-permute-start | bytes 786440 | tf_op jit(solution)/shard_map/ppermute | solution.py:253
  365.0 37.8 %collective-permute-start.56 = (bf16[128,1024]{1,0:T(8,128)(2,1)}, bf16[128,1024]{1,0:T(8,128)(2,1)}, u32[]{:S(2)}, u32[]{:S(2)}) collective-permute-start(bf16[128,1024]{1,0:T(8,128)(2,1)} %get-tuple-element.204), channel_id=1, source_target_pairs={{2,0},{6,1},{0,2},{4,3},{3,4},{7,5},{1,6},{5,7},{10,8},{14,9},{8,1... | collective-permute-start | bytes 786440 | tf_op jit(solution)/shard_map/ppermute | solution.py:253
  402.8 40.6 %collective-permute-start.84 = (bf16[4,256,512]{1,2,0:T(8,128)(2,1)}, bf16[4,256,512]{1,2,0:T(8,128)(2,1)}, u32[]{:S(2)}, u32[]{:S(2)}) collective-permute-start(bf16[4,256,512]{1,2,0:T(8,128)(2,1)} %copy.96), channel_id=1, source_target_pairs={{0,4},{1,5},{2,6},{3,7},{4,0},{5,1},{6,2},{7,3},{8,12},{9,13},{10,... | collective-permute-start | bytes 3145736 | tf_op jit(solution)/shard_map/ppermute | solution.py:253
  403.3 123.5 %collective-permute-start.100 = (bf16[4,656,512]{2,1,0:T(8,128)(2,1)}, bf16[4,656,512]{2,1,0:T(8,128)(2,1)}, u32[]{:S(2)}, u32[]{:S(2)}) collective-permute-start(bf16[4,656,512]{2,1,0:T(8,128)(2,1)} %bitcast.111), channel_id=1, source_target_pairs={{0,4},{1,5},{2,6},{3,7},{4,0},{5,1},{6,2},{7,3},{8,12},{9,13},{10,... | collective-permute-start | bytes 8060936 | tf_op jit(solution)/shard_map/ppermute | solution.py:253
  433.0 59.1 %collective-permute-start.67 = (bf16[128,1024]{1,0:T(8,128)(2,1)}, bf16[128,1024]{1,0:T(8,128)(2,1)S(1)}, u32[]{:S(2)}, u32[]{:S(2)}) collective-permute-start(bf16[128,1024]{1,0:T(8,128)(2,1)} %get-tuple-element.183), channel_id=1, source_target_pairs={{6,0},{2,1},{4,2},{0,3},{7,4},{3,5},{5,6},{1,7},{14,8},{10,9},{12,... | collective-permute-start | bytes 786440 | tf_op jit(solution)/shard_map/ppermute | solution.py:253
  434.1 59.4 %collective-permute-start.66 = (bf16[128,1024]{1,0:T(8,128)(2,1)}, bf16[128,1024]{1,0:T(8,128)(2,1)S(1)}, u32[]{:S(2)}, u32[]{:S(2)}) collective-permute-start(bf16[128,1024]{1,0:T(8,128)(2,1)} %get-tuple-element.184), channel_id=1, source_target_pairs={{2,0},{6,1},{0,2},{4,3},{3,4},{7,5},{1,6},{5,7},{10,8},{14,9},{8,1... | collective-permute-start | bytes 786440 | tf_op jit(solution)/shard_map/ppermute | solution.py:253
  445.8 41.9 %collective-permute-start.85 = (bf16[2,256,128]{1,2,0:T(8,128)(2,1)}, bf16[2,256,128]{1,2,0:T(8,128)(2,1)S(1)}, u32[]{:S(2)}, u32[]{:S(2)}) collective-permute-start(bf16[2,256,128]{1,2,0:T(8,128)(2,1)} %get-tuple-element.175), channel_id=1, source_target_pairs={{0,16},{1,17},{2,18},{3,19},{4,20},{5,21},{6,22},{7,23},{8,24},{9,... | collective-permute-start | bytes 393224 | tf_op jit(solution)/shard_map/ppermute | solution.py:253
  446.7 43.5 %collective-permute-start.87 = (bf16[2,256,128]{1,2,0:T(8,128)(2,1)}, bf16[2,256,128]{1,2,0:T(8,128)(2,1)}, u32[]{:S(2)}, u32[]{:S(2)}) collective-permute-start(bf16[2,256,128]{1,2,0:T(8,128)(2,1)} %get-tuple-element.174), channel_id=1, source_target_pairs={{0,8},{1,9},{2,10},{3,11},{4,12},{5,13},{6,14},{7,15},{8,0},{9,1},... | collective-permute-start | bytes 393224 | tf_op jit(solution)/shard_map/ppermute | solution.py:253
  492.1 38.6 %collective-permute-start.92 = (bf16[4,656,512]{2,1,0:T(8,128)(2,1)}, bf16[4,656,512]{2,1,0:T(8,128)(2,1)S(1)}, u32[]{:S(2)}, u32[]{:S(2)}) collective-permute-start(bf16[4,656,512]{2,1,0:T(8,128)(2,1)} %bitcast.412), channel_id=1, source_target_pairs={{0,4},{1,5},{2,6},{3,7},{4,0},{5,1},{6,2},{7,3},{8,12},{9,13},{10,... | collective-permute-start | bytes 8060936 | tf_op jit(solution)/shard_map/ppermute | solution.py:253
  493.6 29.1 %collective-permute-start.76 = (bf16[4,384,512]{2,1,0:T(8,128)(2,1)}, bf16[4,384,512]{2,1,0:T(8,128)(2,1)S(1)}, u32[]{:S(2)}, u32[]{:S(2)}) collective-permute-start(bf16[4,384,512]{2,1,0:T(8,128)(2,1)} %bitcast.414), channel_id=1, source_target_pairs={{0,4},{1,5},{2,6},{3,7},{4,0},{5,1},{6,2},{7,3},{8,12},{9,13},{10,... | collective-permute-start | bytes 4718600 | tf_op jit(solution)/shard_map/ppermute | solution.py:253
  563.2 38.5 %collective-permute-start.104 = (bf16[4,656,128]{2,1,0:T(8,128)(2,1)}, bf16[4,656,128]{2,1,0:T(8,128)(2,1)}, u32[]{:S(2)}, u32[]{:S(2)}) collective-permute-start(bf16[4,656,128]{2,1,0:T(8,128)(2,1)} %pad_maximum_fusion.9), channel_id=1, source_target_pairs={{0,16},{1,17},{2,18},{3,19},{4,20},{5,21},{6,22},{7,23},{8,24},{9,... | collective-permute-start | bytes 2015240 | tf_op jit(solution)/shard_map/ppermute | solution.py:253
  568.0 34.7 %collective-permute-start.102 = (bf16[4,656,128]{2,1,0:T(8,128)(2,1)}, bf16[4,656,128]{2,1,0:T(8,128)(2,1)}, u32[]{:S(2)}, u32[]{:S(2)}) collective-permute-start(bf16[4,656,128]{2,1,0:T(8,128)(2,1)} %pad_maximum_fusion.8), channel_id=1, source_target_pairs={{0,8},{1,9},{2,10},{3,11},{4,12},{5,13},{6,14},{7,15},{8,0},{9,1},... | collective-permute-start | bytes 2015240 | tf_op jit(solution)/shard_map/ppermute | solution.py:253
  (245 other events, 3173.2 us)

commit v2 on v1

v2 whole, which is shorter than its diff:
```python
import jax
import jax.numpy as jnp
from jax import lax
from jax.experimental import pallas as pl
from jax.experimental.pallas import tpu as pltpu
from jax.sharding import PartitionSpec as P

D = 1024
H = 16
DH = 64
FF = 2624
SEQ = 1024
STEP = 10

epsilon_norm = 1e-05
rope_theta = 160000.0
beta_first = 0.9
beta_second = 0.98
epsilon_adam = 1e-06
weight_decay = 1e-05

AXES = ("dp", "tensor")
bf16 = jnp.bfloat16
f32 = jnp.float32


def dot_nt(left, right):
    return lax.dot_general(left, right, (((1,), (1,)), ((), ())), preferred_element_type=f32)


def dot_tn(left, right):
    return lax.dot_general(left, right, (((0,), (0,)), ((), ())), preferred_element_type=f32)


def dot_nn(left, right):
    return jnp.dot(left, right, preferred_element_type=f32)


def adamw_update(weight, first_moment, second_moment, gradient, step_rate):
    first_new = beta_first * first_moment + (1.0 - beta_first) * gradient
    second_new = beta_second * second_moment + (1.0 - beta_second) * gradient * gradient
    first_hat = first_new / (1.0 - beta_first**STEP)
    second_hat = second_new / (1.0 - beta_second**STEP)
    weight_new = weight - step_rate * (
        first_hat / (jnp.sqrt(second_hat) + epsilon_adam) + weight_decay * weight
    )
    return (weight_new, first_new, second_new)


def whole(array):
    return pl.BlockSpec(array.shape, lambda i, rank=array.ndim: (0,) * rank)


def by_block(array):
    return pl.BlockSpec((1,) + array.shape[1:], lambda z: (z, 0, 0))


def by_rows(array, steps):
    return pl.BlockSpec((array.shape[0] // steps, array.shape[1]), lambda i: (i, 0))


def like(shape, dtype=bf16):
    return jax.ShapeDtypeStruct(shape, dtype)


microseconds = {
    "feature_order": 3.0,
    "first_norm": 4.0,
    "qkv_projection": 6.0,
    "attention_forward": 9.0,
    "attention_output": 2.5,
    "second_norm": 4.0,
    "expand": 12.0,
    "contract": 5.0,
    "layer_output": 2.0,
    "weight_gradient": 5.0,
    "grad_lifted": 6.0,
    "grad_normed_two": 8.0,
    "second_norm_gradient": 5.0,
    "grad_attended": 2.5,
    "attention_backward": 14.0,
    "grad_normed_one": 6.0,
    "first_norm_gradient": 3.0,
}


def cost(name):
    return pl.CostEstimate(
        flops=int(microseconds[name] * 0.35e9),
        bytes_accessed=int(microseconds[name] * 1.2e6),
        transcendentals=0,
    )


def call(kernel, name, grid, in_specs, out_specs, out_shape, scratch=()):
    return pl.pallas_call(
        kernel,
        grid=grid,
        in_specs=in_specs,
        out_specs=out_specs,
        out_shape=out_shape,
        scratch_shapes=list(scratch),
        compiler_params=pltpu.CompilerParams(vmem_limit_bytes=28 << 20),
        cost_estimate=cost(name),
        name=name,
    )


def swap_halves(values):
    lane = lax.broadcasted_iota(jnp.int32, values.shape, 1)
    return jnp.where(
        lane % DH < DH // 2,
        pltpu.roll(values, values.shape[1] - DH // 2, 1),
        pltpu.roll(values, DH // 2, 1),
    )


def normalize(values):
    centered = values - jnp.mean(values, axis=1, keepdims=True)
    scale = lax.rsqrt(jnp.mean(centered * centered, axis=1, keepdims=True) + epsilon_norm)
    return centered * scale, scale


def unnormalize(grads, values, gain):
    hats, scale = normalize(values)
    gain_grad = jnp.sum(grads * hats, axis=0, keepdims=True)
    errors = grads * gain
    average = jnp.mean(errors, axis=1, keepdims=True)
    along = jnp.mean(errors * hats, axis=1, keepdims=True)
    return scale * (errors - average - hats * along), gain_grad


def pick(ref, index_ref):
    count = index_ref.shape[0]
    if count == 1:
        return ref[...]
    block = ref.shape[1] // count
    parts = [ref[:, pl.ds(pl.multiple_of(index_ref[j] * block, block), block)] for j in range(count)]
    return jnp.concatenate(parts, axis=1)


scalars = pl.BlockSpec(memory_space=pltpu.SMEM)


def order_call(values, index):
    def kernel(index_ref, in_ref, out_ref):
        out_ref[...] = pick(in_ref, index_ref)

    tile = by_rows(values, 2)
    return call(
        kernel, "feature_order", (2,), [scalars, tile], tile, like(values.shape, values.dtype)
    )(index, values)


def norm_call(x, gains, index):
    def kernel(index_ref, x_ref, gain_ref, x_out_ref, out_ref):
        values = pick(x_ref, index_ref)
        x_out_ref[...] = values
        hats, _ = normalize(values.astype(f32))
        out_ref[...] = (hats * gain_ref[0:1, :]).astype(bf16)

    tile = by_rows(x, 4)
    return call(
        kernel, "first_norm", (4,), [scalars, tile, whole(gains)], [tile] * 2, [like(x.shape)] * 2
    )(index, x, gains)


def qkv_call(x, w_query, query_start, w_key_value, cosine, sine):
    rows, blocks = x.shape[0], w_query.shape[0]

    def kernel(x_ref, wq_ref, wkv_ref, cos_ref, sin_ref, q_ref, k_ref, v_ref):
        w = jnp.concatenate([wq_ref[0, query_start:], wkv_ref[0, :256]], axis=0)
        mixed = dot_nt(x_ref[...], w)
        cosine, sine = cos_ref[...], sin_ref[...]
        query, key = mixed[:, :128], mixed[:, 128:256]
        query = query * cosine + swap_halves(query) * sine
        key = key * cosine + swap_halves(key) * sine
        q_ref[0] = query.astype(bf16) * bf16(DH**-0.5)
        k_ref[0] = key.astype(bf16)
        v_ref[0] = mixed[:, 256:].astype(bf16)

    out = like((blocks, rows, 128))
    return call(
        kernel,
        "qkv_projection",
        (blocks,),
        [whole(x), by_block(w_query), by_block(w_key_value), whole(cosine), whole(sine)],
        [by_block(out)] * 3,
        [out] * 3,
    )(x, w_query, w_key_value, cosine, sine)


def pair_specs(array, first, halves):
    rows = array.shape[1]
    return (
        pl.BlockSpec((1, rows // halves, array.shape[2]), lambda z, i: (first + z, i, 0)),
        pl.BlockSpec((1, rows, array.shape[2]), lambda z, i: (first + z, 0, 0)),
    )


def attend_call(query, key, value, first, count):
    rows = query.shape[1]

    def kernel(q_ref, k_ref, v_ref, out_ref, lse_ref):
        query, key = q_ref[0], k_ref[0]
        value_t = v_ref[0].astype(f32).T.astype(bf16)
        lane = lax.broadcasted_iota(jnp.int32, query.shape, 1)
        outs = []
        for head in range(2):
            query_head = jnp.where(lane // DH == head, query, jnp.zeros_like(query))
            scores = dot_nt(key, query_head)
            peak = jnp.max(scores, axis=0, keepdims=True)
            weights = jnp.exp(scores - peak)
            total = jnp.sum(weights, axis=0, keepdims=True)
            out = dot_nn(value_t[head * DH : (head + 1) * DH], weights.astype(bf16))
            outs.append(out / total)
            lse_ref[0, head : head + 1, :] = peak + jnp.log(total)
        out_ref[0] = jnp.concatenate(outs, axis=0).T.astype(bf16)

    half, full = pair_specs(query, first, 2)
    out_half, _ = pair_specs(query, 0, 2)
    lse = pl.BlockSpec((1, 2, rows // 2), lambda z, i: (z, 0, i))
    return call(
        kernel,
        "attention_forward",
        (count, 2),
        [half, full, full],
        [out_half, lse],
        [like((count, rows, 128)), like((count, 2, rows), f32)],
    )(query, key, value)


def attend_back_call(query, key, value, grad, out, lse, cosine, sine, first, count):
    rows = query.shape[1]

    def kernel(
        q_ref, k_ref, v_ref, grad_ref, out_ref, lse_ref, cos_ref, sin_ref, dq_ref, dkv_ref,
        key_total, value_total,
    ):
        step = pl.program_id(1)
        query, key, value, grad = q_ref[0], k_ref[0], v_ref[0], grad_ref[0]
        key_t = key.astype(f32).T.astype(bf16)
        product_t = (grad.astype(f32) * out_ref[0].astype(f32)).T
        lane = lax.broadcasted_iota(jnp.int32, query.shape, 1)
        grad_key = jnp.zeros((rows, 128), f32)
        grad_value = jnp.zeros((rows, 128), f32)
        grad_queries = []
        for head in range(2):
            mine = lane // DH == head
            query_head = jnp.where(mine, query, jnp.zeros_like(query))
            grad_head = jnp.where(mine, grad, jnp.zeros_like(grad))
            delta = jnp.sum(product_t[head * DH : (head + 1) * DH], axis=0, keepdims=True)
            weights = jnp.exp(dot_nt(key, query_head) - lse_ref[0, head : head + 1, :])
            grad_soft = dot_nt(value, grad_head)
            grad_scores = (weights * (grad_soft - delta)).astype(bf16)
            grad_value += dot_nn(weights.astype(bf16), grad_head)
            grad_key += dot_nn(grad_scores, query_head)
            grad_queries.append(dot_nn(key_t[head * DH : (head + 1) * DH], grad_scores))
        half = query.shape[0]
        grad_query = jnp.concatenate(grad_queries, axis=0).T * (DH**-0.5)
        start = pl.multiple_of(step * half, half)
        cosine, sine = cos_ref[pl.ds(start, half), :], sin_ref[pl.ds(start, half), :]
        dq_ref[0] = (grad_query * cosine - swap_halves(grad_query) * sine).astype(bf16)

        @pl.when(step == 0)
        def _():
            key_total[...] = grad_key
            value_total[...] = grad_value

        @pl.when(step == 1)
        def _():
            total = key_total[...] + grad_key
            back = total * cos_ref[...] - swap_halves(total) * sin_ref[...]
            dkv_ref[0, :, :128] = back.astype(bf16)
            dkv_ref[0, :, 128:] = (value_total[...] + grad_value).astype(bf16)

    half, full = pair_specs(query, first, 2)
    out_half, _ = pair_specs(query, 0, 2)
    lse_spec = pl.BlockSpec((1, 2, rows // 2), lambda z, i: (z, 0, i))
    table = pl.BlockSpec(cosine.shape, lambda z, i: (0, 0))
    return call(
        kernel,
        "attention_backward",
        (count, 2),
        [half, full, full, half, out_half, lse_spec, table, table],
        [out_half, pl.BlockSpec((1, rows, 256), lambda z, i: (z, 0, 0))],
        [like((count, rows, 128)), like((count, rows, 256))],
        [pltpu.VMEM((rows, 128), f32)] * 2,
    )(query, key, value, grad, out, lse, cosine, sine)


def lanes_of(refs):
    return jnp.concatenate([r[j] for r in refs for j in range(r.shape[0])], axis=1)


def blocks_by_rows(array, steps):
    return pl.BlockSpec(
        (array.shape[0], array.shape[1] // steps, array.shape[2]), lambda i: (0, i, 0)
    )


def rows_of(ref, start, stop):
    if start == 0 and stop == ref.shape[1]:
        return ref[...].reshape(-1, ref.shape[2])
    return jnp.concatenate([ref[z, start:stop] for z in range(ref.shape[0])], axis=0)


def attention_output_call(att, w, start):
    rows = att[0].shape[1]

    def kernel(*refs):
        *att_refs, w_ref, out_ref = refs
        out_ref[...] = dot_nn(lanes_of(att_refs), rows_of(w_ref, start, w_ref.shape[1])).astype(bf16)

    out = like((rows, w.shape[2]))
    return call(
        kernel,
        "attention_output",
        (2,),
        [blocks_by_rows(a, 2) for a in att] + [whole(w)],
        by_rows(out, 2),
        out,
    )(*att, w)


def swapped_rows(array):
    return pl.BlockSpec((array.shape[0] // 4, array.shape[1]), lambda i: ((i + 2) % 4, 0))


def middle_call(x, part, got, gains):
    def kernel(x_ref, part_ref, got_ref, gain_ref, mid_ref, out_ref):
        middle = x_ref[...].astype(f32) + (part_ref[...].astype(f32) + got_ref[...].astype(f32))
        mid_ref[...] = middle
        hats, _ = normalize(middle)
        out_ref[...] = (hats * gain_ref[1:2, :]).astype(bf16)

    tile = by_rows(x, 4)
    return call(
        kernel,
        "second_norm",
        (4,),
        [tile, tile, swapped_rows(got), whole(gains)],
        [tile, tile],
        [like(x.shape, f32), like(x.shape)],
    )(x, part, got, gains)


def lift_call(x, up, gate):
    hidden = up.shape[0] * up.shape[1]

    def kernel(x_ref, up_ref, gate_ref, hid_ref, to_in_ref, to_gate_ref):
        x = x_ref[...]
        w_up, w_gate = (r[...].reshape(hidden, -1) for r in (up_ref, gate_ref))
        for start in range(0, hidden, 512):
            part = slice(start, min(start + 512, hidden))
            lifted = dot_nt(x, w_up[part])
            gate = dot_nt(x, w_gate[part])
            phi = 0.5 * (1.0 + lax.erf(lifted * (0.5**0.5)))
            gelu = lifted * phi
            slope = phi + lifted * jnp.exp(-0.5 * lifted * lifted) * 0.3989422804014327
            hid_ref[:, part] = (gelu * gate).astype(bf16)
            to_in_ref[:, part] = (gate * slope).astype(bf16)
            to_gate_ref[:, part] = gelu.astype(bf16)

    out = like((x.shape[0], hidden))
    return call(
        kernel,
        "expand",
        (2,),
        [by_rows(x, 2), whole(up), whole(gate)],
        [by_rows(out, 2)] * 3,
        [out] * 3,
    )(x, up, gate)


def lower_call(hidden, w, middle):
    rows, width = middle.shape

    def kernel(hid_ref, w_ref, mid_ref, own_ref, oth_ref):
        total = dot_nn(hid_ref[...], w_ref[...].reshape(-1, width))

        @pl.when(pl.program_id(0) == 1)
        def _():
            own_ref[...] = mid_ref[...] + total

        @pl.when(pl.program_id(0) == 0)
        def _():
            oth_ref[...] = total.astype(bf16)

    first = pl.BlockSpec((rows // 2, width), lambda i: (0, 0))
    return call(
        kernel,
        "contract",
        (2,),
        [pl.BlockSpec((rows // 2, hidden.shape[1]), lambda i: (1 - i, 0)), whole(w), first],
        [first, first],
        [like((rows // 2, width), f32), like((rows // 2, width))],
    )(hidden, w, middle)


def output_call(own, got, index):
    def kernel(index_ref, own_ref, got_ref, out_ref):
        out_ref[...] = (pick(own_ref, index_ref) + pick(got_ref, index_ref).astype(f32)).astype(bf16)

    tile = by_rows(own, 2)
    return call(kernel, "layer_output", (2,), [scalars, tile, tile], tile, like(own.shape))(
        index, own, got
    )


def weight_gradient_call(lefts, right, blocks, split, extra=None):
    flat = lefts[0].ndim == 2
    columns = lefts[0].shape[1] // blocks if flat else lefts[0].shape[2]
    more = [] if extra is None else [extra]
    lead = sum(e.shape[0] for e in more)
    height = lead + columns
    width = right.shape[1]
    half = blocks // 2

    def kernel(*refs):
        left_refs = refs[: len(lefts)]
        right_ref = refs[len(lefts)]
        extra_refs = refs[len(lefts) + 1 : len(lefts) + 1 + len(more)]
        outs = refs[len(lefts) + 1 + len(more) :]
        left = left_refs[0][...] if flat else lanes_of(left_refs)

        def put(ref, place, values, part):
            ref[place, lead:] = values
            for e in extra_refs:
                ref[place, :lead] = e[:, part]

        for start in range(0, width, 512):
            grads = dot_tn(left, right_ref[:, start : start + 512]).astype(bf16)
            for z in range(blocks):
                block = grads[z * columns : (z + 1) * columns]
                if not split:
                    put(outs[0], (z, slice(start, start + 512)), block, None)
                    continue
                mine, x_rest, y_rest, to_x, to_y = outs
                for j in range(start // 256, start // 256 + 2):
                    part = slice(256 * j, 256 * j + 256)
                    values = block[:, 256 * j - start : 256 * j - start + 256]
                    if j == 0:
                        put(mine, z, values, part)
                    elif j == 1:
                        put(*((to_x, half + z) if z < half else (x_rest, z - half)), values, part)
                    elif j == 2:
                        put(*((y_rest, z) if z < half else (to_y, z)), values, part)
                    else:
                        put(*((to_x, z) if z < half else (to_y, z - half)), values, part)

    if split:
        out_shape = [like((n, height, width // 4)) for n in (blocks, half, half, blocks, blocks)]
    else:
        out_shape = [like((blocks, height, width))]

        def kernel(*refs):
            left_refs = refs[: len(lefts)]
            right_ref, out_ref = refs[len(lefts)], refs[-1]
            left = left_refs[0][...] if flat else lanes_of(left_refs)
            grads = dot_tn(left, right_ref[...]).astype(bf16)
            for z in range(blocks):
                out_ref[z, lead:] = grads[z * columns : (z + 1) * columns]
                if more:
                    out_ref[z, :lead] = refs[len(lefts) + 1][...]

    return call(
        kernel,
        "weight_gradient",
        (1,),
        [whole(a) for a in (*lefts, right, *more)],
        [whole(o) for o in out_shape],
        out_shape,
    )(*lefts, right, *more)


def hidden_back_call(dy, w, to_in, to_gate):
    hidden = to_in.shape[1]

    def kernel(dy_ref, w_ref, to_in_ref, to_gate_ref, in_ref, gate_ref):
        w = w_ref[...].reshape(hidden, -1)
        for start in range(0, hidden, 512):
            part = slice(start, min(start + 512, hidden))
            grad = dot_nt(dy_ref[...], w[part])
            in_ref[:, part] = (grad * to_in_ref[:, part].astype(f32)).astype(bf16)
            gate_ref[:, part] = (grad * to_gate_ref[:, part].astype(f32)).astype(bf16)

    tile = by_rows(to_in, 2)
    return call(
        kernel,
        "grad_lifted",
        (2,),
        [by_rows(dy, 2), whole(w), tile, tile],
        [tile, tile],
        [like(to_in.shape)] * 2,
    )(dy, w, to_in, to_gate)


def two_part_call(grad_in, grad_gate, up, gate):
    width = up.shape[2]

    def kernel(in_ref, gate_ref, up_ref, w_gate_ref, out_ref):
        total = dot_nn(in_ref[...], up_ref[...].reshape(-1, width))
        total += dot_nn(gate_ref[...], w_gate_ref[...].reshape(-1, width))
        out_ref[...] = total.astype(bf16)

    out = like((grad_in.shape[0], width))
    return call(
        kernel,
        "grad_normed_two",
        (2,),
        [by_rows(grad_in, 2), by_rows(grad_gate, 2), whole(up), whole(gate)],
        by_rows(out, 2),
        out,
    )(grad_in, grad_gate, up, gate)


def two_back_call(part, got, middle, dy, gains):
    rows, width = middle.shape

    def kernel(part_ref, got_ref, mid_ref, dy_ref, gain_ref, grad_ref, low_ref, gain_grad_ref):
        i = pl.program_id(0)
        grads = part_ref[...].astype(f32) + got_ref[...].astype(f32)
        back, gain_grad = unnormalize(grads, mid_ref[...], gain_ref[1:2, :])
        grad = dy_ref[...].astype(f32) + back
        low_ref[...] = grad.astype(bf16)

        @pl.when(i == 0)
        def _():
            gain_grad_ref[...] = jnp.zeros_like(gain_grad_ref)

        @pl.when(i < 2)
        def _():
            grad_ref[...] = grad
            gain_grad_ref[...] += jnp.broadcast_to(gain_grad, gain_grad_ref.shape)

    tile = by_rows(middle, 4)
    row = like((8, width), f32)
    return call(
        kernel,
        "second_norm_gradient",
        (4,),
        [tile, swapped_rows(got), tile, tile, whole(gains)],
        [
            pl.BlockSpec((rows // 4, width), lambda i: (jnp.minimum(i, 1), 0)),
            tile,
            whole(row),
        ],
        [like((rows // 2, width), f32), like(middle.shape), row],
    )(part, got, middle, dy, gains)


def att_grad_call(grad, w, start):
    blocks = w.shape[0]
    columns = w.shape[1] - start

    def kernel(g_ref, w_ref, out_ref):
        out = dot_nt(g_ref[...], rows_of(w_ref, start, w_ref.shape[1])).astype(bf16)
        for z in range(blocks):
            out_ref[z] = out[:, z * columns : (z + 1) * columns]

    out = like((blocks, grad.shape[0], columns))
    return call(
        kernel,
        "grad_attended",
        (2,),
        [by_rows(grad, 2), whole(w)],
        blocks_by_rows(out, 2),
        out,
    )(grad, w)


def one_part_call(queries, keys_values, w_query, query_start, w_key_value):
    rows, width = queries[0].shape[1], w_query.shape[2]
    count = len(queries)

    def kernel(*refs):
        left_refs = refs[: 2 * count]
        wq_ref, wkv_ref, own_ref, oth_ref = refs[2 * count :]
        left = lanes_of(left_refs)
        w = jnp.concatenate(
            [rows_of(wq_ref, query_start, wq_ref.shape[1]), rows_of(wkv_ref, 0, 256)], axis=0
        )
        total = dot_nn(left, w)

        @pl.when(pl.program_id(0) == 1)
        def _():
            own_ref[...] = total

        @pl.when(pl.program_id(0) == 0)
        def _():
            oth_ref[...] = total.astype(bf16)

    def half(array):
        shape = (array.shape[0], rows // 2, array.shape[2])
        return pl.BlockSpec(shape, lambda i: (0, 1 - i, 0))

    first = pl.BlockSpec((rows // 2, width), lambda i: (0, 0))
    return call(
        kernel,
        "grad_normed_one",
        (2,),
        [half(a) for a in (*queries, *keys_values)] + [whole(w_query), whole(w_key_value)],
        [first, first],
        [like((rows // 2, width), f32), like((rows // 2, width))],
    )(*queries, *keys_values, w_query, w_key_value)


def one_back_call(own, got, x, grad_middle, gains, gain_two, index):
    rows, width = own.shape

    def kernel(
        index_ref, own_ref, got_ref, x_ref, mid_ref, gain_ref, gain_two_ref, grad_ref, gain_grad_ref,
        total_ref, low_ref,
    ):
        i = pl.program_id(0)
        grads = own_ref[...] + got_ref[...].astype(f32)
        back, gain_grad = unnormalize(grads, x_ref[...].astype(f32), gain_ref[0:1, :])
        low_ref[...] = (mid_ref[...] + back).astype(bf16)
        grad_ref[...] = pick(low_ref, index_ref)

        @pl.when(i == 0)
        def _():
            total_ref[...] = gain_grad

        @pl.when(i == 1)
        def _():
            total = total_ref[...] + gain_grad
            row = lax.broadcasted_iota(jnp.int32, gain_grad_ref.shape, 0)
            both = jnp.where(row == 0, total, jnp.where(row == 1, gain_two_ref[0:1, :], 0.0))
            gain_grad_ref[...] = both.astype(bf16)

    tile = by_rows(own, 2)
    x_tile = pl.BlockSpec((rows // 2, width), lambda i: (i, 0))
    gain_grads = like((16, width))
    return call(
        kernel,
        "first_norm_gradient",
        (2,),
        [scalars, tile, tile, x_tile, tile, whole(gains), whole(gain_two)],
        [tile, whole(gain_grads)],
        [like(own.shape), gain_grads],
        [pltpu.VMEM((1, width), f32), pltpu.VMEM((rows // 2, width), bf16)],
    )(index, own, got, x, grad_middle, gains, gain_two)


def make_per_device(dp, tensor):
    count = dp * tensor
    chips = dp // 2
    chip_bits = chips.bit_length() - 1
    square = chip_bits == 2
    half = tensor // 2

    def permute(value, pairs):
        return lax.ppermute(value, AXES, pairs)

    def exchange(value, mask):
        return permute(value, [(i, i ^ mask) for i in range(count)])

    def over_chip(value, bit):
        return exchange(value, (2 * tensor) << bit)

    def over_core(value):
        pieces = max(1, value.size // (1 << 18))
        if value.ndim != 2 or value.shape[0] % (16 * pieces):
            pieces = 1
        rows = value.shape[0] // pieces
        got = [exchange(value[i * rows : (i + 1) * rows], tensor) for i in range(pieces)]
        return got[0] if pieces == 1 else jnp.concatenate(got, axis=0)

    def spread_pairs(r):
        pairs = []
        for i in range(count):
            z = i % tensor
            core = (i // tensor) % 2
            chip = i // (2 * tensor)
            pairs.append((i, (chip * 2 + z % 2) * tensor + (r ^ (z // 2)) * 2 + core))
        return pairs

    def by_column(blocks, me_z):
        for bit in range(tensor.bit_length() - 1):
            odd = (me_z >> bit) % 2 == 1
            blocks = [jnp.where(odd, blocks[k ^ (1 << bit)], blocks[k]) for k in range(tensor)]
        return blocks

    def gather_column(rows, me_z):
        return by_column([rows] + [exchange(rows, k) for k in range(1, tensor)], me_z)

    def gather_plane(columns):
        current = columns[None]
        for bit in range(chip_bits):
            current = jnp.concatenate([current, over_chip(current, bit)], axis=0)
        return current.transpose(1, 2, 0, 3).reshape(columns.shape[:2] + (-1,))

    def low_sum(*values):
        return sum(v.astype(f32) for v in values).astype(bf16)

    def reduce_plane(parts):
        current = parts
        for bit in reversed(range(chip_bits)):
            middle = current.shape[0] // 2
            current = low_sum(current[:middle], over_chip(current[middle:], bit))
        return current[0]

    def reduce_column(blocks):
        result = blocks[0].astype(f32)
        for k in range(1, tensor):
            result = result + exchange(blocks[k], k).astype(f32)
        return result

    def per_device(
        inputs,
        cotangent,
        attention_in,
        attention_out,
        expand_weight,
        contract_weight,
        norm_gains,
        attention_in_first,
        attention_in_second,
        attention_out_first,
        attention_out_second,
        expand_first,
        expand_second,
        contract_first,
        contract_second,
        gains_first,
        gains_second,
    ):
        block = attention_in.shape[0]
        head_columns = attention_in.shape[2]
        hidden_local = expand_weight.shape[2]
        local_rows = inputs.shape[2]
        me_dp = lax.axis_index("dp")
        me_z = lax.axis_index("tensor")
        core = me_dp % 2
        z_high = me_z // 2

        me_chip = me_dp // 2
        index = me_chip ^ jnp.arange(chips, dtype=jnp.int32)
        aligned = block % 128 == 0
        kernel_index = index if aligned else jnp.zeros((1,), jnp.int32)

        def outside(values):
            if aligned:
                return values
            shaped = values.reshape(values.shape[0], chips, 2 * block)
            return jnp.take(shaped, index, axis=1).reshape(values.shape)

        def spread(values, r):
            part = lax.dynamic_index_in_dim(values[:, 0], r ^ z_high, 0, keepdims=False)
            return permute(part, spread_pairs(r))

        def collect(values, r):
            part = values[r * local_rows : (r + 1) * local_rows]
            return permute(part, [(b, a) for a, b in spread_pairs(r)])

        def assemble(first, second):
            odd = z_high == 1
            return jnp.stack([jnp.where(odd, second, first), jnp.where(odd, first, second)])[:, None]

        row_starts = [
            ((r ^ z_high) * 2 + (core ^ c)) * local_rows for c in range(2) for r in range(2)
        ]
        positions = jnp.concatenate([s + jnp.arange(local_rows) for s in row_starts]).astype(f32)
        exponents = jnp.arange(0, DH, 2).astype(f32) / DH
        angles = positions[:, None] * jnp.power(rope_theta, -exponents)[None, :]
        cosine, sine = jnp.cos(angles), jnp.sin(angles)
        cosine = jnp.concatenate([cosine] * 4, axis=-1)
        sine = jnp.concatenate([-sine, sine] * 2, axis=-1)

        cut = (hidden_local // 2 + 15) // 16 * 16
        spare = 2 * cut - hidden_local
        head_cut = head_columns // 2
        low_in = attention_in.astype(bf16).reshape(block, 3, 2, head_cut).transpose(2, 1, 3, 0)
        low_out = attention_out.astype(bf16).reshape(block, 2, head_cut).transpose(1, 2, 0)
        low_expand = jnp.pad(expand_weight.astype(bf16).transpose(1, 2, 0), ((0, 0), (0, spare), (0, 0)))
        low_expand = low_expand.reshape(2, 2, cut, block).transpose(1, 0, 2, 3)
        low_contract = jnp.pad(contract_weight.astype(bf16).T, ((0, spare), (0, 0)))
        low_contract = low_contract.reshape(2, cut, block)
        low_gains = jnp.pad(norm_gains.astype(bf16), ((0, 14), (0, 0)))
        lead = low_gains.shape[0]
        both = jnp.concatenate(
            [
                jnp.stack([low_gains, low_gains]),
                low_in.reshape(2, -1, block),
                low_out,
                low_expand.reshape(2, -1, block),
                low_contract,
            ],
            axis=1,
        )
        sizes = [lead + head_cut, 3 * head_cut, cut, cut, cut]
        starts = [sum(sizes[:k]) for k in range(len(sizes) + 1)]
        last = len(sizes)
        first_core = core == 0

        def side_by_side(mine, got):
            return jnp.concatenate(
                [jnp.where(first_core, mine, got), jnp.where(first_core, got, mine)], axis=-1
            )

        state = {"tables": (cosine, sine), "x_in": inputs, "cot": cotangent, "both": both}
        held = []
        again = []

        def run(work):
            nonlocal state
            new = {}
            late = held[:]
            held[:] = again
            again.clear()
            work(state, new)
            for values in late:
                new.update(values)
            state.update(new)
            names = list(state)
            state = dict(zip(names, lax.optimization_barrier([state[n] for n in names])))

        def columns(s, new, first, count):
            low = s["low"][starts[first] : starts[first + count]]
            blocks = gather_column(low, me_z)
            for k in range(first, first + count):
                a, b = starts[k] - starts[first], starts[k + 1] - starts[first]
                new["column", k] = jnp.stack([block[a:b] for block in blocks])

        def plane(s, new, k):
            if not square:
                if k < last:
                    new["w", k] = gather_plane(s.pop(("column", k)))
                return
            sends, first_rows = ([], []), 0
            if k < last:
                column = s["column", k]
                first_rows = column.shape[0] * column.shape[1]
                for way in range(2):
                    sends[way].append(column.reshape(first_rows, -1))
            if k > 0:
                got = s["near", k - 1]
                rows = half * sizes[k - 1]
                sends[0].append(got[1][rows : 2 * rows])
                sends[1].append(got[0][:rows])
            got = tuple(over_chip(jnp.concatenate(sends[way], axis=0), way) for way in range(2))
            if k < last:
                new["near", k] = got
            if k > 0:
                shape = (tensor, sizes[k - 1], -1)
                rows = tensor * sizes[k - 1]
                x_got, y_got = s.pop(("near", k - 1))
                diagonal = jnp.concatenate([got[1][first_rows:], got[0][first_rows:]], axis=0)
                new["w", k - 1] = jnp.concatenate(
                    [
                        s.pop(("column", k - 1)),
                        x_got[:rows].reshape(shape),
                        y_got[:rows].reshape(shape),
                        diagonal.reshape(shape),
                    ],
                    axis=-1,
                )

        def f0(s, new):
            pair = s.pop("both")
            mine = jnp.where(first_core, pair[0], pair[1])
            got = over_core(jnp.where(first_core, pair[1], pair[0]))
            new["low"] = side_by_side(mine, got)

        run(f0)

        def f1(s, new):
            columns(s, new, 0, 1)
            late = lax.all_gather(s["low"][starts[3] :], "tensor", axis=0)
            again.append({("column", 3): late[:, : sizes[3]], ("column", 4): late[:, sizes[3] :]})

        run(f1)

        def f2(s, new):
            plane(s, new, 0)
            columns(s, new, 1, 1)

        run(f2)

        def f3(s, new):
            plane(s, new, 1)
            columns(s, new, 2, 1)
            new["x0"] = spread(s["x_in"], 0)

        run(f3)

        def f4(s, new):
            plane(s, new, 2)
            rows = jnp.concatenate([s.pop("x0"), spread(s.pop("x_in"), 1)], axis=0)
            new["x_own"] = rows

        run(f4)

        def f5(s, new):
            plane(s, new, 3)
            rows = s.pop("x_own")
            x_raw = jnp.concatenate([rows, over_core(rows)], axis=0)
            new["gains"] = s["w", 0][0, :lead].astype(f32)
            new["x"], new["normed"] = norm_call(outside(x_raw), new["gains"], kernel_index)
            query, key, value = qkv_call(new["normed"], s["w", 0], lead, s["w", 1], *s["tables"])
            new["qkv"] = (query, key, value)
            new["att", 0], new["lse", 0] = attend_call(query, key, value, 0, tensor // 2)
            new["y0"] = spread(s["cot"], 0)

        run(f5)

        def f6(s, new):
            plane(s, new, 4)
            new["att", 1], new["lse", 1] = attend_call(*s["qkv"], tensor // 2, tensor // 2)
            new["part"] = attention_output_call((s["att", 0], new["att", 1]), s["w", 1], 2 * head_cut)
            new["y_own"] = jnp.concatenate([s.pop("y0"), spread(s.pop("cot"), 1)], axis=0)

        run(f6)

        def f7(s, new):
            plane(s, new, 5)
            part, rows = s.pop("part"), s.pop("y_own")
            new["middle"], new["normed_two"] = middle_call(
                s["x"], part, over_core(part), s["gains"]
            )
            new["hidden"], new["to_in"], new["to_gate"] = lift_call(
                new["normed_two"], s["w", 2], s["w", 3]
            )
            y_raw = jnp.concatenate([rows, over_core(rows)], axis=0)
            new["dy"] = order_call(outside(y_raw), kernel_index)
            made(new, 0, [new["hidden"]], new["dy"])

        def made(new, k, lefts, right, extra=None):
            grads = weight_gradient_call(lefts, right, tensor, square and aligned, extra)
            if not square or not aligned:
                (full,) = grads
                grads = full.reshape(full.shape[:2] + (chips, -1)).transpose(2, 0, 1, 3)
            new["g", k] = grads

        def near(s, new, k):
            if not square:
                new["f", k] = [b for b in reduce_plane(s.pop(("g", k)))]
                return
            mine, x_rest, y_rest, to_x, to_y = s.pop(("g", k))
            x_got, y_got = over_chip(to_x, 0), over_chip(to_y, 1)
            new["n", k] = (
                low_sum(x_rest, y_got[:half]),
                low_sum(y_rest, x_got[:half]),
                mine,
                x_got,
                y_got,
            )

        def far(s, new, k):
            if not square:
                return
            x_second, y_second, mine, x_near, y_near = s.pop(("n", k))
            x_got, y_got = over_chip(x_second, 0), over_chip(y_second, 1)
            new["f", k] = [
                low_sum(mine[j], x_near[half + j], y_got[j]) for j in range(half)
            ] + [low_sum(mine[half + j], y_near[half + j], x_got[j]) for j in range(half)]

        def scatter(s, k):
            total = lax.psum_scatter(
                jnp.stack(s.pop(("f", k))), "tensor", scatter_dimension=0, tiled=False
            )
            held.append({("sum", k): total})

        def column(s, new, *chunks):
            blocks = [by_column(s.pop(("f", k)), me_z) for k in chunks]
            total = reduce_column([jnp.concatenate(b, axis=0) for b in zip(*blocks)])
            start = 0
            for k, b in zip(chunks, blocks):
                new["sum", k] = total[start : start + b[0].shape[0]].astype(bf16)
                start += b[0].shape[0]

        def trade(s, new, *chunks):
            sums = [s.pop(("sum", k)) for k in chunks]
            total = jnp.concatenate(sums, axis=0)
            mine = jnp.where(first_core, total[:, :block], total[:, block:])
            got = over_core(jnp.where(first_core, total[:, block:], total[:, :block]))
            start = 0
            for k, rows in zip(chunks, [a.shape[0] for a in sums]):
                a, b = mine[start : start + rows], got[start : start + rows]
                new["grad", k] = (
                    jnp.where(first_core, a, b).astype(f32),
                    jnp.where(first_core, b, a).astype(f32),
                )
                start += rows

        run(f7)

        def s1(s, new):
            near(s, new, 0)
            g_in, g_gate = hidden_back_call(s["dy"], s["w", 4], s.pop("to_in"), s.pop("to_gate"))
            new["g_gate"] = g_gate
            new["part"] = two_part_call(g_in, g_gate, s.pop(("w", 2)), s.pop(("w", 3)))
            made(new, 1, [g_in], s["normed_two"])
            new["low_own"], new["low_other"] = lower_call(
                s.pop("hidden"), s.pop(("w", 4)), s["middle"]
            )

        run(s1)

        def attention_back(s, new, p):
            new["dq", p], new["dkv", p] = attend_back_call(
                *s["qkv"], s["g_att"], s["att", p], s.pop(("lse", p)), *s["tables"],
                p * (tensor // 2), tensor // 2,
            )

        def s2(s, new):
            far(s, new, 0)
            near(s, new, 1)
            part = s.pop("part")
            new["grad_mid"], new["mid_low"], new["gain_two"] = two_back_call(
                part, over_core(part), s.pop("middle"), s.pop("dy"), s["gains"]
            )
            made(new, 2, [s.pop("g_gate")], s.pop("normed_two"))
            s["g_att"] = new["g_att"] = att_grad_call(new["mid_low"], s["w", 1], 2 * head_cut)
            attention_back(s, new, 0)
            new["out"] = outside(
                output_call(s.pop("low_own"), over_core(s.pop("low_other")), kernel_index)
            )

        run(s2)

        def s3(s, new):
            scatter(s, 0)
            far(s, new, 1)
            near(s, new, 2)
            attention_back(s, new, 1)
            made(new, 3, [s["att", 0], s["att", 1]], s["mid_low"])
            new["out0"] = collect(s["out"], 0)
            held.append({"out1": collect(s["out"], 1)})

        run(s3)

        def s4(s, new):
            scatter(s, 1)
            far(s, new, 2)
            near(s, new, 3)
            made(new, 4, [s["dkv", 0], s["dkv", 1]], s["normed"])
            new["own"], new["other"] = one_part_call(
                (s["dq", 0], s["dq", 1]), (s["dkv", 0], s["dkv", 1]), s["w", 0], lead, s["w", 1]
            )

        run(s4)

        def s5(s, new):
            scatter(s, 2)
            far(s, new, 3)
            near(s, new, 4)
            dx, gain_grads = one_back_call(
                s.pop("own"), over_core(s.pop("other")), s.pop("x"), s.pop("grad_mid"), s["gains"],
                s.pop("gain_two"), kernel_index,
            )
            new["dx"] = outside(dx)
            made(new, 5, [s["dq", 0], s["dq", 1]], s["normed"], gain_grads)

        run(s5)

        def s6(s, new):
            far(s, new, 4)
            near(s, new, 5)
            column(s, new, 3)
            held.append({"dx0": collect(s["dx"], 0), "dx1": collect(s["dx"], 1)})

        run(s6)

        def s7(s, new):
            far(s, new, 5)
            column(s, new, 4)
            trade(s, new, 0, 1, 2, 3)

        run(s7)

        def s8(s, new):
            column(s, new, 5)

        run(s8)

        def s9(s, new):
            trade(s, new, 4, 5)

        run(s9)

        layer_output = assemble(state["out0"], state["out1"])
        input_gradient = assemble(state["dx0"], state["dx1"])
        def joined(k, rows):
            return jnp.concatenate(state["grad", k], axis=0)[:rows]

        grad_down, grad_up, grad_gate = (joined(k, hidden_local) for k in range(3))
        grad_out = joined(3, head_columns)
        key_value = [g.reshape(2, head_cut, block) for g in state["grad", 4]]
        query = [g[lead:] for g in state["grad", 5]]
        grad_qkv = jnp.stack(
            [jnp.concatenate(query, axis=0)]
            + [jnp.concatenate([g[i] for g in key_value], axis=0) for i in range(2)]
        ).transpose(2, 0, 1)
        gain_total = sum(g[:2] for g in state["grad", 5])
        grad_expand = jnp.stack([grad_up, grad_gate]).transpose(2, 0, 1)
        step_rates = (
            2.5 * D ** (-0.5),
            2.5 * max(1, 4 * H * DH // SEQ) ** (-0.5),
            2.5 * D ** (-0.5),
            2.5 * FF ** (-0.5),
            0.25,
        )
        grad_qkv, grad_out, grad_expand, grad_down = lax.optimization_barrier(
            (grad_qkv, grad_out.T, grad_expand, grad_down.T)
        )
        qkv_new = adamw_update(
            attention_in, attention_in_first, attention_in_second, grad_qkv, step_rates[0]
        )
        out_new = adamw_update(
            attention_out, attention_out_first, attention_out_second, grad_out, step_rates[1]
        )
        expand_new = adamw_update(
            expand_weight, expand_first, expand_second, grad_expand, step_rates[2]
        )
        contract_new = adamw_update(
            contract_weight, contract_first, contract_second, grad_down, step_rates[3]
        )
        gains_new = adamw_update(norm_gains, gains_first, gains_second, gain_total, step_rates[4])
        return (
            layer_output,
            input_gradient,
            *qkv_new,
            *out_new,
            *expand_new,
            *contract_new,
            *gains_new,
        )

    return per_device


def solution(mesh):
    activation = P(None, "dp", "tensor", None)
    cube = P("dp", None, "tensor")
    flat = P("dp", "tensor")
    gain = P(None, "dp")
    return jax.shard_map(
        make_per_device(mesh.shape["dp"], mesh.shape["tensor"]),
        mesh=mesh,
        in_specs=(
            activation, activation, cube, flat, cube, flat, gain,
            cube, cube, flat, flat, cube, cube, flat, flat, gain, gain,
        ),
        out_specs=(
            activation, activation, cube, cube, cube, flat, flat, flat,
            cube, cube, cube, flat, flat, flat, gain, gain, gain,
        ),
        check_vma=False,
    )
```

time: 660 us -> 476 us (0.72)
  matrix products: 97.5 us -> 0 us
  blocking collectives: 57.1 us -> 0 us
  waiting for transfers between devices: 174 us -> 126 us
  Pallas kernels: 67.1 us -> 109 us
  starting transfers between devices: 134 us -> 92.6 us
  between operations: 3.55 us -> 16.6 us
  local copies, waits for them, and re-layouts: 55.6 us -> 62.8 us
    dot_general x32 -> x0, matrix products: 97.5 us -> none  [the longest x12 34.7 us: dot_nn(): return jnp.dot(left, right, preferred_element_type=f32)]
    ppermute x116 -> x81, waiting for transfers between devices: 174 us -> 126 us  [permute(): return lax.ppermute(value, AXES, pairs)]
    pallas_call x8 -> x24, Pallas kernels: 67.1 us -> 109 us  [the longest x2 25.9 us: attend_back_call(): call(kernel, 'attention_backward', (count, 2), [half, full, full, half, o...]
    ppermute x116 -> x81, starting transfers between devices: 134 us -> 92.4 us  [permute(): return lax.ppermute(value, AXES, pairs)]
    psum x1 -> x0, blocking collectives: 37.4 us -> none  [per_device(): gain_total = lax.psum(gain_grads, AXES)]
    unnamed x328 -> x285, local copies, waits for them, and re-layouts: 13.4 us -> 43.8 us
    all_gather x1 -> x0, blocking collectives: 19.6 us -> none  [per_device(): lax.all_gather(norm_gains.astype(bf16), 'dp', axis=1, tiled=True)]
    convert_element_type x25 -> x30, other arithmetic: 16.9 us -> 28.4 us  [the longest x18 22.9 us: low_sum(): return sum((v.astype(f32) for v in values)).astype(bf16)]
  transfers between devices with their start and end apart: 116 -> 85, of which waited for: 51 -> 26; matrix products, arithmetic and copies ran while one was open for 22% -> 12% of each run, Pallas kernels for 8% -> 20%
where the time goes in v2:
time: 476 us; the launch traced here: 467 us
  waiting for transfers between devices  126 us (26%)
  Pallas kernels  109 us (23%)
  starting transfers between devices  92.6 us (19%)
  local copies, waits for them, and re-layouts  62.8 us (13%)
  other arithmetic  59.7 us (13%)
  between operations  16.6 us (3%)
    ppermute x81, waiting for transfers between devices, permute(): return lax.ppermute(value, AXES, pairs)  126 us
    ppermute x81, starting transfers between devices, permute(): return lax.ppermute(value, AXES, pairs)  92.4 us
    unnamed x285, local copies, waits for them, and re-layouts  43.8 us
    pallas_call x2, Pallas kernels, attend_back_call(): call(kernel, 'attention_backward', (count, 2), [half, full, full, half, o...  25.9 us
    convert_element_type x18, other arithmetic, low_sum(): return sum((v.astype(f32) for v in values)).astype(bf16)  22.9 us
    pallas_call x6, Pallas kernels, weight_gradient_call(): call(kernel, 'weight_gradient', (1,), [whole(a) for a in (*lefts, right,...  18.4 us
    pallas_call x2, Pallas kernels, attend_call(): call(kernel, 'attention_forward', (count, 2), [half, full, full], [out_ha...  16.8 us
  transfers between devices with their start and end apart: 85, of which 26 were waited for; matrix products, arithmetic and copies ran while one was open for 12% of the time, Pallas kernels for 20%

profile of v2, /device:TPU:0, one launch (start us, length us, event | category | flops | bytes accessed | tf_op | source)
XLA Modules:
  0.0 467.1 jit_solution(3053009986117306189)
XLA Ops:
  16.0 4.7 %collective-permute-start.1 = (bf16[144,256]{1,0:T(8,128)(2,1)S(1)}, bf16[144,256]{1,0:T(8,128)(2,1)S(1)}, u32[]{:S(2)}, u32[]{:S(2)}) collective-permute-start(bf16[144,256]{1,0:T(8,128)(2,1)S(1)} %slice.510), channel_id=1, source_target_pairs={{0,3},{1,2},{2,1},{3,0},{4,7},{5,6},{6,5},{7,4},{8,11},{9,10},{10,... | collective-permute-start | bytes 221192 | tf_op jit(solution)/shard_map/ppermute | solution.py:655
  37.4 20.5 %collective-permute-done.7 = bf16[384,256]{1,0:T(8,128)(2,1)S(1)} collective-permute-done((bf16[384,256]{1,0:T(8,128)(2,1)S(1)}, bf16[384,256]{1,0:T(8,128)(2,1)S(1)}, u32[]{:S(2)}, u32[]{:S(2)}) %collective-permute-start.7) | collective-permute-done | bytes 196640 | tf_op jit(solution)/shard_map/ppermute | solution.py:655
  67.2 4.4 collective-permute-start.13
  74.9 5.4 %collective-permute-start.14 = (bf16[256,1024]{1,0:T(8,128)(2,1)}, bf16[256,1024]{1,0:T(8,128)(2,1)}, u32[]{:S(2)}, u32[]{:S(2)}) collective-permute-start(bf16[256,1024]{1,0:T(8,128)(2,1)} %dynamic-slice_bitcast_fusion.3), channel_id=1, source_target_pairs={{0,0},{1,4},{2,2},{3,6},{4,1},{5,5},{6,3},{7,7},{8,8},{9,12},{10,1... | collective-permute-start | bytes 1572872 | tf_op jit(solution)/shard_map/ppermute | solution.py:655
  80.2 4.0 collective-permute-done.12
  98.7 20.3 %collective-permute-done.17 = bf16[256,1024]{1,0:T(8,128)(2,1)S(1)} collective-permute-done((bf16[256,1024]{1,0:T(8,128)(2,1)S(1)}, bf16[256,1024]{1,0:T(8,128)(2,1)S(1)}, u32[]{:S(2)}, u32[]{:S(2)}) %collective-permute-start.17) | collective-permute-done | bytes 524320 | tf_op jit(solution)/shard_map/ppermute | solution.py:655
  134.2 6.5 %qkv_projection.1 = (bf16[4,1024,128]{2,1,0:T(8,128)(2,1)S(1)}, bf16[4,1024,128]{2,1,0:T(8,128)(2,1)S(1)}, bf16[4,1024,128]{2,1,0:T(8,128)(2,1)S(1)}) custom-call(bf16[1024,1024]{1,0:T(8,128)(2,1)S(1)} %get-tuple-element.640.x_ref.refs_2_, bf16[4,144,1024]{2,1,0:T(8,128)(2,1)S(1)} %copy-done.15, ...), custom_call_target="tpu_custom_call" | custom-call | flops 2100000000 | bytes 7200000 | tf_op jit(solution)/shard_map/qkv_projection/pallas_call | solution.py:183
  140.7 8.4 %attention_forward.2 = (bf16[2,1024,128]{2,1,0:T(8,128)(2,1)S(1)}, f32[2,2,1024]{2,1,0:T(2,128)S(1)}) custom-call(bf16[4,1024,128]{2,1,0:T(8,128)(2,1)S(1)} %get-tuple-element.576.q_ref, bf16[4,1024,128]{2,1,0:T(8,128)(2,1)S(1)} %get-tuple-element.577.k_ref, bf16[4,1024,128]{2,1,0:T(8,128)(2,1)S(1)} %get-tuple-element.578.v_ref), custom_call_target="tpu_custom_call" | custom-call | flops 3150000128 | bytes 10800000 | tf_op jit(solution)/shard_map/attention_forward/pallas_call | solution.py:223
  156.1 8.4 %attention_forward.3 = (bf16[2,1024,128]{2,1,0:T(8,128)(2,1)S(1)}, f32[2,2,1024]{2,1,0:T(2,128)S(1)}) custom-call(bf16[4,1024,128]{2,1,0:T(8,128)(2,1)S(1)} %get-tuple-element.576.q_ref, bf16[4,1024,128]{2,1,0:T(8,128)(2,1)S(1)} %get-tuple-element.577.k_ref, bf16[4,1024,128]{2,1,0:T(8,128)(2,1)S(1)} %get-tuple-element.578.v_ref), custom_call_target="tpu_custom_call" | custom-call | flops 3150000128 | bytes 10800000 | tf_op jit(solution)/shard_map/attention_forward/pallas_call | solution.py:223
  166.1 13.6 %collective-permute-done.25 = bf16[256,1024]{1,0:T(8,128)(2,1)S(1)} collective-permute-done((bf16[256,1024]{1,0:T(8,128)(2,1)S(1)}, bf16[256,1024]{1,0:T(8,128)(2,1)S(1)}, u32[]{:S(2)}, u32[]{:S(2)}) %collective-permute-start.25) | collective-permute-done | bytes 524320 | tf_op jit(solution)/shard_map/ppermute | solution.py:655
  183.0 8.1 %collective-permute-done.27 = bf16[672,256]{1,0:T(8,128)(2,1)S(1)} collective-permute-done((bf16[672,256]{1,0:T(8,128)(2,1)S(1)}, bf16[672,256]{1,0:T(8,128)(2,1)S(1)}, u32[]{:S(2)}, u32[]{:S(2)}) %collective-permute-start.27) | collective-permute-done | bytes 344096 | tf_op jit(solution)/shard_map/ppermute | solution.py:655
  197.0 7.6 %expand.1 = (bf16[1024,1344]{1,0:T(8,128)(2,1)S(1)}, bf16[1024,1344]{1,0:T(8,128)(2,1)S(1)}, bf16[1024,1344]{1,0:T(8,128)(2,1)S(1)}) custom-call(bf16[1024,1024]{1,0:T(8,128)(2,1)S(1)} %get-tuple-element.558.x_ref.refs_1_, bf16[4,336,1024]{2,1,0:T(8,128)(2,1)S(1)} %pad_maximum_fusion.1.up_ref, bf16[4,336,1024]{2,1,0:T(8,128)(2,1)S(1)} %pad_maximum_fusion.2.gate_ref.w_gate_ref), custom_call_target="tpu_custom_call" | custom-call | flops 4200000000 | bytes 14400000 | tf_op jit(solution)/shard_map/expand/pallas_call | solution.py:366
  204.6 3.9 weight_gradient.6
  214.5 4.0 weight_gradient.7
  228.4 7.0 %grad_normed_two.1.part_ref = bf16[1024,1024]{1,0:T(8,128)(2,1)S(1)} custom-call(bf16[1024,1344]{1,0:T(8,128)(2,1)S(1)} %copy-done.8, bf16[1024,1344]{1,0:T(8,128)(2,1)S(1)} %copy-done.6, bf16[4,336,1024]{2,1,0:T(8,128)(2,1)S(1)} %pad_maximum_fusion.1.up_ref, bf16[4,336,1024]{2,1,0:T(8,128)(2,1)S(1)} %pad_maximum_fusion.2.gate_ref.w_gate_ref), custom_call_target="tpu_custom_call" | custom-call | flops 2800000000 | bytes 9600000 | tf_op jit(solution)/shard_map/grad_normed_two/pallas_call | solution.py:508
  240.6 7.6 %collective-permute-done.41 = bf16[2,336,256]{2,1,0:T(8,128)(2,1)S(1)} collective-permute-done((bf16[2,336,256]{2,1,0:T(8,128)(2,1)S(1)}, bf16[2,336,256]{2,1,0:T(8,128)(2,1)S(1)}, u32[]{:S(2)}, u32[]{:S(2)}) %collective-permute-start.41) | collective-permute-done | bytes 344096 | tf_op jit(solution)/shard_map/ppermute | solution.py:655
  249.3 4.0 weight_gradient.8
  266.4 12.8 %attention_backward.2 = (bf16[2,1024,128]{2,1,0:T(8,128)(2,1)S(1)}, bf16[2,1024,256]{2,1,0:T(8,128)(2,1)S(1)}) custom-call(bf16[4,1024,128]{2,1,0:T(8,128)(2,1)S(1)} %copy-done.67, bf16[4,1024,128]{2,1,0:T(8,128)(2,1)S(1)} %copy-done.70, bf16[4,1024,128]{2,1,0:T(8,128)(2,1)S(1)} %copy-done.73, bf16[4,1024,128]{2,1,0:T(8,128)(2,1)S(1)} %grad_attended.1.grad_ref, ...), custom_call_target="tpu_custom_call" | custom-call | flops 4899999744 | bytes 16800000 | tf_op jit(solution)/shard_map/attention_backward/pallas_call | solution.py:281
  286.3 5.3 %collective-permute-start.50 = (bf16[256,1024]{1,0:T(8,128)(2,1)}, bf16[256,1024]{1,0:T(8,128)(2,1)}, u32[]{:S(2)}, u32[]{:S(2)}) collective-permute-start(bf16[256,1024]{1,0:T(8,128)(2,1)} %get-tuple-element.855), channel_id=1, source_target_pairs={{0,0},{4,1},{2,2},{6,3},{1,4},{5,5},{3,6},{7,7},{8,8},{12,9},{10,1... | collective-permute-start | bytes 1572872 | tf_op jit(solution)/shard_map/ppermute | solution.py:655
  301.4 13.0 %attention_backward.3 = (bf16[2,1024,128]{2,1,0:T(8,128)(2,1)S(1)}, bf16[2,1024,256]{2,1,0:T(8,128)(2,1)S(1)}) custom-call(bf16[4,1024,128]{2,1,0:T(8,128)(2,1)S(1)} %copy-done.68, bf16[4,1024,128]{2,1,0:T(8,128)(2,1)S(1)} %copy-done.71, bf16[4,1024,128]{2,1,0:T(8,128)(2,1)S(1)} %copy-done.74, bf16[4,1024,128]{2,1,0:T(8,128)(2,1)S(1)} %copy-done.20, ...), custom_call_target="tpu_custom_call" | custom-call | flops 4899999744 | bytes 16800000 | tf_op jit(solution)/shard_map/attention_backward/pallas_call | solution.py:281
  333.2 4.0 grad_normed_one.1
  382.8 5.6 %collective-permute-start.75 = (bf16[256,1024]{1,0:T(8,128)(2,1)}, bf16[256,1024]{1,0:T(8,128)(2,1)}, u32[]{:S(2)}, u32[]{:S(2)}) collective-permute-start(bf16[256,1024]{1,0:T(8,128)(2,1)} %get-tuple-element.851), channel_id=1, source_target_pairs={{0,0},{4,1},{2,2},{6,3},{1,4},{5,5},{3,6},{7,7},{8,8},{12,9},{10,1... | collective-permute-start | bytes 1572872 | tf_op jit(solution)/shard_map/ppermute | solution.py:655
  398.5 11.9 %collective-permute-done.73 = bf16[256,256]{1,0:T(8,128)(2,1)S(1)} collective-permute-done((bf16[256,256]{1,0:T(8,128)(2,1)S(1)}, bf16[256,256]{1,0:T(8,128)(2,1)S(1)}, u32[]{:S(2)}, u32[]{:S(2)}) %collective-permute-start.73) | collective-permute-done | bytes 131104 | tf_op jit(solution)/shard_map/ppermute | solution.py:655
  411.5 10.4 %collective-permute-done.72 = bf16[256,256]{1,0:T(8,128)(2,1)S(1)} collective-permute-done((bf16[256,256]{1,0:T(8,128)(2,1)S(1)}, bf16[256,256]{1,0:T(8,128)(2,1)S(1)}, u32[]{:S(2)}, u32[]{:S(2)}) %collective-permute-start.72) | collective-permute-done | bytes 131104 | tf_op jit(solution)/shard_map/ppermute | solution.py:655
  (617 shorter events, 249.0 us)
Async XLA Ops:
  7.2 80.7 %all-gather.3.cloned.1.call-start = ((), (), s32[]{:S(2)}) async-start(), calls=%async_computation.6 | async-start | bytes 1720320 | tf_op jit(solution)/shard_map/all_gather | solution.py:871
  30.1 27.7 %collective-permute-start.7 = (bf16[384,256]{1,0:T(8,128)(2,1)S(1)}, bf16[384,256]{1,0:T(8,128)(2,1)S(1)}, u32[]{:S(2)}, u32[]{:S(2)}) collective-permute-start(bf16[384,256]{1,0:T(8,128)(2,1)S(1)} %slice.511), channel_id=1, source_target_pairs={{0,2},{1,3},{2,0},{3,1},{4,6},{5,7},{6,4},{7,5},{8,10},{9,11},{10,... | collective-permute-start | bytes 589832 | tf_op jit(solution)/shard_map/ppermute | solution.py:655
  30.2 28.4 %collective-permute-start.8 = (bf16[384,256]{1,0:T(8,128)(2,1)S(1)}, bf16[384,256]{1,0:T(8,128)(2,1)}, u32[]{:S(2)}, u32[]{:S(2)}) collective-permute-start(bf16[384,256]{1,0:T(8,128)(2,1)S(1)} %slice.511), channel_id=1, source_target_pairs={{0,1},{1,0},{2,3},{3,2},{4,5},{5,4},{6,7},{7,6},{8,9},{9,8},{10,11... | collective-permute-start | bytes 589832 | tf_op jit(solution)/shard_map/ppermute | solution.py:655
  32.8 317.3 %reduce-scatter.4.cloned.1.call-start = ((), (), s32[]{:S(2)}) async-start(), calls=%async_computation.3 | async-start | bytes 860160 | tf_op jit(solution)/shard_map/reduce_scatter | solution.py:961
  32.9 26.9 %collective-permute-start.4 = (bf16[576,256]{1,0:T(8,128)(2,1)S(1)}, bf16[576,256]{1,0:T(8,128)(2,1)S(1)}, u32[]{:S(2)}, u32[]{:S(2)}) collective-permute-start(bf16[576,256]{1,0:T(8,128)(2,1)S(1)} %bitcast.196), channel_id=1, source_target_pairs={{0,8},{1,9},{2,10},{3,11},{4,12},{5,13},{6,14},{7,15},{8,0},{9,1},... | collective-permute-start | bytes 884744 | tf_op jit(solution)/shard_map/ppermute | solution.py:655
  34.4 25.4 %collective-permute-start.5 = (bf16[576,256]{1,0:T(8,128)(2,1)S(1)}, bf16[576,256]{1,0:T(8,128)(2,1)S(1)}, u32[]{:S(2)}, u32[]{:S(2)}) collective-permute-start(bf16[576,256]{1,0:T(8,128)(2,1)S(1)} %bitcast.197), channel_id=1, source_target_pairs={{0,16},{1,17},{2,18},{3,19},{4,20},{5,21},{6,22},{7,23},{8,24},{9,... | collective-permute-start | bytes 884744 | tf_op jit(solution)/shard_map/ppermute | solution.py:655
  93.1 27.1 %collective-permute-start.15 = (bf16[2112,256]{1,0:T(8,128)(2,1)}, bf16[2112,256]{1,0:T(8,128)(2,1)}, u32[]{:S(2)}, u32[]{:S(2)}) collective-permute-start(bf16[2112,256]{1,0:T(8,128)(2,1)} %get-tuple-element.883), channel_id=1, source_target_pairs={{0,8},{1,9},{2,10},{3,11},{4,12},{5,13},{6,14},{7,15},{8,0},{9,1},... | collective-permute-start | bytes 3244040 | tf_op jit(solution)/shard_map/ppermute | solution.py:655
  94.5 26.6 %collective-permute-start.16 = (bf16[2112,256]{1,0:T(8,128)(2,1)}, bf16[2112,256]{1,0:T(8,128)(2,1)}, u32[]{:S(2)}, u32[]{:S(2)}) collective-permute-start(bf16[2112,256]{1,0:T(8,128)(2,1)} %get-tuple-element.882), channel_id=1, source_target_pairs={{0,16},{1,17},{2,18},{3,19},{4,20},{5,21},{6,22},{7,23},{8,24},{9,... | collective-permute-start | bytes 3244040 | tf_op jit(solution)/shard_map/ppermute | solution.py:655
  152.5 27.3 %collective-permute-start.23 = (bf16[2016,256]{1,0:T(8,128)(2,1)S(1)}, bf16[2016,256]{1,0:T(8,128)(2,1)S(1)}, u32[]{:S(2)}, u32[]{:S(2)}) collective-permute-start(bf16[2016,256]{1,0:T(8,128)(2,1)S(1)} %get-tuple-element.879), channel_id=1, source_target_pairs={{0,8},{1,9},{2,10},{3,11},{4,12},{5,13},{6,14},{7,15},{8,0},{9,1},... | collective-permute-start | bytes 3096584 | tf_op jit(solution)/shard_map/ppermute | solution.py:655
  153.9 25.9 %collective-permute-start.24 = (bf16[2016,256]{1,0:T(8,128)(2,1)S(1)}, bf16[2016,256]{1,0:T(8,128)(2,1)S(1)}, u32[]{:S(2)}, u32[]{:S(2)}) collective-permute-start(bf16[2016,256]{1,0:T(8,128)(2,1)S(1)} %get-tuple-element.878), channel_id=1, source_target_pairs={{0,16},{1,17},{2,18},{3,19},{4,20},{5,21},{6,22},{7,23},{8,24},{9,... | collective-permute-start | bytes 3096584 | tf_op jit(solution)/shard_map/ppermute | solution.py:655
  208.5 26.8 %collective-permute-start.34 = (bf16[4,336,256]{2,1,0:T(8,128)(2,1)}, bf16[4,336,256]{2,1,0:T(8,128)(2,1)}, u32[]{:S(2)}, u32[]{:S(2)}) collective-permute-start(bf16[4,336,256]{2,1,0:T(8,128)(2,1)} %get-tuple-element.509), channel_id=1, source_target_pairs={{0,16},{1,17},{2,18},{3,19},{4,20},{5,21},{6,22},{7,23},{8,24},{9,... | collective-permute-start | bytes 2064392 | tf_op jit(solution)/shard_map/ppermute | solution.py:655
  209.3 27.1 %collective-permute-start.35 = (bf16[4,336,256]{2,1,0:T(8,128)(2,1)}, bf16[4,336,256]{2,1,0:T(8,128)(2,1)}, u32[]{:S(2)}, u32[]{:S(2)}) collective-permute-start(bf16[4,336,256]{2,1,0:T(8,128)(2,1)} %get-tuple-element.511), channel_id=1, source_target_pairs={{0,8},{1,9},{2,10},{3,11},{4,12},{5,13},{6,14},{7,15},{8,0},{9,1},... | collective-permute-start | bytes 2064392 | tf_op jit(solution)/shard_map/ppermute | solution.py:655
  281.2 35.4 %collective-permute-start.47 = (bf16[2,336,256]{2,1,0:T(8,128)(2,1)}, bf16[2,336,256]{2,1,0:T(8,128)(2,1)}, u32[]{:S(2)}, u32[]{:S(2)}) collective-permute-start(bf16[2,336,256]{2,1,0:T(8,128)(2,1)} %add_convert_fusion.3), channel_id=1, source_target_pairs={{0,8},{1,9},{2,10},{3,11},{4,12},{5,13},{6,14},{7,15},{8,0},{9,1},... | collective-permute-start | bytes 1032200 | tf_op jit(solution)/shard_map/ppermute | solution.py:655
  281.8 35.4 %collective-permute-start.46 = (bf16[2,336,256]{2,1,0:T(8,128)(2,1)}, bf16[2,336,256]{2,1,0:T(8,128)(2,1)}, u32[]{:S(2)}, u32[]{:S(2)}) collective-permute-start(bf16[2,336,256]{2,1,0:T(8,128)(2,1)} %add_convert_fusion.2), channel_id=1, source_target_pairs={{0,16},{1,17},{2,18},{3,19},{4,20},{5,21},{6,22},{7,23},{8,24},{9,... | collective-permute-start | bytes 1032200 | tf_op jit(solution)/shard_map/ppermute | solution.py:655
  282.6 36.0 %collective-permute-start.48 = (bf16[4,336,256]{2,1,0:T(8,128)(2,1)}, bf16[4,336,256]{2,1,0:T(8,128)(2,1)}, u32[]{:S(2)}, u32[]{:S(2)}) collective-permute-start(bf16[4,336,256]{2,1,0:T(8,128)(2,1)} %get-tuple-element.594), channel_id=1, source_target_pairs={{0,16},{1,17},{2,18},{3,19},{4,20},{5,21},{6,22},{7,23},{8,24},{9,... | collective-permute-start | bytes 2064392 | tf_op jit(solution)/shard_map/ppermute | solution.py:655
  283.8 36.6 %collective-permute-start.49 = (bf16[4,336,256]{2,1,0:T(8,128)(2,1)}, bf16[4,336,256]{2,1,0:T(8,128)(2,1)}, u32[]{:S(2)}, u32[]{:S(2)}) collective-permute-start(bf16[4,336,256]{2,1,0:T(8,128)(2,1)} %get-tuple-element.596), channel_id=1, source_target_pairs={{0,8},{1,9},{2,10},{3,11},{4,12},{5,13},{6,14},{7,15},{8,0},{9,1},... | collective-permute-start | bytes 2064392 | tf_op jit(solution)/shard_map/ppermute | solution.py:655
  286.3 35.9 %collective-permute-start.50 = (bf16[256,1024]{1,0:T(8,128)(2,1)}, bf16[256,1024]{1,0:T(8,128)(2,1)}, u32[]{:S(2)}, u32[]{:S(2)}) collective-permute-start(bf16[256,1024]{1,0:T(8,128)(2,1)} %get-tuple-element.855), channel_id=1, source_target_pairs={{0,0},{4,1},{2,2},{6,3},{1,4},{5,5},{3,6},{7,7},{8,8},{12,9},{10,1... | collective-permute-start | bytes 1572872 | tf_op jit(solution)/shard_map/ppermute | solution.py:655
  292.6 79.9 %reduce-scatter.6.cloned.1.call-start = ((), (), s32[]{:S(2)}) async-start(), calls=%async_computation.4 | async-start | bytes 860160 | tf_op jit(solution)/shard_map/reduce_scatter | solution.py:961
  316.6 33.5 %collective-permute-start.55 = (bf16[256,1024]{1,0:T(8,128)(2,1)}, bf16[256,1024]{1,0:T(8,128)(2,1)}, u32[]{:S(2)}, u32[]{:S(2)}) collective-permute-start(bf16[256,1024]{1,0:T(8,128)(2,1)} %get-tuple-element.854), channel_id=1, source_target_pairs={{2,0},{6,1},{0,2},{4,3},{3,4},{7,5},{1,6},{5,7},{10,8},{14,9},{8,1... | collective-permute-start | bytes 1572872 | tf_op jit(solution)/shard_map/ppermute | solution.py:655
  327.3 63.9 %reduce-scatter.8.cloned.1.call-start = ((), (), s32[]{:S(2)}) async-start(), calls=%async_computation.5 | async-start | bytes 860160 | tf_op jit(solution)/shard_map/reduce_scatter | solution.py:961
  382.8 45.5 %collective-permute-start.75 = (bf16[256,1024]{1,0:T(8,128)(2,1)}, bf16[256,1024]{1,0:T(8,128)(2,1)}, u32[]{:S(2)}, u32[]{:S(2)}) collective-permute-start(bf16[256,1024]{1,0:T(8,128)(2,1)} %get-tuple-element.851), channel_id=1, source_target_pairs={{0,0},{4,1},{2,2},{6,3},{1,4},{5,5},{3,6},{7,7},{8,8},{12,9},{10,1... | collective-permute-start | bytes 1572872 | tf_op jit(solution)/shard_map/ppermute | solution.py:655
  388.4 39.8 %collective-permute-start.76 = (bf16[256,1024]{1,0:T(8,128)(2,1)}, bf16[256,1024]{1,0:T(8,128)(2,1)S(1)}, u32[]{:S(2)}, u32[]{:S(2)}) collective-permute-start(bf16[256,1024]{1,0:T(8,128)(2,1)} %get-tuple-element.850), channel_id=1, source_target_pairs={{2,0},{6,1},{0,2},{4,3},{3,4},{7,5},{1,6},{5,7},{10,8},{14,9},{8,1... | collective-permute-start | bytes 1572872 | tf_op jit(solution)/shard_map/ppermute | solution.py:655
  392.2 29.8 %collective-permute-start.72 = (bf16[256,256]{1,0:T(8,128)(2,1)S(1)}, bf16[256,256]{1,0:T(8,128)(2,1)S(1)}, u32[]{:S(2)}, u32[]{:S(2)}) collective-permute-start(bf16[256,256]{1,0:T(8,128)(2,1)S(1)} %get-tuple-element.899), channel_id=1, source_target_pairs={{0,2},{1,3},{2,0},{3,1},{4,6},{5,7},{6,4},{7,5},{8,10},{9,11},{10,... | collective-permute-start | bytes 393224 | tf_op jit(solution)/shard_map/ppermute | solution.py:655
  394.2 29.2 %collective-permute-start.71 = (bf16[256,256]{1,0:T(8,128)(2,1)S(1)}, bf16[256,256]{1,0:T(8,128)(2,1)S(1)}, u32[]{:S(2)}, u32[]{:S(2)}) collective-permute-start(bf16[256,256]{1,0:T(8,128)(2,1)S(1)} %get-tuple-element.898), channel_id=1, source_target_pairs={{0,1},{1,0},{2,3},{3,2},{4,5},{5,4},{6,7},{7,6},{8,9},{9,8},{10,11... | collective-permute-start | bytes 393224 | tf_op jit(solution)/shard_map/ppermute | solution.py:655
  (198 other events, 1705.8 us)
Sparse Core Ops, SparseCore 0:
  32.9 50.3 all-gather.2
  292.7 19.1 reduce-scatter.3
  327.4 22.6 reduce-scatter.5
  355.3 19.8 reduce-scatter.7

commit v3 on v2

--- a/solution.py
+++ b/solution.py
@@ -48,7 +48,9 @@
 
 
 def whole(array):
-    return pl.BlockSpec(array.shape, lambda i, rank=array.ndim: (0,) * rank)
+    return pl.BlockSpec(
+        array.shape, lambda i, rank=array.ndim: (0,) * rank, pipeline_mode=pl.Buffered(1)
+    )
 
 
 def by_block(array):
@@ -63,25 +65,31 @@
     return jax.ShapeDtypeStruct(shape, dtype)
 
 
-microseconds = {
-    "feature_order": 3.0,
-    "first_norm": 4.0,
-    "qkv_projection": 6.0,
-    "attention_forward": 9.0,
-    "attention_output": 2.5,
-    "second_norm": 4.0,
-    "expand": 12.0,
-    "contract": 5.0,
-    "layer_output": 2.0,
-    "weight_gradient": 5.0,
-    "grad_lifted": 6.0,
-    "grad_normed_two": 8.0,
-    "second_norm_gradient": 5.0,
-    "grad_attended": 2.5,
-    "attention_backward": 14.0,
-    "grad_normed_one": 6.0,
-    "first_norm_gradient": 3.0,
-}
+def kept(array):
+    return pltpu.HBM(array.shape, array.dtype)
+
+
+microseconds = dict(
+    feature_order=3.0,
+    gathered_weight=3.0,
+    gradient_sums=3.0,
+    first_norm=4.0,
+    qkv_projection=6.0,
+    attention_forward=9.0,
+    attention_output=2.5,
+    second_norm=4.0,
+    expand=12.0,
+    contract=5.0,
+    layer_output=2.0,
+    weight_gradient=5.0,
+    grad_lifted=6.0,
+    grad_normed_two=8.0,
+    second_norm_gradient=5.0,
+    grad_attended=2.5,
+    attention_backward=14.0,
+    grad_normed_one=6.0,
+    first_norm_gradient=3.0,
+)
 
 
 def cost(name):
@@ -137,6 +145,10 @@
     block = ref.shape[1] // count
     parts = [ref[:, pl.ds(pl.multiple_of(index_ref[j] * block, block), block)] for j in range(count)]
     return jnp.concatenate(parts, axis=1)
+
+
+def in_hbm(*arrays):
+    return tuple(pltpu.with_memory_space_constraint(a, pltpu.HBM) for a in arrays)
 
 
 scalars = pl.BlockSpec(memory_space=pltpu.SMEM)
@@ -196,6 +208,37 @@
         pl.BlockSpec((1, rows // halves, array.shape[2]), lambda z, i: (first + z, i, 0)),
         pl.BlockSpec((1, rows, array.shape[2]), lambda z, i: (first + z, 0, 0)),
     )
+
+
+def weave_call(column, x_near, y_near, x_far, y_far, far_rows):
+    blocks, rows, width = column.shape
+    half = blocks // 2
+
+    def kernel(col_ref, x_ref, y_ref, x_far_ref, y_far_ref, out_ref):
+        z = pl.program_id(0)
+        out_ref[0, :, :width] = col_ref[0]
+        out_ref[0, :, width : 2 * width] = x_ref[...]
+        out_ref[0, :, 2 * width : 3 * width] = y_ref[...]
+        start = pl.multiple_of(far_rows + z % half * rows, 16)
+
+        @pl.when(z < half)
+        def _():
+            out_ref[0, :, 3 * width :] = y_far_ref[pl.ds(start, rows), :]
+
+        @pl.when(z >= half)
+        def _():
+            out_ref[0, :, 3 * width :] = x_far_ref[pl.ds(start, rows), :]
+
+    near = pl.BlockSpec((rows, width), lambda z: (z, 0))
+    out = like((blocks, rows, 4 * width))
+    return call(
+        kernel,
+        "gathered_weight",
+        (blocks,),
+        [by_block(column), near, near, whole(x_far), whole(y_far)],
+        by_block(out),
+        out,
+    )(column, x_near, y_near, x_far, y_far)
 
 
 def attend_call(query, key, value, first, count):
@@ -286,7 +329,7 @@
         [out_half, pl.BlockSpec((1, rows, 256), lambda z, i: (z, 0, 0))],
         [like((count, rows, 128)), like((count, rows, 256))],
         [pltpu.VMEM((rows, 128), f32)] * 2,
-    )(query, key, value, grad, out, lse, cosine, sine)
+    )(*in_hbm(query, key, value, grad, out, lse, cosine, sine))
 
 
 def lanes_of(refs):
@@ -470,8 +513,49 @@
         (1,),
         [whole(a) for a in (*lefts, right, *more)],
         [whole(o) for o in out_shape],
+        [kept(o) for o in out_shape],
+    )(*lefts, right, *more)
+
+
+def combine_call(first, second, x_got, y_got, near_rows):
+    operands, out_shape = [], []
+    if first is not None:
+        operands += first[1:]
+        out_shape += [like(first[1].shape)] * 2
+    if second is not None:
+        operands += second
+        out_shape += [like(second[0].shape)]
+
+    def kernel(*refs):
+        ins, outs = list(refs[2 : 2 + len(operands)]), list(refs[2 + len(operands) :])
+        x_ref, y_ref = refs[:2]
+        if first is not None:
+            x_rest, y_rest, x_out, y_out = ins.pop(0), ins.pop(0), outs.pop(0), outs.pop(0)
+            half, rows = x_rest.shape[:2]
+            for j in range(half):
+                part = slice(j * rows, (j + 1) * rows)
+                x_out[j] = (x_rest[j].astype(f32) + y_ref[part].astype(f32)).astype(bf16)
+                y_out[j] = (y_rest[j].astype(f32) + x_ref[part].astype(f32)).astype(bf16)
+        if second is not None:
+            mine, x_near, y_near = ins
+            half, rows = mine.shape[0] // 2, mine.shape[1]
+            for j in range(half):
+                near = slice((half + j) * rows, (half + j + 1) * rows)
+                far = slice(near_rows + j * rows, near_rows + (j + 1) * rows)
+                for place, near_ref, far_ref in ((j, x_near, y_ref), (half + j, y_near, x_ref)):
+                    total = mine[place].astype(f32) + near_ref[near].astype(f32)
+                    outs[0][place] = (total + far_ref[far].astype(f32)).astype(bf16)
+
+    results = call(
+        kernel,
+        "gradient_sums",
+        (1,),
+        [whole(a) for a in (x_got, y_got, *operands)],
+        [whole(o) for o in out_shape],
         out_shape,
-    )(*lefts, right, *more)
+    )(x_got, y_got, *operands)
+    near = results[:2] if first is not None else None
+    return near, results[-1] if second is not None else None
 
 
 def hidden_back_call(dy, w, to_in, to_gate):
@@ -603,7 +687,7 @@
         [half(a) for a in (*queries, *keys_values)] + [whole(w_query), whole(w_key_value)],
         [first, first],
         [like((rows // 2, width), f32), like((rows // 2, width))],
-    )(*queries, *keys_values, w_query, w_key_value)
+    )(*in_hbm(*queries, *keys_values, w_query, w_key_value))
 
 
 def one_back_call(own, got, x, grad_middle, gains, gain_two, index):
@@ -644,6 +728,59 @@
     )(index, own, got, x, grad_middle, gains, gain_two)
 
 
+(
+    X_IN,
+    COT,
+    BOTH,
+    PAIR,
+    LOW,
+    INNER,
+    COLUMN,
+    W,
+    NEAR,
+    GRAD,
+    TABLES,
+    X0,
+    X_OWN,
+    GAINS,
+    X,
+    NORMED,
+    QKV,
+    ATT,
+    LSE,
+    Y0,
+    PART,
+    Y_OWN,
+    MIDDLE,
+    NORMED_TWO,
+    HIDDEN,
+    TO_IN,
+    TO_GATE,
+    DY,
+    G,
+    F,
+    N,
+    SUM,
+    G_GATE,
+    OUT,
+    DQ,
+    DKV,
+    G_ATT,
+    GRAD_MID,
+    MID_LOW,
+    GAIN_TWO,
+    OUT1,
+    OWN,
+    OTHER,
+    OUT0,
+    GAIN_GRADS,
+    DX,
+    DX1,
+    DX0,
+    UPDATED,
+) = range(49)
+
+
 def make_per_device(dp, tensor):
     count = dp * tensor
     chips = dp // 2
@@ -660,10 +797,7 @@
     def over_chip(value, bit):
         return exchange(value, (2 * tensor) << bit)
 
-    def over_core(value):
-        pieces = max(1, value.size // (1 << 18))
-        if value.ndim != 2 or value.shape[0] % (16 * pieces):
-            pieces = 1
+    def over_core(value, pieces=1):
         rows = value.shape[0] // pieces
         got = [exchange(value[i * rows : (i + 1) * rows], tensor) for i in range(pieces)]
         return got[0] if pieces == 1 else jnp.concatenate(got, axis=0)
@@ -683,8 +817,19 @@
             blocks = [jnp.where(odd, blocks[k ^ (1 << bit)], blocks[k]) for k in range(tensor)]
         return blocks
 
-    def gather_column(rows, me_z):
-        return by_column([rows] + [exchange(rows, k) for k in range(1, tensor)], me_z)
+    inner = [(i, i ^ 3) for i in range(count) if i % tensor in (1, 2)]
+    outward = [(i, i ^ 1) for i in range(count) if i % tensor in (1, 2)]
+
+    def gather_near_z(rows, me_z):
+        got = exchange(rows, 1)
+        low = me_z % 2 == 0
+        return jnp.stack([jnp.where(low, rows, got), jnp.where(low, got, rows)])
+
+    def gather_far_z(pair, got, me_z):
+        sent = permute(got, outward)
+        other = jnp.where((me_z == 0) | (me_z == 3), sent, got)
+        low = me_z < 2
+        return jnp.concatenate([jnp.where(low, pair, other), jnp.where(low, other, pair)], axis=0)
 
     def gather_plane(columns):
         current = columns[None]
@@ -759,15 +904,17 @@
             odd = z_high == 1
             return jnp.stack([jnp.where(odd, second, first), jnp.where(odd, first, second)])[:, None]
 
-        row_starts = [
-            ((r ^ z_high) * 2 + (core ^ c)) * local_rows for c in range(2) for r in range(2)
-        ]
-        positions = jnp.concatenate([s + jnp.arange(local_rows) for s in row_starts]).astype(f32)
-        exponents = jnp.arange(0, DH, 2).astype(f32) / DH
-        angles = positions[:, None] * jnp.power(rope_theta, -exponents)[None, :]
-        cosine, sine = jnp.cos(angles), jnp.sin(angles)
-        cosine = jnp.concatenate([cosine] * 4, axis=-1)
-        sine = jnp.concatenate([-sine, sine] * 2, axis=-1)
+        def rotary_tables():
+            row_starts = [
+                ((r ^ z_high) * 2 + (core ^ c)) * local_rows for c in range(2) for r in range(2)
+            ]
+            positions = jnp.concatenate([s + jnp.arange(local_rows) for s in row_starts]).astype(f32)
+            exponents = jnp.arange(0, DH, 2).astype(f32) / DH
+            angles = positions[:, None] * jnp.power(rope_theta, -exponents)[None, :]
+            cosine, sine = jnp.cos(angles), jnp.sin(angles)
+            cosine = jnp.concatenate([cosine] * 4, axis=-1)
+            sine = jnp.concatenate([-sine, sine] * 2, axis=-1)
+            return cosine, sine
 
         cut = (hidden_local // 2 + 15) // 16 * 16
         spare = 2 * cut - hidden_local
@@ -800,7 +947,7 @@
                 [jnp.where(first_core, mine, got), jnp.where(first_core, got, mine)], axis=-1
             )
 
-        state = {"tables": (cosine, sine), "x_in": inputs, "cot": cotangent, "both": both}
+        state = {X_IN: inputs, COT: cotangent, BOTH: both}
         held = []
         again = []
 
@@ -817,285 +964,44 @@
             names = list(state)
             state = dict(zip(names, lax.optimization_barrier([state[n] for n in names])))
 
-        def columns(s, new, first, count):
-            low = s["low"][starts[first] : starts[first + count]]
-            blocks = gather_column(low, me_z)
-            for k in range(first, first + count):
-                a, b = starts[k] - starts[first], starts[k + 1] - starts[first]
-                new["column", k] = jnp.stack([block[a:b] for block in blocks])
+        def column_a(s, new, k):
+            stop = starts[k + 1] if k < 3 else starts[last]
+            new[PAIR, k] = gather_near_z(s[LOW][starts[k] : stop], me_z)
+
+        def column_b(s, new, k):
+            new[INNER, k] = permute(s[PAIR, k], inner)
+
+        def column_c(s, new, k):
+            column = gather_far_z(s.pop((PAIR, k)), s.pop((INNER, k)), me_z)
+            if k < 3:
+                new[COLUMN, k] = column
+            else:
+                new[COLUMN, 3], new[COLUMN, 4] = column[:, : sizes[3]], column[:, sizes[3] :]
 
         def plane(s, new, k):
             if not square:
                 if k < last:
-                    new["w", k] = gather_plane(s.pop(("column", k)))
+                    new[W, k] = gather_plane(s.pop((COLUMN, k)))
                 return
             sends, first_rows = ([], []), 0
             if k < last:
-                column = s["column", k]
+                column = s[COLUMN, k]
                 first_rows = column.shape[0] * column.shape[1]
                 for way in range(2):
                     sends[way].append(column.reshape(first_rows, -1))
             if k > 0:
-                got = s["near", k - 1]
+                got = s[NEAR, k - 1]
                 rows = half * sizes[k - 1]
                 sends[0].append(got[1][rows : 2 * rows])
                 sends[1].append(got[0][:rows])
             got = tuple(over_chip(jnp.concatenate(sends[way], axis=0), way) for way in range(2))
             if k < last:
-                new["near", k] = got
+                new[NEAR, k] = got
             if k > 0:
-                shape = (tensor, sizes[k - 1], -1)
-                rows = tensor * sizes[k - 1]
-                x_got, y_got = s.pop(("near", k - 1))
-                diagonal = jnp.concatenate([got[1][first_rows:], got[0][first_rows:]], axis=0)
-                new["w", k - 1] = jnp.concatenate(
-                    [
-                        s.pop(("column", k - 1)),
-                        x_got[:rows].reshape(shape),
-                        y_got[:rows].reshape(shape),
-                        diagonal.reshape(shape),
-                    ],
-                    axis=-1,
+                new[W, k - 1] = weave_call(
+                    s.pop((COLUMN, k - 1)), *s.pop((NEAR, k - 1)), *got, first_rows
                 )
 
-        def f0(s, new):
-            pair = s.pop("both")
-            mine = jnp.where(first_core, pair[0], pair[1])
-            got = over_core(jnp.where(first_core, pair[1], pair[0]))
-            new["low"] = side_by_side(mine, got)
-
-        run(f0)
-
-        def f1(s, new):
-            columns(s, new, 0, 1)
-            late = lax.all_gather(s["low"][starts[3] :], "tensor", axis=0)
-            again.append({("column", 3): late[:, : sizes[3]], ("column", 4): late[:, sizes[3] :]})
-
-        run(f1)
-
-        def f2(s, new):
-            plane(s, new, 0)
-            columns(s, new, 1, 1)
-
-        run(f2)
-
-        def f3(s, new):
-            plane(s, new, 1)
-            columns(s, new, 2, 1)
-            new["x0"] = spread(s["x_in"], 0)
-
-        run(f3)
-
-        def f4(s, new):
-            plane(s, new, 2)
-            rows = jnp.concatenate([s.pop("x0"), spread(s.pop("x_in"), 1)], axis=0)
-            new["x_own"] = rows
-
-        run(f4)
-
-        def f5(s, new):
-            plane(s, new, 3)
-            rows = s.pop("x_own")
-            x_raw = jnp.concatenate([rows, over_core(rows)], axis=0)
-            new["gains"] = s["w", 0][0, :lead].astype(f32)
-            new["x"], new["normed"] = norm_call(outside(x_raw), new["gains"], kernel_index)
-            query, key, value = qkv_call(new["normed"], s["w", 0], lead, s["w", 1], *s["tables"])
-            new["qkv"] = (query, key, value)
-            new["att", 0], new["lse", 0] = attend_call(query, key, value, 0, tensor // 2)
-            new["y0"] = spread(s["cot"], 0)
-
-        run(f5)
-
-        def f6(s, new):
-            plane(s, new, 4)
-            new["att", 1], new["lse", 1] = attend_call(*s["qkv"], tensor // 2, tensor // 2)
-            new["part"] = attention_output_call((s["att", 0], new["att", 1]), s["w", 1], 2 * head_cut)
-            new["y_own"] = jnp.concatenate([s.pop("y0"), spread(s.pop("cot"), 1)], axis=0)
-
-        run(f6)
-
-        def f7(s, new):
-            plane(s, new, 5)
-            part, rows = s.pop("part"), s.pop("y_own")
-            new["middle"], new["normed_two"] = middle_call(
-                s["x"], part, over_core(part), s["gains"]
-            )
-            new["hidden"], new["to_in"], new["to_gate"] = lift_call(
-                new["normed_two"], s["w", 2], s["w", 3]
-            )
-            y_raw = jnp.concatenate([rows, over_core(rows)], axis=0)
-            new["dy"] = order_call(outside(y_raw), kernel_index)
-            made(new, 0, [new["hidden"]], new["dy"])
-
-        def made(new, k, lefts, right, extra=None):
-            grads = weight_gradient_call(lefts, right, tensor, square and aligned, extra)
-            if not square or not aligned:
-                (full,) = grads
-                grads = full.reshape(full.shape[:2] + (chips, -1)).transpose(2, 0, 1, 3)
-            new["g", k] = grads
-
-        def near(s, new, k):
-            if not square:
-                new["f", k] = [b for b in reduce_plane(s.pop(("g", k)))]
-                return
-            mine, x_rest, y_rest, to_x, to_y = s.pop(("g", k))
-            x_got, y_got = over_chip(to_x, 0), over_chip(to_y, 1)
-            new["n", k] = (
-                low_sum(x_rest, y_got[:half]),
-                low_sum(y_rest, x_got[:half]),
-                mine,
-                x_got,
-                y_got,
-            )
-
-        def far(s, new, k):
-            if not square:
-                return
-            x_second, y_second, mine, x_near, y_near = s.pop(("n", k))
-            x_got, y_got = over_chip(x_second, 0), over_chip(y_second, 1)
-            new["f", k] = [
-                low_sum(mine[j], x_near[half + j], y_got[j]) for j in range(half)
-            ] + [low_sum(mine[half + j], y_near[half + j], x_got[j]) for j in range(half)]
-
-        def scatter(s, k):
-            total = lax.psum_scatter(
-                jnp.stack(s.pop(("f", k))), "tensor", scatter_dimension=0, tiled=False
-            )
-            held.append({("sum", k): total})
-
-        def column(s, new, *chunks):
-            blocks = [by_column(s.pop(("f", k)), me_z) for k in chunks]
-            total = reduce_column([jnp.concatenate(b, axis=0) for b in zip(*blocks)])
-            start = 0
-            for k, b in zip(chunks, blocks):
-                new["sum", k] = total[start : start + b[0].shape[0]].astype(bf16)
-                start += b[0].shape[0]
-
-        def trade(s, new, *chunks):
-            sums = [s.pop(("sum", k)) for k in chunks]
-            total = jnp.concatenate(sums, axis=0)
-            mine = jnp.where(first_core, total[:, :block], total[:, block:])
-            got = over_core(jnp.where(first_core, total[:, block:], total[:, :block]))
-            start = 0
-            for k, rows in zip(chunks, [a.shape[0] for a in sums]):
-                a, b = mine[start : start + rows], got[start : start + rows]
-                new["grad", k] = (
-                    jnp.where(first_core, a, b).astype(f32),
-                    jnp.where(first_core, b, a).astype(f32),
-                )
-                start += rows
-
-        run(f7)
-
-        def s1(s, new):
-            near(s, new, 0)
-            g_in, g_gate = hidden_back_call(s["dy"], s["w", 4], s.pop("to_in"), s.pop("to_gate"))
-            new["g_gate"] = g_gate
-            new["part"] = two_part_call(g_in, g_gate, s.pop(("w", 2)), s.pop(("w", 3)))
-            made(new, 1, [g_in], s["normed_two"])
-            new["low_own"], new["low_other"] = lower_call(
-                s.pop("hidden"), s.pop(("w", 4)), s["middle"]
-            )
-
-        run(s1)
-
-        def attention_back(s, new, p):
-            new["dq", p], new["dkv", p] = attend_back_call(
-                *s["qkv"], s["g_att"], s["att", p], s.pop(("lse", p)), *s["tables"],
-                p * (tensor // 2), tensor // 2,
-            )
-
-        def s2(s, new):
-            far(s, new, 0)
-            near(s, new, 1)
-            part = s.pop("part")
-            new["grad_mid"], new["mid_low"], new["gain_two"] = two_back_call(
-                part, over_core(part), s.pop("middle"), s.pop("dy"), s["gains"]
-            )
-            made(new, 2, [s.pop("g_gate")], s.pop("normed_two"))
-            s["g_att"] = new["g_att"] = att_grad_call(new["mid_low"], s["w", 1], 2 * head_cut)
-            attention_back(s, new, 0)
-            new["out"] = outside(
-                output_call(s.pop("low_own"), over_core(s.pop("low_other")), kernel_index)
-            )
-
-        run(s2)
-
-        def s3(s, new):
-            scatter(s, 0)
-            far(s, new, 1)
-            near(s, new, 2)
-            attention_back(s, new, 1)
-            made(new, 3, [s["att", 0], s["att", 1]], s["mid_low"])
-            new["out0"] = collect(s["out"], 0)
-            held.append({"out1": collect(s["out"], 1)})
-
-        run(s3)
-
-        def s4(s, new):
-            scatter(s, 1)
-            far(s, new, 2)
-            near(s, new, 3)
-            made(new, 4, [s["dkv", 0], s["dkv", 1]], s["normed"])
-            new["own"], new["other"] = one_part_call(
-                (s["dq", 0], s["dq", 1]), (s["dkv", 0], s["dkv", 1]), s["w", 0], lead, s["w", 1]
-            )
-
-        run(s4)
-
-        def s5(s, new):
-            scatter(s, 2)
-            far(s, new, 3)
-            near(s, new, 4)
-            dx, gain_grads = one_back_call(
-                s.pop("own"), over_core(s.pop("other")), s.pop("x"), s.pop("grad_mid"), s["gains"],
-                s.pop("gain_two"), kernel_index,
-            )
-            new["dx"] = outside(dx)
-            made(new, 5, [s["dq", 0], s["dq", 1]], s["normed"], gain_grads)
-
-        run(s5)
-
-        def s6(s, new):
-            far(s, new, 4)
-            near(s, new, 5)
-            column(s, new, 3)
-            held.append({"dx0": collect(s["dx"], 0), "dx1": collect(s["dx"], 1)})
-
-        run(s6)
-
-        def s7(s, new):
-            far(s, new, 5)
-            column(s, new, 4)
-            trade(s, new, 0, 1, 2, 3)
-
-        run(s7)
-
-        def s8(s, new):
-            column(s, new, 5)
-
-        run(s8)
-
-        def s9(s, new):
-            trade(s, new, 4, 5)
-
-        run(s9)
-
-        layer_output = assemble(state["out0"], state["out1"])
-        input_gradient = assemble(state["dx0"], state["dx1"])
-        def joined(k, rows):
-            return jnp.concatenate(state["grad", k], axis=0)[:rows]
-
-        grad_down, grad_up, grad_gate = (joined(k, hidden_local) for k in range(3))
-        grad_out = joined(3, head_columns)
-        key_value = [g.reshape(2, head_cut, block) for g in state["grad", 4]]
-        query = [g[lead:] for g in state["grad", 5]]
-        grad_qkv = jnp.stack(
-            [jnp.concatenate(query, axis=0)]
-            + [jnp.concatenate([g[i] for g in key_value], axis=0) for i in range(2)]
-        ).transpose(2, 0, 1)
-        gain_total = sum(g[:2] for g in state["grad", 5])
-        grad_expand = jnp.stack([grad_up, grad_gate]).transpose(2, 0, 1)
         step_rates = (
             2.5 * D ** (-0.5),
             2.5 * max(1, 4 * H * DH // SEQ) ** (-0.5),
@@ -1103,22 +1009,283 @@
             2.5 * FF ** (-0.5),
             0.25,
         )
-        grad_qkv, grad_out, grad_expand, grad_down = lax.optimization_barrier(
-            (grad_qkv, grad_out.T, grad_expand, grad_down.T)
-        )
+
+        def joined(s, k, rows):
+            return jnp.concatenate(s[GRAD, k], axis=0)[:rows]
+
+        def joined_heads(s):
+            key_value = [g.reshape(2, head_cut, block) for g in s[GRAD, 4]]
+            query = [g[lead:] for g in s[GRAD, 5]]
+            grads = jnp.stack(
+                [jnp.concatenate(query, axis=0)]
+                + [jnp.concatenate([g[i] for g in key_value], axis=0) for i in range(2)]
+            )
+            return lax.optimization_barrier(grads.transpose(2, 0, 1))
+
+        def first_updates(s):
+            grad_down, grad_up, grad_gate = (joined(s, k, hidden_local) for k in range(3))
+            grad_expand = jnp.stack([grad_up, grad_gate]).transpose(2, 0, 1)
+            grad_out, grad_expand, grad_down = lax.optimization_barrier(
+                (joined(s, 3, head_columns).T, grad_expand, grad_down.T)
+            )
+            return (
+                adamw_update(
+                    attention_out, attention_out_first, attention_out_second, grad_out, step_rates[1]
+                ),
+                adamw_update(expand_weight, expand_first, expand_second, grad_expand, step_rates[2]),
+                adamw_update(
+                    contract_weight, contract_first, contract_second, grad_down, step_rates[3]
+                ),
+            )
+
+        def f0(s, new):
+            pair = s.pop(BOTH)
+            mine = jnp.where(first_core, pair[0], pair[1])
+            got = over_core(jnp.where(first_core, pair[1], pair[0]))
+            new[LOW] = side_by_side(mine, got)
+
+        run(f0)
+
+        def f1(s, new):
+            column_a(s, new, 0)
+
+        run(f1)
+
+        def f2(s, new):
+            column_b(s, new, 0)
+            column_a(s, new, 1)
+
+        run(f2)
+
+        def f3(s, new):
+            column_c(s, new, 0)
+            column_b(s, new, 1)
+            column_a(s, new, 2)
+            new[TABLES] = rotary_tables()
+
+        run(f3)
+
+        def f4(s, new):
+            plane(s, new, 0)
+            column_c(s, new, 1)
+            column_b(s, new, 2)
+            column_a(s, new, 3)
+
+        run(f4)
+
+        def f5(s, new):
+            plane(s, new, 1)
+            column_c(s, new, 2)
+            column_b(s, new, 3)
+            new[X0] = spread(s[X_IN], 0)
+
+        run(f5)
+
+        def f6(s, new):
+            plane(s, new, 2)
+            column_c(s, new, 3)
+            new[X_OWN] = jnp.concatenate([s.pop(X0), spread(s.pop(X_IN), 1)], axis=0)
+
+        run(f6)
+
+        def f7(s, new):
+            plane(s, new, 3)
+            rows = s.pop(X_OWN)
+            x_raw = jnp.concatenate([rows, over_core(rows, 2)], axis=0)
+            new[GAINS] = s[W, 0][0, :lead].astype(f32)
+            new[X], new[NORMED] = norm_call(outside(x_raw), new[GAINS], kernel_index)
+            query, key, value = qkv_call(new[NORMED], s[W, 0], lead, s[W, 1], *s[TABLES])
+            new[QKV] = (query, key, value)
+            new[ATT, 0], new[LSE, 0] = attend_call(query, key, value, 0, tensor // 2)
+            new[Y0] = spread(s[COT], 0)
+
+        run(f7)
+
+        def f8(s, new):
+            plane(s, new, 4)
+            new[ATT, 1], new[LSE, 1] = attend_call(*s[QKV], tensor // 2, tensor // 2)
+            new[PART] = attention_output_call((s[ATT, 0], new[ATT, 1]), s[W, 1], 2 * head_cut)
+            new[Y_OWN] = jnp.concatenate([s.pop(Y0), spread(s.pop(COT), 1)], axis=0)
+
+        run(f8)
+
+        def f9(s, new):
+            plane(s, new, 5)
+            part, rows = s.pop(PART), s.pop(Y_OWN)
+            new[MIDDLE], new[NORMED_TWO] = middle_call(
+                s[X], part, over_core(part, 4), s[GAINS]
+            )
+            new[HIDDEN], new[TO_IN], new[TO_GATE] = lift_call(
+                new[NORMED_TWO], s[W, 2], s[W, 3]
+            )
+            y_raw = jnp.concatenate([rows, over_core(rows)], axis=0)
+            new[DY] = order_call(outside(y_raw), kernel_index)
+            made(new, 0, [new[HIDDEN]], new[DY])
+
+        def made(new, k, lefts, right, extra=None):
+            grads = weight_gradient_call(lefts, right, tensor, square and aligned, extra)
+            if not square or not aligned:
+                (full,) = grads
+                grads = full.reshape(full.shape[:2] + (chips, -1)).transpose(2, 0, 1, 3)
+            new[G, k] = grads
+
+        def plane_back(s, new, k):
+            if not square:
+                if (G, k) in s:
+                    new[F, k] = [b for b in reduce_plane(s.pop((G, k)))]
+                return
+            flat = lambda a: a.reshape(-1, a.shape[-1])
+            to_x, to_y, rows = [], [], 0
+            if (G, k) in s:
+                mine, x_rest, y_rest, x_out, y_out = s.pop((G, k))
+                rows = x_out.shape[0] * x_out.shape[1]
+                to_x.append(flat(x_out))
+                to_y.append(flat(y_out))
+            if (N, k - 1) in s:
+                x_last, y_last, mine_last, x_near, y_near = s.pop((N, k - 1))
+                to_x.append(flat(x_last))
+                to_y.append(flat(y_last))
+            x_got = over_chip(jnp.concatenate(to_x, axis=0), 0)
+            y_got = over_chip(jnp.concatenate(to_y, axis=0), 1)
+            first = (mine, x_rest, y_rest) if rows else None
+            second = (mine_last, x_near, y_near) if len(to_x) > 1 or not rows else None
+            near, far = combine_call(first, second, x_got, y_got, rows)
+            if first is not None:
+                new[N, k] = (*near, mine, x_got, y_got)
+            if second is not None:
+                new[F, k - 1] = far
+
+        def whole_blocks(blocks):
+            return blocks if square else jnp.stack(blocks)
+
+        def scatter(s, k):
+            total = lax.psum_scatter(
+                whole_blocks(s.pop((F, k))), "tensor", scatter_dimension=0, tiled=False
+            )
+            held.append({(SUM, k): total})
+
+        def column(s, new, *chunks):
+            blocks = [by_column(s.pop((F, k)), me_z) for k in chunks]
+            total = reduce_column([jnp.concatenate(b, axis=0) for b in zip(*blocks)])
+            start = 0
+            for k, b in zip(chunks, blocks):
+                new[SUM, k] = total[start : start + b[0].shape[0]].astype(bf16)
+                start += b[0].shape[0]
+
+        def trade(s, new, *chunks):
+            sums = [s.pop((SUM, k)) for k in chunks]
+            total = jnp.concatenate(sums, axis=0)
+            mine = jnp.where(first_core, total[:, :block], total[:, block:])
+            got = over_core(jnp.where(first_core, total[:, block:], total[:, :block]))
+            start = 0
+            for k, rows in zip(chunks, [a.shape[0] for a in sums]):
+                a, b = mine[start : start + rows], got[start : start + rows]
+                new[GRAD, k] = (
+                    jnp.where(first_core, a, b).astype(f32),
+                    jnp.where(first_core, b, a).astype(f32),
+                )
+                start += rows
+
+        run(f9)
+
+        def s1(s, new):
+            plane_back(s, new, 0)
+            own, other = lower_call(s.pop(HIDDEN), s[W, 4], s[MIDDLE])
+            g_in, g_gate = hidden_back_call(
+                s[DY], s.pop((W, 4)), s.pop(TO_IN), s.pop(TO_GATE)
+            )
+            new[G_GATE] = g_gate
+            new[PART] = two_part_call(g_in, g_gate, s.pop((W, 2)), s.pop((W, 3)))
+            made(new, 1, [g_in], s[NORMED_TWO])
+            new[OUT] = outside(output_call(own, over_core(other), kernel_index))
+
+        run(s1)
+
+        def attention_back(s, new, p):
+            new[DQ, p], new[DKV, p] = attend_back_call(
+                *s[QKV], s[G_ATT], s[ATT, p], s.pop((LSE, p)), *s[TABLES],
+                p * (tensor // 2), tensor // 2,
+            )
+
+        def s2(s, new):
+            plane_back(s, new, 1)
+            part = s.pop(PART)
+            new[GRAD_MID], new[MID_LOW], new[GAIN_TWO] = two_back_call(
+                part, over_core(part, 4), s.pop(MIDDLE), s.pop(DY), s[GAINS]
+            )
+            made(new, 2, [s.pop(G_GATE)], s.pop(NORMED_TWO))
+            s[G_ATT] = new[G_ATT] = att_grad_call(new[MID_LOW], s[W, 1], 2 * head_cut)
+            attention_back(s, new, 0)
+            new[OUT1] = collect(s[OUT], 1)
+
+        run(s2)
+
+        def s3(s, new):
+            scatter(s, 0)
+            plane_back(s, new, 2)
+            attention_back(s, new, 1)
+            made(new, 3, [s[ATT, 0], s[ATT, 1]], s[MID_LOW])
+            new[OWN], new[OTHER] = one_part_call(
+                (s[DQ, 0], new[DQ, 1]), (s[DKV, 0], new[DKV, 1]), s[W, 0], lead, s[W, 1]
+            )
+            new[OUT0] = collect(s[OUT], 0)
+
+        run(s3)
+
+        def s4(s, new):
+            scatter(s, 1)
+            plane_back(s, new, 3)
+            dx, new[GAIN_GRADS] = one_back_call(
+                s.pop(OWN), over_core(s.pop(OTHER), 2), s.pop(X), s.pop(GRAD_MID),
+                s[GAINS], s.pop(GAIN_TWO), kernel_index,
+            )
+            new[DX] = outside(dx)
+            made(new, 4, [s[DKV, 0], s[DKV, 1]], s[NORMED])
+            new[DX1] = collect(new[DX], 1)
+
+        run(s4)
+
+        def s5(s, new):
+            scatter(s, 2)
+            plane_back(s, new, 4)
+            made(new, 5, [s[DQ, 0], s[DQ, 1]], s[NORMED], s.pop(GAIN_GRADS))
+            new[DX0] = collect(s[DX], 0)
+
+        run(s5)
+
+        def s6(s, new):
+            plane_back(s, new, 5)
+            column(s, new, 3)
+
+        run(s6)
+
+        def s7(s, new):
+            plane_back(s, new, 6)
+            column(s, new, 4)
+            trade(s, new, 0, 1, 2, 3)
+
+        run(s7)
+
+        def s8(s, new):
+            column(s, new, 5)
+            new[UPDATED] = first_updates(s)
+
+        run(s8)
+
+        def s9(s, new):
+            trade(s, new, 4, 5)
+
+        run(s9)
+
+        layer_output = assemble(state[OUT0], state[OUT1])
+        input_gradient = assemble(state[DX0], state[DX1])
+        grad_qkv = joined_heads(state)
+        gain_total = sum(g[:2] for g in state[GRAD, 5])
         qkv_new = adamw_update(
             attention_in, attention_in_first, attention_in_second, grad_qkv, step_rates[0]
         )
-        out_new = adamw_update(
-            attention_out, attention_out_first, attention_out_second, grad_out, step_rates[1]
-        )
-        expand_new = adamw_update(
-            expand_weight, expand_first, expand_second, grad_expand, step_rates[2]
-        )
-        contract_new = adamw_update(
-            contract_weight, contract_first, contract_second, grad_down, step_rates[3]
-        )
         gains_new = adamw_update(norm_gains, gains_first, gains_second, gain_total, step_rates[4])
+        out_new, expand_new, contract_new = state[UPDATED]
         return (
             layer_output,
             input_gradient,

time: 476 us -> 440 us (0.924)
  waiting for transfers between devices: 126 us -> 87.4 us
  starting transfers between devices: 92.6 us -> 120 us
  other arithmetic: 59.7 us -> 39.1 us
  local copies, waits for them, and re-layouts: 62.8 us -> 44.3 us
  Pallas kernels: 109 us -> 125 us
    ppermute x81 -> x72, waiting for transfers between devices: 126 us -> 87.3 us  [permute(): return lax.ppermute(value, AXES, pairs)]
    ppermute x81 -> x72, starting transfers between devices: 92.4 us -> 120 us  [permute(): return lax.ppermute(value, AXES, pairs)]
    convert_element_type x23 -> x5, other arithmetic: 23.2 us -> 0.29 us  [the longest x3 0.27 us: column(): new[SUM, k] = total[start:start + b[0].shape[0]].astype(bf16)]
    slice x29 -> x8, local copies, waits for them, and re-layouts: 10.8 us -> 0.09 us  [the longest x4 0.06 us: column_a(): new[PAIR, k] = gather_near_z(s[LOW][starts[k]:stop], me_z)]
    concatenate x16 -> x20, other arithmetic: 7.24 us -> 16.4 us  [the longest x5 6.07 us: plane_back(): y_got = over_chip(jnp.concatenate(to_y, axis=0), 1)]
    pallas_call x0 -> x12, Pallas kernels: none -> 6.92 us  [the longest x7 5.21 us: combine_call(): call(kernel, 'gradient_sums', (1,), [whole(a) for a in (x_got, y_got, *op...]
    unnamed x285 -> x251, local copies, waits for them, and re-layouts: 43.8 us -> 37.7 us
  transfers between devices with their start and end apart: 85 -> 75, of which waited for: 26 -> 28; matrix products, arithmetic and copies ran while one was open for 12% -> 9% of each run, Pallas kernels for 20% -> 26%
where the time goes in v3:
time: 440 us; the launch traced here: 432 us
  Pallas kernels  125 us (28%)
  starting transfers between devices  120 us (27%)
  waiting for transfers between devices  87.4 us (20%)
  local copies, waits for them, and re-layouts  44.3 us (10%)
  other arithmetic  39.1 us (9%)
  between operations  16.2 us (4%)
    ppermute x72, starting transfers between devices, permute(): return lax.ppermute(value, AXES, pairs)  120 us
    ppermute x72, waiting for transfers between devices, permute(): return lax.ppermute(value, AXES, pairs)  87.3 us
    unnamed x251, local copies, waits for them, and re-layouts  37.7 us
    pallas_call x2, Pallas kernels, attend_back_call(): call(kernel, 'attention_backward', (count, 2), [half, full, full, half, o...  29.6 us
    pallas_call x6, Pallas kernels, weight_gradient_call(): call(kernel, 'weight_gradient', (1,), [whole(a) for a in (*lefts, right,...  19.7 us
    pallas_call x2, Pallas kernels, attend_call(): call(kernel, 'attention_forward', (count, 2), [half, full, full], [out_ha...  16.8 us
  transfers between devices with their start and end apart: 75, of which 28 were waited for; matrix products, arithmetic and copies ran while one was open for 9% of the time, Pallas kernels for 26%

profile of v3, /device:TPU:0, one launch (start us, length us, event | category | flops | bytes accessed | tf_op | source)
XLA Modules:
  0.0 431.6 jit_solution(16029332611040701584)
XLA Ops:
  29.7 5.3 %collective-permute-start.6 = (bf16[336,256]{1,0:T(8,128)(2,1)S(1)}, bf16[336,256]{1,0:T(8,128)(2,1)S(1)}, u32[]{:S(2)}, u32[]{:S(2)}) collective-permute-start(bf16[336,256]{1,0:T(8,128)(2,1)S(1)} %slice.248), channel_id=1, source_target_pairs={{0,1},{1,0},{2,3},{3,2},{4,5},{5,4},{6,7},{7,6},{8,9},{9,8},{10,11... | collective-permute-start | bytes 516104 | tf_op jit(solution)/shard_map/ppermute | solution.py:792
  38.6 7.4 %collective-permute-start.11 = (bf16[672,256]{1,0:T(8,128)(2,1)S(1)}, bf16[672,256]{1,0:T(8,128)(2,1)S(1)}, u32[]{:S(2)}, u32[]{:S(2)}) collective-permute-start(bf16[672,256]{1,0:T(8,128)(2,1)S(1)} %slice.249), channel_id=1, source_target_pairs={{0,1},{1,0},{2,3},{3,2},{4,5},{5,4},{6,7},{7,6},{8,9},{9,8},{10,11... | collective-permute-start | bytes 1032200 | tf_op jit(solution)/shard_map/ppermute | solution.py:792
  68.8 5.4 %collective-permute-start.16 = (bf16[256,1024]{1,0:T(8,128)(2,1)}, bf16[256,1024]{1,0:T(8,128)(2,1)}, u32[]{:S(2)}, u32[]{:S(2)}) collective-permute-start(bf16[256,1024]{1,0:T(8,128)(2,1)} %dynamic-slice_bitcast_fusion.3), channel_id=1, source_target_pairs={{0,0},{1,4},{2,2},{3,6},{4,1},{5,5},{6,3},{7,7},{8,8},{9,12},{10,1... | collective-permute-start | bytes 1572872 | tf_op jit(solution)/shard_map/ppermute | solution.py:792
  75.8 5.4 %collective-permute-done.12.x_far_ref.x_ref = bf16[1824,256]{1,0:T(8,128)(2,1)S(1)} collective-permute-done((bf16[1824,256]{1,0:T(8,128)(2,1)}, bf16[1824,256]{1,0:T(8,128)(2,1)S(1)}, u32[]{:S(2)}, u32[]{:S(2)}) %collective-permute-start.12) | collective-permute-done | bytes 933920 | tf_op jit(solution)/shard_map/ppermute | solution.py:792
  83.7 12.2 %collective-permute-start.20 = (bf16[256,1024]{1,0:T(8,128)(2,1)}, bf16[256,1024]{1,0:T(8,128)(2,1)}, u32[]{:S(2)}, u32[]{:S(2)}) collective-permute-start(bf16[256,1024]{1,0:T(8,128)(2,1)} %dynamic-slice_bitcast_fusion.2), channel_id=1, source_target_pairs={{0,2},{1,6},{2,0},{3,4},{4,3},{5,7},{6,1},{7,5},{8,10},{9,14},{10,... | collective-permute-start | bytes 1572872 | tf_op jit(solution)/shard_map/ppermute | solution.py:792
  98.9 8.2 %collective-permute-done.20 = bf16[256,1024]{1,0:T(8,128)(2,1)} collective-permute-done((bf16[256,1024]{1,0:T(8,128)(2,1)}, bf16[256,1024]{1,0:T(8,128)(2,1)}, u32[]{:S(2)}, u32[]{:S(2)}) %collective-permute-start.20) | collective-permute-done | bytes 524320 | tf_op jit(solution)/shard_map/ppermute | solution.py:792
  108.4 7.0 %collective-permute-done.19 = bf16[2,672,256]{2,1,0:T(8,128)(2,1)} collective-permute-done((bf16[2,672,256]{2,1,0:T(8,128)(2,1)}, bf16[2,672,256]{2,1,0:T(8,128)(2,1)}, u32[]{:S(2)}, u32[]{:S(2)}) %collective-permute-start.19) | collective-permute-done | bytes 688160 | tf_op jit(solution)/shard_map/ppermute | solution.py:792
  128.6 6.5 %qkv_projection.1 = (bf16[4,1024,128]{2,1,0:T(8,128)(2,1)S(1)}, bf16[4,1024,128]{2,1,0:T(8,128)(2,1)S(1)}, bf16[4,1024,128]{2,1,0:T(8,128)(2,1)S(1)}) custom-call(bf16[1024,1024]{1,0:T(8,128)(2,1)S(1)} %get-tuple-element.677.x_ref.refs_2_, bf16[4,144,1024]{2,1,0:T(8,128)(2,1)S(1)} %copy-done.32, ...), custom_call_target="tpu_custom_call" | custom-call | flops 2100000000 | bytes 7200000 | tf_op jit(solution)/shard_map/qkv_projection/pallas_call | solution.py:195
  135.2 8.4 %attention_forward.2 = (bf16[2,1024,128]{2,1,0:T(8,128)(2,1)S(1)}, f32[2,2,1024]{2,1,0:T(2,128)S(1)}) custom-call(bf16[4,1024,128]{2,1,0:T(8,128)(2,1)S(1)} %get-tuple-element.607.q_ref, bf16[4,1024,128]{2,1,0:T(8,128)(2,1)S(1)} %get-tuple-element.608.k_ref, bf16[4,1024,128]{2,1,0:T(8,128)(2,1)S(1)} %get-tuple-element.609.v_ref), custom_call_target="tpu_custom_call" | custom-call | flops 3150000128 | bytes 10800000 | tf_op jit(solution)/shard_map/attention_forward/pallas_call | solution.py:266
  150.8 9.6 %collective-permute-start.28 = (bf16[256,1024]{1,0:T(8,128)(2,1)S(1)}, bf16[256,1024]{1,0:T(8,128)(2,1)S(1)}, u32[]{:S(2)}, u32[]{:S(2)}) collective-permute-start(bf16[256,1024]{1,0:T(8,128)(2,1)S(1)} %dynamic-slice_bitcast_fusion), channel_id=1, source_target_pairs={{0,2},{1,6},{2,0},{3,4},{4,3},{5,7},{6,1},{7,5},{8,10},{9,14},{10,... | collective-permute-start | bytes 1572872 | tf_op jit(solution)/shard_map/ppermute | solution.py:792
  160.4 8.4 %attention_forward.3 = (bf16[2,1024,128]{2,1,0:T(8,128)(2,1)S(1)}, f32[2,2,1024]{2,1,0:T(2,128)S(1)}) custom-call(bf16[4,1024,128]{2,1,0:T(8,128)(2,1)S(1)} %get-tuple-element.607.q_ref, bf16[4,1024,128]{2,1,0:T(8,128)(2,1)S(1)} %get-tuple-element.608.k_ref, bf16[4,1024,128]{2,1,0:T(8,128)(2,1)S(1)} %get-tuple-element.609.v_ref), custom_call_target="tpu_custom_call" | custom-call | flops 3150000128 | bytes 10800000 | tf_op jit(solution)/shard_map/attention_forward/pallas_call | solution.py:266
  170.4 6.0 %collective-permute-done.28 = bf16[256,1024]{1,0:T(8,128)(2,1)S(1)} collective-permute-done((bf16[256,1024]{1,0:T(8,128)(2,1)S(1)}, bf16[256,1024]{1,0:T(8,128)(2,1)S(1)}, u32[]{:S(2)}, u32[]{:S(2)}) %collective-permute-start.28) | collective-permute-done | bytes 524320 | tf_op jit(solution)/shard_map/ppermute | solution.py:792
  179.3 4.9 %collective-permute-done.29.x_far_ref = bf16[672,256]{1,0:T(8,128)(2,1)S(1)} collective-permute-done((bf16[672,256]{1,0:T(8,128)(2,1)S(1)}, bf16[672,256]{1,0:T(8,128)(2,1)S(1)}, u32[]{:S(2)}, u32[]{:S(2)}) %collective-permute-start.29) | collective-permute-done | bytes 344096 | tf_op jit(solution)/shard_map/ppermute | solution.py:792
  188.2 7.1 %expand.1 = (bf16[1024,1344]{1,0:T(8,128)(2,1)S(1)}, bf16[1024,1344]{1,0:T(8,128)(2,1)S(1)}, bf16[1024,1344]{1,0:T(8,128)(2,1)S(1)}) custom-call(bf16[1024,1024]{1,0:T(8,128)(2,1)S(1)} %get-tuple-element.591.x_ref.refs_1_, bf16[4,336,1024]{2,1,0:T(8,128)(2,1)S(1)} %gathered_weight.7.up_ref, bf16[4,336,1024]{2,1,0:T(8,128)(2,1)S(1)} %gathered_weight.8.gate_ref.w_gate_ref), custom_call_target="tpu_custom_call" | custom-call | flops 4200000000 | bytes 14400000 | tf_op jit(solution)/shard_map/expand/pallas_call | solution.py:409
  200.7 4.9 %contract.1 = (f32[512,1024]{1,0:T(8,128)S(1)}, bf16[512,1024]{1,0:T(8,128)(2,1)}) custom-call(bf16[1024,1344]{1,0:T(8,128)(2,1)S(1)} %get-tuple-element.554.refs_0_.hid_ref, bf16[4,336,1024]{2,1,0:T(8,128)(2,1)S(1)} %gathered_weight.9.w_ref, f32[1024,1024]{1,0:T(8,128)S(1)} %get-tuple-element.572.mid_ref), custom_call_target="tpu_custom_call" | custom-call | flops 1750000000 | bytes 6000000 | tf_op jit(solution)/shard_map/contract/pallas_call | solution.py:434
  215.2 6.8 %grad_normed_two.1.part_ref = bf16[1024,1024]{1,0:T(8,128)(2,1)S(1)} custom-call(bf16[1024,1344]{1,0:T(8,128)(2,1)S(1)} %get-tuple-element.546.in_ref.refs_0_, bf16[1024,1344]{1,0:T(8,128)(2,1)S(1)} %get-tuple-element.590.gate_ref.refs_0_, bf16[4,336,1024]{2,1,0:T(8,128)(2,1)S(1)} %gathered_weight.7.up_ref, ...), custom_call_target="tpu_custom_call" | custom-call | flops 2800000000 | bytes 9600000 | tf_op jit(solution)/shard_map/grad_normed_two/pallas_call | solution.py:592
  233.3 9.5 %collective-permute-start.45 = (bf16[256,1024]{1,0:T(8,128)(2,1)S(1)}, bf16[256,1024]{1,0:T(8,128)(2,1)S(1)}, u32[]{:S(2)}, u32[]{:S(2)}) collective-permute-start(bf16[256,1024]{1,0:T(8,128)(2,1)S(1)} %slice.273), channel_id=1, source_target_pairs={{2,0},{6,1},{0,2},{4,3},{3,4},{7,5},{1,6},{5,7},{10,8},{14,9},{8,1... | collective-permute-start | bytes 1572872 | tf_op jit(solution)/shard_map/ppermute | solution.py:792
  249.6 14.7 %attention_backward.2 = (bf16[2,1024,128]{2,1,0:T(8,128)(2,1)S(1)}, bf16[2,1024,256]{2,1,0:T(8,128)(2,1)S(1)}) custom-call(bf16[4,1024,128]{2,1,0:T(8,128)(2,1)} %copy-done.66, bf16[4,1024,128]{2,1,0:T(8,128)(2,1)} %copy-done.67, bf16[4,1024,128]{2,1,0:T(8,128)(2,1)} %copy-done.68, bf16[4,1024,128]{2,1,0:T(8,128)(2,1)} %copy-done.33, ...), custom_call_target="tpu_custom_call" | custom-call | flops 4899999744 | bytes 16800000 | tf_op jit(solution)/shard_map/attention_backward/pallas_call | solution.py:324
  274.1 5.4 %collective-permute-start.48 = (bf16[256,1024]{1,0:T(8,128)(2,1)}, bf16[256,1024]{1,0:T(8,128)(2,1)}, u32[]{:S(2)}, u32[]{:S(2)}) collective-permute-start(bf16[256,1024]{1,0:T(8,128)(2,1)} %slice.274), channel_id=1, source_target_pairs={{0,0},{4,1},{2,2},{6,3},{1,4},{5,5},{3,6},{7,7},{8,8},{12,9},{10,1... | collective-permute-start | bytes 1572872 | tf_op jit(solution)/shard_map/ppermute | solution.py:792
  279.6 14.9 %attention_backward.3 = (bf16[2,1024,128]{2,1,0:T(8,128)(2,1)S(1)}, bf16[2,1024,256]{2,1,0:T(8,128)(2,1)S(1)}) custom-call(bf16[4,1024,128]{2,1,0:T(8,128)(2,1)} %copy-done.66, bf16[4,1024,128]{2,1,0:T(8,128)(2,1)} %copy-done.67, bf16[4,1024,128]{2,1,0:T(8,128)(2,1)} %copy-done.68, bf16[4,1024,128]{2,1,0:T(8,128)(2,1)} %copy-done.33, ...), custom_call_target="tpu_custom_call" | custom-call | flops 4899999744 | bytes 16800000 | tf_op jit(solution)/shard_map/attention_backward/pallas_call | solution.py:324
  296.2 6.7 %grad_normed_one.1 = (f32[512,1024]{1,0:T(8,128)S(1)}, bf16[512,1024]{1,0:T(8,128)(2,1)S(1)}) custom-call(bf16[2,1024,128]{2,1,0:T(8,128)(2,1)} %copy-done.73, bf16[2,1024,128]{2,1,0:T(8,128)(2,1)} %copy-done.75, bf16[2,1024,256]{2,1,0:T(8,128)(2,1)} %copy-done.69, bf16[2,1024,256]{2,1,0:T(8,128)(2,1)} %copy-done.71, bf16[4,144,1024]{2,1,0:T(8,128)(2,1)} %copy-done.31, ...), custom_call_target="tpu_custom_call" | custom-call | flops 2100000000 | bytes 7200000 | tf_op jit(solution)/shard_map/grad_normed_one/pallas_call | solution.py:683
  331.2 18.7 %collective-permute-done.53 = bf16[256,1024]{1,0:T(8,128)(2,1)} collective-permute-done((bf16[256,1024]{1,0:T(8,128)(2,1)}, bf16[256,1024]{1,0:T(8,128)(2,1)}, u32[]{:S(2)}, u32[]{:S(2)}) %collective-permute-start.53) | collective-permute-done | bytes 524320 | tf_op jit(solution)/shard_map/ppermute | solution.py:792
  356.6 5.5 %collective-permute-start.56 = (bf16[256,1024]{1,0:T(8,128)(2,1)}, bf16[256,1024]{1,0:T(8,128)(2,1)}, u32[]{:S(2)}, u32[]{:S(2)}) collective-permute-start(bf16[256,1024]{1,0:T(8,128)(2,1)} %slice.278), channel_id=1, source_target_pairs={{0,0},{4,1},{2,2},{6,3},{1,4},{5,5},{3,6},{7,7},{8,8},{12,9},{10,1... | collective-permute-start | bytes 1572872 | tf_op jit(solution)/shard_map/ppermute | solution.py:792
  398.0 4.2 collective-permute-done.65
  (543 shorter events, 222.3 us)
Async XLA Ops:
  7.2 324.0 %reduce-scatter.4.cloned.1.call-start = ((), (), s32[]{:S(2)}) async-start(), calls=%async_computation.3 | async-start | bytes 860160 | tf_op jit(solution)/shard_map/reduce_scatter | solution.py:1162
  62.1 19.1 %collective-permute-start.12 = (bf16[1824,256]{1,0:T(8,128)(2,1)}, bf16[1824,256]{1,0:T(8,128)(2,1)S(1)}, u32[]{:S(2)}, u32[]{:S(2)}) collective-permute-start(bf16[1824,256]{1,0:T(8,128)(2,1)} %get-tuple-element.873), channel_id=1, source_target_pairs={{0,8},{1,9},{2,10},{3,11},{4,12},{5,13},{6,14},{7,15},{8,0},{9,1},... | collective-permute-start | bytes 2801672 | tf_op jit(solution)/shard_map/ppermute | solution.py:792
  63.6 18.8 %collective-permute-start.13 = (bf16[1824,256]{1,0:T(8,128)(2,1)}, bf16[1824,256]{1,0:T(8,128)(2,1)S(1)}, u32[]{:S(2)}, u32[]{:S(2)}) collective-permute-start(bf16[1824,256]{1,0:T(8,128)(2,1)} %get-tuple-element.872), channel_id=1, source_target_pairs={{0,16},{1,17},{2,18},{3,19},{4,20},{5,21},{6,22},{7,23},{8,24},{9,... | collective-permute-start | bytes 2801672 | tf_op jit(solution)/shard_map/ppermute | solution.py:792
  83.7 23.4 %collective-permute-start.20 = (bf16[256,1024]{1,0:T(8,128)(2,1)}, bf16[256,1024]{1,0:T(8,128)(2,1)}, u32[]{:S(2)}, u32[]{:S(2)}) collective-permute-start(bf16[256,1024]{1,0:T(8,128)(2,1)} %dynamic-slice_bitcast_fusion.2), channel_id=1, source_target_pairs={{0,2},{1,6},{2,0},{3,4},{4,3},{5,7},{6,1},{7,5},{8,10},{9,14},{10,... | collective-permute-start | bytes 1572872 | tf_op jit(solution)/shard_map/ppermute | solution.py:792
  95.9 19.5 %collective-permute-start.19 = (bf16[2,672,256]{2,1,0:T(8,128)(2,1)}, bf16[2,672,256]{2,1,0:T(8,128)(2,1)}, u32[]{:S(2)}, u32[]{:S(2)}) collective-permute-start(bf16[2,672,256]{2,1,0:T(8,128)(2,1)} %collective-permute-done.15), channel_id=1, source_target_pairs={{1,0},{2,3},{5,4},{6,7},{9,8},{10,11},{13,12},{14,15},{17,16},{18,... | collective-permute-start | bytes 2064392 | tf_op jit(solution)/shard_map/ppermute | solution.py:792
  98.4 18.6 %collective-permute-start.17 = (bf16[2112,256]{1,0:T(8,128)(2,1)}, bf16[2112,256]{1,0:T(8,128)(2,1)S(1)}, u32[]{:S(2)}, u32[]{:S(2)}) collective-permute-start(bf16[2112,256]{1,0:T(8,128)(2,1)} %get-tuple-element.879), channel_id=1, source_target_pairs={{0,8},{1,9},{2,10},{3,11},{4,12},{5,13},{6,14},{7,15},{8,0},{9,1},... | collective-permute-start | bytes 3244040 | tf_op jit(solution)/shard_map/ppermute | solution.py:792
  98.9 19.0 %collective-permute-start.18 = (bf16[2112,256]{1,0:T(8,128)(2,1)S(1)}, bf16[2112,256]{1,0:T(8,128)(2,1)S(1)}, u32[]{:S(2)}, u32[]{:S(2)}) collective-permute-start(bf16[2112,256]{1,0:T(8,128)(2,1)S(1)} %get-tuple-element.878), channel_id=1, source_target_pairs={{0,16},{1,17},{2,18},{3,19},{4,20},{5,21},{6,22},{7,23},{8,24},{9,... | collective-permute-start | bytes 3244040 | tf_op jit(solution)/shard_map/ppermute | solution.py:792
  123.7 24.0 %collective-permute-start.21 = (bf16[2016,256]{1,0:T(8,128)(2,1)S(1)}, bf16[2016,256]{1,0:T(8,128)(2,1)S(1)}, u32[]{:S(2)}, u32[]{:S(2)}) collective-permute-start(bf16[2016,256]{1,0:T(8,128)(2,1)S(1)} %get-tuple-element.877), channel_id=1, source_target_pairs={{0,8},{1,9},{2,10},{3,11},{4,12},{5,13},{6,14},{7,15},{8,0},{9,1},... | collective-permute-start | bytes 3096584 | tf_op jit(solution)/shard_map/ppermute | solution.py:792
  124.3 23.6 %collective-permute-start.22 = (bf16[2016,256]{1,0:T(8,128)(2,1)S(1)}, bf16[2016,256]{1,0:T(8,128)(2,1)S(1)}, u32[]{:S(2)}, u32[]{:S(2)}) collective-permute-start(bf16[2016,256]{1,0:T(8,128)(2,1)S(1)} %get-tuple-element.876), channel_id=1, source_target_pairs={{0,16},{1,17},{2,18},{3,19},{4,20},{5,21},{6,22},{7,23},{8,24},{9,... | collective-permute-start | bytes 3096584 | tf_op jit(solution)/shard_map/ppermute | solution.py:792
  125.1 23.1 %collective-permute-start.25 = (bf16[256,1024]{1,0:T(8,128)(2,1)S(1)}, bf16[256,1024]{1,0:T(8,128)(2,1)S(1)}, u32[]{:S(2)}, u32[]{:S(2)}) collective-permute-start(bf16[256,1024]{1,0:T(8,128)(2,1)S(1)} %dynamic-slice_bitcast_fusion.1), channel_id=1, source_target_pairs={{0,0},{1,4},{2,2},{3,6},{4,1},{5,5},{6,3},{7,7},{8,8},{9,12},{10,1... | collective-permute-start | bytes 1572872 | tf_op jit(solution)/shard_map/ppermute | solution.py:792
  148.5 28.0 %collective-permute-start.26 = (bf16[2016,256]{1,0:T(8,128)(2,1)S(1)}, bf16[2016,256]{1,0:T(8,128)(2,1)S(1)}, u32[]{:S(2)}, u32[]{:S(2)}) collective-permute-start(bf16[2016,256]{1,0:T(8,128)(2,1)S(1)} %get-tuple-element.875), channel_id=1, source_target_pairs={{0,8},{1,9},{2,10},{3,11},{4,12},{5,13},{6,14},{7,15},{8,0},{9,1},... | collective-permute-start | bytes 3096584 | tf_op jit(solution)/shard_map/ppermute | solution.py:792
  150.1 26.4 %collective-permute-start.27 = (bf16[2016,256]{1,0:T(8,128)(2,1)S(1)}, bf16[2016,256]{1,0:T(8,128)(2,1)S(1)}, u32[]{:S(2)}, u32[]{:S(2)}) collective-permute-start(bf16[2016,256]{1,0:T(8,128)(2,1)S(1)} %get-tuple-element.874), channel_id=1, source_target_pairs={{0,16},{1,17},{2,18},{3,19},{4,20},{5,21},{6,22},{7,23},{8,24},{9,... | collective-permute-start | bytes 3096584 | tf_op jit(solution)/shard_map/ppermute | solution.py:792
  150.8 25.6 %collective-permute-start.28 = (bf16[256,1024]{1,0:T(8,128)(2,1)S(1)}, bf16[256,1024]{1,0:T(8,128)(2,1)S(1)}, u32[]{:S(2)}, u32[]{:S(2)}) collective-permute-start(bf16[256,1024]{1,0:T(8,128)(2,1)S(1)} %dynamic-slice_bitcast_fusion), channel_id=1, source_target_pairs={{0,2},{1,6},{2,0},{3,4},{4,3},{5,7},{6,1},{7,5},{8,10},{9,14},{10,... | collective-permute-start | bytes 1572872 | tf_op jit(solution)/shard_map/ppermute | solution.py:792
  205.6 18.8 %collective-permute-start.38 = (bf16[512,1024]{1,0:T(8,128)(2,1)}, bf16[512,1024]{1,0:T(8,128)(2,1)S(1)}, u32[]{:S(2)}, u32[]{:S(2)}) collective-permute-start(bf16[512,1024]{1,0:T(8,128)(2,1)} %get-tuple-element.556), channel_id=1, source_target_pairs={{0,4},{1,5},{2,6},{3,7},{4,0},{5,1},{6,2},{7,3},{8,12},{9,13},{10,... | collective-permute-start | bytes 3145736 | tf_op jit(solution)/shard_map/ppermute | solution.py:792
  205.7 17.9 %collective-permute-start.36 = (bf16[1344,256]{1,0:T(8,128)(2,1)}, bf16[1344,256]{1,0:T(8,128)(2,1)S(1)}, u32[]{:S(2)}, u32[]{:S(2)}) collective-permute-start(bf16[1344,256]{1,0:T(8,128)(2,1)} %bitcast.32), channel_id=1, source_target_pairs={{0,8},{1,9},{2,10},{3,11},{4,12},{5,13},{6,14},{7,15},{8,0},{9,1},... | collective-permute-start | bytes 2064392 | tf_op jit(solution)/shard_map/ppermute | solution.py:792
  227.3 37.1 %collective-permute-start.44 = (bf16[2016,256]{1,0:T(8,128)(2,1)S(1)}, bf16[2016,256]{1,0:T(8,128)(2,1)S(1)}, u32[]{:S(2)}, u32[]{:S(2)}) collective-permute-start(bf16[2016,256]{1,0:T(8,128)(2,1)S(1)} %pad_maximum_fusion.14), channel_id=1, source_target_pairs={{0,16},{1,17},{2,18},{3,19},{4,20},{5,21},{6,22},{7,23},{8,24},{9,... | collective-permute-start | bytes 3096584 | tf_op jit(solution)/shard_map/ppermute | solution.py:792
  228.0 36.3 %collective-permute-start.43 = (bf16[2016,256]{1,0:T(8,128)(2,1)S(1)}, bf16[2016,256]{1,0:T(8,128)(2,1)S(1)}, u32[]{:S(2)}, u32[]{:S(2)}) collective-permute-start(bf16[2016,256]{1,0:T(8,128)(2,1)S(1)} %pad_maximum_fusion.13), channel_id=1, source_target_pairs={{0,8},{1,9},{2,10},{3,11},{4,12},{5,13},{6,14},{7,15},{8,0},{9,1},... | collective-permute-start | bytes 3096584 | tf_op jit(solution)/shard_map/ppermute | solution.py:792
  233.3 33.6 %collective-permute-start.45 = (bf16[256,1024]{1,0:T(8,128)(2,1)S(1)}, bf16[256,1024]{1,0:T(8,128)(2,1)S(1)}, u32[]{:S(2)}, u32[]{:S(2)}) collective-permute-start(bf16[256,1024]{1,0:T(8,128)(2,1)S(1)} %slice.273), channel_id=1, source_target_pairs={{2,0},{6,1},{0,2},{4,3},{3,4},{7,5},{1,6},{5,7},{10,8},{14,9},{8,1... | collective-permute-start | bytes 1572872 | tf_op jit(solution)/shard_map/ppermute | solution.py:792
  268.8 37.5 %collective-permute-start.47 = (bf16[2016,256]{1,0:T(8,128)(2,1)}, bf16[2016,256]{1,0:T(8,128)(2,1)S(1)}, u32[]{:S(2)}, u32[]{:S(2)}) collective-permute-start(bf16[2016,256]{1,0:T(8,128)(2,1)} %pad_maximum_fusion.16), channel_id=1, source_target_pairs={{0,16},{1,17},{2,18},{3,19},{4,20},{5,21},{6,22},{7,23},{8,24},{9,... | collective-permute-start | bytes 3096584 | tf_op jit(solution)/shard_map/ppermute | solution.py:792
  272.5 33.9 %collective-permute-start.46 = (bf16[2016,256]{1,0:T(8,128)(2,1)}, bf16[2016,256]{1,0:T(8,128)(2,1)S(1)}, u32[]{:S(2)}, u32[]{:S(2)}) collective-permute-start(bf16[2016,256]{1,0:T(8,128)(2,1)} %pad_maximum_fusion.15), channel_id=1, source_target_pairs={{0,8},{1,9},{2,10},{3,11},{4,12},{5,13},{6,14},{7,15},{8,0},{9,1},... | collective-permute-start | bytes 3096584 | tf_op jit(solution)/shard_map/ppermute | solution.py:792
  274.1 34.3 %collective-permute-start.48 = (bf16[256,1024]{1,0:T(8,128)(2,1)}, bf16[256,1024]{1,0:T(8,128)(2,1)}, u32[]{:S(2)}, u32[]{:S(2)}) collective-permute-start(bf16[256,1024]{1,0:T(8,128)(2,1)} %slice.274), channel_id=1, source_target_pairs={{0,0},{4,1},{2,2},{6,3},{1,4},{5,5},{3,6},{7,7},{8,8},{12,9},{10,1... | collective-permute-start | bytes 1572872 | tf_op jit(solution)/shard_map/ppermute | solution.py:792
  279.5 89.1 %reduce-scatter.6.cloned.1.call-start = ((), (), s32[]{:S(2)}) async-start(), calls=%async_computation.4 | async-start | bytes 860160 | tf_op jit(solution)/shard_map/reduce_scatter | solution.py:1162
  317.1 32.8 %collective-permute-start.53 = (bf16[256,1024]{1,0:T(8,128)(2,1)}, bf16[256,1024]{1,0:T(8,128)(2,1)}, u32[]{:S(2)}, u32[]{:S(2)}) collective-permute-start(bf16[256,1024]{1,0:T(8,128)(2,1)} %slice.277), channel_id=1, source_target_pairs={{2,0},{6,1},{0,2},{4,3},{3,4},{7,5},{1,6},{5,7},{10,8},{14,9},{8,1... | collective-permute-start | bytes 1572872 | tf_op jit(solution)/shard_map/ppermute | solution.py:792
  317.2 70.1 %reduce-scatter.8.cloned.1.call-start = ((), (), s32[]{:S(2)}) async-start(), calls=%async_computation.5 | async-start | bytes 860160 | tf_op jit(solution)/shard_map/reduce_scatter | solution.py:1162
  (169 other events, 1491.9 us)
Sparse Core Ops, SparseCore 0:
  279.6 19.2 reduce-scatter.3
  317.3 28.9 reduce-scatter.5
  362.3 22.1 reduce-scatter.7
